TPU v7x, 32 devices: a whole 2x2x4 slice. The times are simulated.
32 devices in a mesh: dp: 16 (over z, x, core), tensor: 2 (over y).
Axes of the slice: x: 2, y: 2, z: 4, core: 2. Of those that a mesh axis runs over, the one named last changes fastest.
Arguments:
- tokens: bfloat16 [32768, 1024], P(('dp', 'tensor')), may hold values from -6 to 6
- lengths: int32 [32], P('dp'), may hold values from 1 to 1024, 24576 in all
- in_proj: float32 [3, 1024, 1024], P(None, 'dp', 'tensor'), may hold values from -0.1875 to 0.1875
- conv_weight: float32 [3, 1024], replicated, may hold values from -3.5 to 3.5
- out_proj: float32 [1024, 1024], P('tensor', 'dp'), may hold values from -0.1875 to 0.1875
- norm_gain: float32 [1024], replicated, may hold values from 0.1 to 1.9
- ffn_gain: float32 [1024], replicated, may hold values from 0.1 to 1.9
- w_gate: float32 [1024, 4608], P('dp', 'tensor'), may hold values from -0.1875 to 0.1875
- w_up: float32 [1024, 4608], P('dp', 'tensor'), may hold values from -0.1875 to 0.1875
- w_down: float32 [4608, 1024], P('tensor', 'dp'), may hold values from -0.09375 to 0.09375
- cotangent: bfloat16 [32768, 1024], P(('dp', 'tensor')), may hold values from -6 to 6
Outputs:
- result: bfloat16 [32768, 1024], P(('dp', 'tensor'))
- grad_tokens: float32 [32768, 1024], P(('dp', 'tensor'))
- grad_in_proj: float32 [3, 1024, 1024], P(None, 'dp', 'tensor')
- grad_conv: float32 [3, 1024], replicated
- grad_out_proj: float32 [1024, 1024], P('tensor', 'dp')
- grad_norm_gain: float32 [1024], replicated
- grad_ffn_gain: float32 [1024], replicated
- grad_gate: float32 [1024, 4608], P('dp', 'tensor')
- grad_up: float32 [1024, 4608], P('dp', 'tensor')
- grad_down: float32 [4608, 1024], P('tensor', 'dp')
All inputs are finite; a program needn't handle non-finite values. No bound on the sum of `lengths` on one device may be relied on, other than what follows from the above.
Results may differ from a plain program's by a relative error of at most 0.025.
Values may be sent and summed in bfloat16 or wider, within the bound.
No kernel may reach another device: no remote copies, remote signals or barrier semaphores. Data moves between devices by JAX's collectives and lax.ppermute only.
A program may use at most 256 MiB of HBM per device.

v0:
```python
import jax
import jax.numpy as jnp
from jax import lax
from jax.sharding import PartitionSpec as P

SLOTS = 1024


EPS = 1e-05


def dot_tn(left, right):
    return lax.dot_general(
        left, right, (((0,), (0,)), ((), ())), preferred_element_type=jnp.float32
    )


def dot_nt(left, right):
    return lax.dot_general(
        left, right, (((1,), (1,)), ((), ())), preferred_element_type=jnp.float32
    )


def shift_down(values, shift, position):
    moved = jnp.concatenate(
        [jnp.zeros((shift, values.shape[1]), values.dtype), values[:-shift]], axis=0
    )
    return jnp.where((position >= shift)[:, None], moved, jnp.zeros_like(moved))


def shift_up(values, shift):
    return jnp.concatenate(
        [values[shift:], jnp.zeros((shift, values.shape[1]), values.dtype)], axis=0
    )


def norm_stats(values):
    inverse = lax.rsqrt(jnp.mean(values * values, axis=-1, keepdims=True) + EPS)
    return (inverse, values * inverse)


def norm_back(grad_normed, gain, inverse, unit):
    scaled = grad_normed * gain
    return inverse * (scaled - unit * jnp.mean(scaled * unit, axis=-1, keepdims=True))


def body(
    tokens,
    lengths,
    in_proj,
    conv_weight,
    out_proj,
    norm_gain,
    ffn_gain,
    w_gate,
    w_up,
    w_down,
    cotangent,
):
    own_rows, width = tokens.shape
    tensor_size = lax.axis_size("tensor")
    rank = lax.axis_index("tensor")
    half = in_proj.shape[2]
    kernel = conv_weight.shape[0]
    rows = own_rows * tensor_size
    index_rows = jnp.arange(rows, dtype=jnp.int32)
    position = index_rows % SLOTS
    sequence = index_rows // SLOTS
    members = jnp.arange(lengths.shape[0], dtype=jnp.int32)
    hits = (sequence[:, None] == members[None, :]) & (position[:, None] < lengths[None, :])
    alive = jnp.sum(jnp.where(hits, 1.0, 0.0), axis=1).astype(jnp.float32)
    alive_own = lax.dynamic_slice_in_dim(alive, rank * own_rows, own_rows)
    conv_half = lax.dynamic_slice_in_dim(conv_weight, rank * half, half, 1)
    in_full, out_full = (
        lax.all_gather(in_proj.astype(jnp.bfloat16), "dp", axis=1, tiled=True),
        lax.all_gather(out_proj.astype(jnp.bfloat16), "dp", axis=1, tiled=True),
    )
    tokens_f = tokens.astype(jnp.float32)
    inverse_one, unit_one = norm_stats(tokens_f)
    normed = (unit_one * norm_gain).astype(jnp.bfloat16)
    normed_all = lax.all_gather(normed, "tensor", axis=0, tiled=True)
    project = jnp.einsum("rd,kde->kre", normed_all, in_full, preferred_element_type=jnp.float32)
    b_part, c_part, x_part = (project[0], project[1], project[2])
    gated = b_part * x_part * alive[:, None]
    mixed = conv_half[0] * gated
    for shift in range(1, kernel):
        mixed = mixed + conv_half[shift] * shift_down(gated, shift, position)
    branch = (c_part * mixed).astype(jnp.bfloat16)
    mixer_terms = jnp.dot(branch, out_full, preferred_element_type=jnp.float32)
    mixer_out = lax.psum_scatter(
        mixer_terms.astype(jnp.bfloat16), "tensor", scatter_dimension=0, tiled=True
    ).astype(jnp.float32)
    hidden = tokens_f + mixer_out
    gate_full, up_full, down_full = (
        lax.all_gather(w_gate.astype(jnp.bfloat16), "dp", axis=0, tiled=True),
        lax.all_gather(w_up.astype(jnp.bfloat16), "dp", axis=0, tiled=True),
        lax.all_gather(w_down.astype(jnp.bfloat16), "dp", axis=1, tiled=True),
    )
    inverse_two, unit_two = norm_stats(hidden)
    normed_two = (unit_two * ffn_gain).astype(jnp.bfloat16)
    normed_two_all = lax.all_gather(normed_two, "tensor", axis=0, tiled=True)
    gate = jnp.dot(normed_two_all, gate_full, preferred_element_type=jnp.float32)
    upward = jnp.dot(normed_two_all, up_full, preferred_element_type=jnp.float32)
    sigma = jax.nn.sigmoid(gate)
    active = (gate * sigma * upward).astype(jnp.bfloat16)
    ffn_terms = jnp.dot(active, down_full, preferred_element_type=jnp.float32)
    ffn_out = lax.psum_scatter(
        ffn_terms.astype(jnp.bfloat16), "tensor", scatter_dimension=0, tiled=True
    ).astype(jnp.float32)
    result = (hidden + ffn_out).astype(jnp.bfloat16)
    grad_out = cotangent.astype(jnp.float32) * alive_own[:, None]
    grad_ffn_all = lax.all_gather(grad_out.astype(jnp.bfloat16), "tensor", axis=0, tiled=True)
    grad_active = dot_nt(grad_ffn_all, down_full)
    grad_wdown = dot_tn(active, grad_ffn_all)
    grad_gate_rows = (grad_active * upward * sigma * (1.0 + gate * (1.0 - sigma))).astype(
        jnp.bfloat16
    )
    grad_up_rows = (grad_active * gate * sigma).astype(jnp.bfloat16)
    grad_wgate = dot_tn(normed_two_all, grad_gate_rows)
    grad_wup = dot_tn(normed_two_all, grad_up_rows)
    norm_terms = dot_nt(grad_gate_rows, gate_full) + dot_nt(grad_up_rows, up_full)
    grad_normed_two = lax.psum_scatter(
        norm_terms.astype(jnp.bfloat16), "tensor", scatter_dimension=0, tiled=True
    ).astype(jnp.float32)
    gain_two_part = jnp.sum(grad_normed_two * unit_two, axis=0)
    grad_hidden = grad_out + norm_back(grad_normed_two, ffn_gain, inverse_two, unit_two)
    grad_mix_all = lax.all_gather(grad_hidden.astype(jnp.bfloat16), "tensor", axis=0, tiled=True)
    grad_branch = dot_nt(grad_mix_all, out_full)
    grad_wout = dot_tn(branch, grad_mix_all)
    grad_c = grad_branch * mixed
    grad_mixed = grad_branch * c_part
    tap_grads = [jnp.sum(grad_mixed * gated, axis=0)]
    grad_gated = conv_half[0] * grad_mixed
    for shift in range(1, kernel):
        masked = jnp.where((position >= shift)[:, None], grad_mixed, jnp.zeros_like(grad_mixed))
        tap_grads.append(jnp.sum(grad_mixed * shift_down(gated, shift, position), axis=0))
        grad_gated = grad_gated + conv_half[shift] * shift_up(masked, shift)
    grad_gated = grad_gated * alive[:, None]
    grad_project = jnp.stack([grad_gated * x_part, grad_c, grad_gated * b_part]).astype(
        jnp.bfloat16
    )
    grad_win = jnp.einsum(
        "rd,kre->kde", normed_all, grad_project, preferred_element_type=jnp.float32
    )
    input_terms = jnp.einsum(
        "kre,kde->rd", grad_project, in_full, preferred_element_type=jnp.float32
    )
    grad_normed = lax.psum_scatter(
        input_terms.astype(jnp.bfloat16), "tensor", scatter_dimension=0, tiled=True
    ).astype(jnp.float32)
    gain_one_part = jnp.sum(grad_normed * unit_one, axis=0)
    grad_tokens = grad_hidden + norm_back(grad_normed, norm_gain, inverse_one, unit_one)
    conv_full = jnp.zeros((kernel, width), jnp.float32)
    conv_full = lax.dynamic_update_slice_in_dim(conv_full, jnp.stack(tap_grads), rank * half, 1)
    gain_one, gain_two, conv_total = lax.psum(
        (gain_one_part, gain_two_part, conv_full), ("dp", "tensor")
    )
    in_shard, out_shard, gate_shard, up_shard, down_shard = (
        lax.psum_scatter(grad_win, "dp", scatter_dimension=1, tiled=True),
        lax.psum_scatter(grad_wout, "dp", scatter_dimension=1, tiled=True),
        lax.psum_scatter(grad_wgate, "dp", scatter_dimension=0, tiled=True),
        lax.psum_scatter(grad_wup, "dp", scatter_dimension=0, tiled=True),
        lax.psum_scatter(grad_wdown, "dp", scatter_dimension=1, tiled=True),
    )
    return (
        result,
        grad_tokens,
        in_shard,
        conv_total,
        out_shard,
        gain_one,
        gain_two,
        gate_shard,
        up_shard,
        down_shard,
    )


def solution(mesh):
    in_specs = (
        P(("dp", "tensor"), None),
        P("dp"),
        P(None, "dp", "tensor"),
        P(),
        P("tensor", "dp"),
        P(),
        P(),
        P("dp", "tensor"),
        P("dp", "tensor"),
        P("tensor", "dp"),
        P(("dp", "tensor"), None),
    )
    out_specs = (
        P(("dp", "tensor"), None),
        P(("dp", "tensor"), None),
        P(None, "dp", "tensor"),
        P(),
        P("tensor", "dp"),
        P(),
        P(),
        P("dp", "tensor"),
        P("dp", "tensor"),
        P("tensor", "dp"),
    )
    return jax.shard_map(body, mesh=mesh, in_specs=in_specs, out_specs=out_specs, check_vma=False)
```

profile of v0, /device:TPU:0, one launch (start us, length us, event | category | flops | bytes accessed | tf_op | source)
XLA Modules:
  0.0 1431.9 jit_solution(3071411859619356338)
XLA Ops:
  15.5 56.9 %all-gather.10.cloned.1.call-done = bf16[2048,1024]{1,0:T(8,128)(2,1)} async-done(((bf16[1024,1024]{1,0:T(8,128)(2,1)}), bf16[2048,1024]{1,0:T(8,128)(2,1)}) %all-gather.10.cloned.1.call-update) | async-done | bytes 4194320 | tf_op jit(solution)/shard_map/all_gather | solution.py:81
  72.5 48.0 %all-gather.12.cloned.1.call-done = bf16[3,1024,512]{2,1,0:T(8,128)(2,1)} async-done(((bf16[3,64,512]{2,1,0:T(8,128)(2,1)}), bf16[3,1024,512]{2,1,0:T(8,128)(2,1)}) %all-gather.12.cloned.1.call-update) | async-done | bytes 3145744 | tf_op jit(solution)/shard_map/all_gather | solution.py:75
  120.5 9.4 convolution_bitcast_fusion
  140.5 19.5 %all-gather.14.cloned.1.call-done = bf16[512,1024]{0,1:T(8,128)(2,1)} async-done(((bf16[512,64]{0,1:T(8,128)(2,1)}), bf16[512,1024]{0,1:T(8,128)(2,1)}) %all-gather.14.cloned.1.call-update) | async-done | bytes 1048592 | tf_op jit(solution)/shard_map/all_gather | solution.py:76
  167.5 51.5 %reduce-scatter.9.cloned.1.call-done = bf16[1024,1024]{1,0:T(8,128)(2,1)} async-done(((bf16[2048,1024]{1,0:T(8,128)(2,1)}), bf16[1024,1024]{1,0:T(8,128)(2,1)}) %reduce-scatter.9.cloned.1.call-update) | async-done | bytes 2097168 | tf_op jit(solution)/shard_map/reduce_scatter | solution.py:90
  229.0 46.2 %all-gather.18.cloned.1.call-done = bf16[1024,2304]{1,0:T(8,128)(2,1)} async-done(((bf16[64,2304]{1,0:T(8,128)(2,1)}), bf16[1024,2304]{1,0:T(8,128)(2,1)}) %all-gather.18.cloned.1.call-update) | async-done | bytes 4718608 | tf_op jit(solution)/shard_map/all_gather | solution.py:95
  275.2 57.4 %all-gather.16.cloned.1.call-done = bf16[2048,1024]{1,0:T(8,128)(2,1)} async-done(((bf16[1024,1024]{1,0:T(8,128)(2,1)}), bf16[2048,1024]{1,0:T(8,128)(2,1)}) %all-gather.16.cloned.1.call-update) | async-done | bytes 4194320 | tf_op jit(solution)/shard_map/all_gather | solution.py:101
  332.6 16.7 %fusion.42 = f32[2048,2304]{1,0:T(8,128)} fusion(bf16[2048,1024]{1,0:T(8,128)(2,1)} %all-gather.16.cloned.1.call-done, bf16[1024,2304]{1,0:T(8,128)(2,1)} %all-gather.18.cloned.1.call-done), kind=kOutput, calls=%fused_computation.89 | convolution fusion | flops 9663676416 | bytes 27787264 | tf_op jit(solution)/shard_map/dot_general | solution.py:102
  349.3 39.6 %all-gather.20.cloned.1.call-done = bf16[1024,2304]{1,0:T(8,128)(2,1)} async-done(((bf16[64,2304]{1,0:T(8,128)(2,1)}), bf16[1024,2304]{1,0:T(8,128)(2,1)}) %all-gather.20.cloned.1.call-update) | async-done | bytes 4718608 | tf_op jit(solution)/shard_map/all_gather | solution.py:96
  389.0 16.7 %fusion.43 = f32[2048,2304]{1,0:T(8,128)} fusion(bf16[2048,1024]{1,0:T(8,128)(2,1)} %all-gather.16.cloned.1.call-done, bf16[1024,2304]{1,0:T(8,128)(2,1)} %all-gather.20.cloned.1.call-done), kind=kOutput, calls=%fused_computation.90 | convolution fusion | flops 9663676416 | bytes 27787264 | tf_op jit(solution)/shard_map/dot_general | solution.py:103
  405.7 40.2 %all-gather.24.cloned.1.call-done = bf16[2048,1024]{1,0:T(8,128)(2,1)} async-done(((bf16[1024,1024]{1,0:T(8,128)(2,1)}), bf16[2048,1024]{1,0:T(8,128)(2,1)}) %all-gather.24.cloned.1.call-update) | async-done | bytes 4194320 | tf_op jit(solution)/shard_map/all_gather | solution.py:112
  445.9 56.4 %all-gather.22.cloned.1.call-done = bf16[2304,1024]{0,1:T(8,128)(2,1)} async-done(((bf16[2304,64]{0,1:T(8,128)(2,1)}), bf16[2304,1024]{0,1:T(8,128)(2,1)}) %all-gather.22.cloned.1.call-update) | async-done | bytes 4718608 | tf_op jit(solution)/shard_map/all_gather | solution.py:97
  502.3 36.0 %multiply_convert_fusion = (bf16[2048,2304]{1,0:T(8,128)(2,1)}, bf16[2048,2304]{1,0:T(8,128)(2,1)}, bf16[2048,2304]{1,0:T(8,128)(2,1)}) fusion(f32[2048,2304]{1,0:T(8,128)} %fusion.42, f32[2048,2304]{1,0:T(8,128)} %fusion.43, bf16[2048,1024]{1,0:T(8,128)(2,1)} %all-gather.24.cloned.1.call-done, bf16[2304,1024]{0,1:T(8,128)(2,1)} %all-gather.22.cloned.1.call-done), kind=kOutput, calls=%fused_computation | convolution fusion | flops 9739173888 | bytes 74973184 | tf_op jit(solution)/shard_map/dot_general | solution.py:19
  538.3 16.1 %fusion.44 = f32[2048,1024]{1,0:T(8,128)} fusion(bf16[2048,2304]{1,0:T(8,128)(2,1)} %get-tuple-element.56, bf16[1024,2304]{1,0:T(8,128)(2,1)} %all-gather.18.cloned.1.call-done), kind=kOutput, calls=%fused_computation.91 | convolution fusion | flops 9663676416 | bytes 22544384 | tf_op jit(solution)/shard_map/dot_general | solution.py:19
  554.4 14.3 add_convert_fusion
  568.9 52.8 %reduce-scatter.13.cloned.1.call-done = bf16[1024,1024]{1,0:T(8,128)(2,1)} async-done(((bf16[2048,1024]{1,0:T(8,128)(2,1)}), bf16[1024,1024]{1,0:T(8,128)(2,1)}) %reduce-scatter.13.cloned.1.call-update) | async-done | bytes 2097168 | tf_op jit(solution)/shard_map/reduce_scatter | solution.py:122
  629.2 56.7 %all-gather.26.cloned.1.call-done = bf16[2048,1024]{1,0:T(8,128)(2,1)} async-done(((bf16[1024,1024]{1,0:T(8,128)(2,1)}), bf16[2048,1024]{1,0:T(8,128)(2,1)}) %all-gather.26.cloned.1.call-update) | async-done | bytes 4194320 | tf_op jit(solution)/shard_map/all_gather | solution.py:127
  685.9 10.7 multiply_reduce_fusion.2
  716.5 9.4 copy.27
  726.2 11.7 bitcast_convert_fusion
  738.0 15.4 %convolution_convert_fusion = bf16[2048,1024]{1,0:T(8,128)(2,1)} fusion(bf16[2048,2304]{1,0:T(8,128)(2,1)} %get-tuple-element.57, bf16[2304,1024]{0,1:T(8,128)(2,1)} %all-gather.22.cloned.1.call-done), kind=kOutput, calls=%fused_computation.57 | convolution fusion | flops 9665773568 | bytes 18350080 | tf_op jit(solution)/shard_map/dot_general | solution.py:106
  753.5 15.6 %fusion.46 = f32[1024,2304]{1,0:T(8,128)} fusion(bf16[2048,1024]{1,0:T(8,128)(2,1)} %all-gather.16.cloned.1.call-done, bf16[2048,2304]{1,0:T(8,128)(2,1)} %get-tuple-element.56), kind=kOutput, calls=%fused_computation.93 | convolution fusion | flops 9663676416 | bytes 23068672 | tf_op jit(solution)/shard_map/dot_general | solution.py:13
  769.4 15.5 %fusion.47 = f32[1024,2304]{1,0:T(8,128)} fusion(bf16[2048,1024]{1,0:T(8,128)(2,1)} %all-gather.16.cloned.1.call-done, bf16[2048,2304]{1,0:T(8,128)(2,1)} %get-tuple-element.55), kind=kOutput, calls=%fused_computation.94 | convolution fusion | flops 9663676416 | bytes 23068672 | tf_op jit(solution)/shard_map/dot_general | solution.py:13
  784.9 15.5 %fusion.48 = f32[2304,1024]{0,1:T(8,128)} fusion(bf16[2048,2304]{1,0:T(8,128)(2,1)} %get-tuple-element.57, bf16[2048,1024]{1,0:T(8,128)(2,1)} %all-gather.24.cloned.1.call-done), kind=kOutput, calls=%fused_computation.95 | convolution fusion | flops 9663676416 | bytes 23068672 | tf_op jit(solution)/shard_map/dot_general | solution.py:13
  808.3 87.6 %all-reduce.8.cloned.1.call-done = f32[3,1024,512]{2,0,1:T(4,128)} async-done(((f32[3,1024,512]{2,0,1:T(4,128)}), f32[3,1024,512]{2,0,1:T(4,128)}) %all-reduce.8.cloned.1.call-update) | async-done | bytes 6291472
  898.0 55.1 %reduce-scatter.15.cloned.1.call-done = bf16[1024,1024]{1,0:T(8,128)(2,1)} async-done(((bf16[2048,1024]{1,0:T(8,128)(2,1)}), bf16[1024,1024]{1,0:T(8,128)(2,1)}) %reduce-scatter.15.cloned.1.call-update) | async-done | bytes 2097168 | tf_op jit(solution)/shard_map/reduce_scatter | solution.py:148
  956.2 40.7 %all-reduce.5 = (f32[3,1024]{1,0:T(4,128)}, f32[1024]{0:T(1024)}, f32[1024]{0:T(1024)}) all-reduce(f32[3,1024]{1,0:T(4,128)S(1)} %maximum_dynamic-update-slice_fusion, f32[1024]{0:T(1024)S(1)} %get-tuple-element.42, f32[1024]{0:T(1024)S(1)} %get-tuple-element.40), channel_id=1, replica_groups=mesh['dp'=16,'tensor'=2] {'dp','tensor'}, use_global_device_ids=true, to_apply=%region_13.14 | all-reduce | flops 5120 | bytes 40960 | tf_op jit(solution)/shard_map/psum | solution.py:155
  996.9 14.0 reduce-scatter.11.cloned.1.call-done
  1018.5 108.7 %reduce-scatter.19.cloned.1.call-done = f32[64,2304]{1,0:T(8,128)} async-done(((f32[1024,2304]{1,0:T(8,128)}), f32[64,2304]{1,0:T(8,128)}) %reduce-scatter.19.cloned.1.call-update) | async-done | bytes 589840 | tf_op jit(solution)/shard_map/reduce_scatter | solution.py:161
  1127.1 115.7 %reduce-scatter.21.cloned.1.call-done = f32[64,2304]{1,0:T(8,128)} async-done(((f32[1024,2304]{1,0:T(8,128)}), f32[64,2304]{1,0:T(8,128)}) %reduce-scatter.21.cloned.1.call-update) | async-done | bytes 589840 | tf_op jit(solution)/shard_map/reduce_scatter | solution.py:162
  1242.8 116.2 %reduce-scatter.23.cloned.1.call-done = f32[2304,64]{0,1:T(8,128)} async-done(((f32[2304,1024]{0,1:T(8,128)}), f32[2304,64]{0,1:T(8,128)}) %reduce-scatter.23.cloned.1.call-update) | async-done | bytes 589840 | tf_op jit(solution)/shard_map/reduce_scatter | solution.py:163
  1359.0 65.5 %reduce-scatter.17.cloned.1.call-done = f32[512,64]{0,1:T(8,128)} async-done(((f32[512,1024]{0,1:T(8,128)}), f32[512,64]{0,1:T(8,128)}) %reduce-scatter.17.cloned.1.call-update) | async-done | bytes 131088 | tf_op jit(solution)/shard_map/reduce_scatter | solution.py:160
  (158 shorter events, 84.1 us)
Async XLA Ops:
  7.2 65.3 %all-gather.10.cloned.1.call-start = ((), (), s32[]{:S(2)}) async-start(), calls=%async_computation.8 | async-start | bytes 6291456 | tf_op jit(solution)/shard_map/all_gather | solution.py:81
  9.4 120.5 %copy-start.20 = (f32[1024]{0:T(1024)}, f32[1024]{0:T(1024)S(1)}, u32[]{:S(2)}) copy-start(f32[1024]{0:T(1024)S(1)} %add_rsqrt_fusion.1) | copy-start | bytes 12292
  12.9 107.6 %all-gather.12.cloned.1.call-start = ((), (), s32[]{:S(2)}) async-start(), calls=%async_computation.9 | async-start | bytes 3342336 | tf_op jit(solution)/shard_map/all_gather | solution.py:75
  13.7 146.3 %all-gather.14.cloned.1.call-start = ((), (), s32[]{:S(2)}) async-start(), calls=%async_computation.10 | async-start | bytes 1114112 | tf_op jit(solution)/shard_map/all_gather | solution.py:76
  14.4 204.6 %reduce-scatter.9.cloned.1.call-start = ((), (), s32[]{:S(2)}) async-start(), calls=%async_computation.11 | async-start | bytes 6291456 | tf_op jit(solution)/shard_map/reduce_scatter | solution.py:90
  14.5 115.9 %copy-start.23 = (pred[2048]{0:T(1024)(128)(4,1)}, pred[2048]{0:T(1024)(128)(4,1)S(1)}, u32[]{:S(2)}) copy-start(pred[2048]{0:T(1024)(128)(4,1)S(1)} %get-tuple-element.66) | copy-start | bytes 6148
  14.5 115.9 %copy-start.25 = (pred[2048]{0:T(1024)(128)(4,1)}, pred[2048]{0:T(1024)(128)(4,1)S(1)}, u32[]{:S(2)}) copy-start(pred[2048]{0:T(1024)(128)(4,1)S(1)} %get-tuple-element.67) | copy-start | bytes 6148
  14.6 209.9 %copy-start.16 = (f32[2048]{0:T(1024)}, f32[2048]{0:T(1024)S(1)}, u32[]{:S(2)}) copy-start(f32[2048]{0:T(1024)S(1)} %fusion.29) | copy-start | bytes 24580
  15.5 114.9 %copy-start.27 = (f32[1,512]{1,0:T(1,128)}, f32[1,512]{1,0:T(1,128)S(1)}, u32[]{:S(2)}) copy-start(f32[1,512]{1,0:T(1,128)S(1)} %get-tuple-element.61) | copy-start | bytes 6148
  15.5 114.9 %copy-start.29 = (f32[1,512]{1,0:T(1,128)}, f32[1,512]{1,0:T(1,128)S(1)}, u32[]{:S(2)}) copy-start(f32[1,512]{1,0:T(1,128)S(1)} %get-tuple-element.62) | copy-start | bytes 6148
  15.5 114.9 %copy-start.31 = (f32[1,512]{1,0:T(1,128)}, f32[1,512]{1,0:T(1,128)S(1)}, u32[]{:S(2)}) copy-start(f32[1,512]{1,0:T(1,128)S(1)} %get-tuple-element.63) | copy-start | bytes 6148
  140.5 19.6 %copy-start.7 = (bf16[2048,512]{1,0:T(8,128)(2,1)}, bf16[2048,512]{1,0:T(8,128)(2,1)S(1)}, u32[]{:S(2)}) copy-start(bf16[2048,512]{1,0:T(8,128)(2,1)S(1)} %get-tuple-element.53) | copy-start | bytes 6291460
  165.6 53.4 %copy-start.1 = (bf16[1024,1024]{1,0:T(8,128)(2,1)S(1)}, bf16[1024,1024]{1,0:T(8,128)(2,1)}, u32[]{:S(2)}) copy-start(bf16[1024,1024]{1,0:T(8,128)(2,1)} %param.11) | copy-start | bytes 6291460
  165.6 55.9 %copy-start.19 = (f32[1024]{0:T(1024)S(1)}, f32[1024]{0:T(1024)}, u32[]{:S(2)}) copy-start(f32[1024]{0:T(1024)} %param.17) | copy-start | bytes 12292
  165.6 109.6 %all-gather.18.cloned.1.call-start = ((), (), s32[]{:S(2)}) async-start(), calls=%async_computation.13 | async-start | bytes 5013504 | tf_op jit(solution)/shard_map/all_gather | solution.py:95
  167.4 165.2 %all-gather.16.cloned.1.call-start = ((), (), s32[]{:S(2)}) async-start(), calls=%async_computation.12 | async-start | bytes 6291456 | tf_op jit(solution)/shard_map/all_gather | solution.py:101
  223.7 165.3 %all-gather.20.cloned.1.call-start = ((), (), s32[]{:S(2)}) async-start(), calls=%async_computation.14 | async-start | bytes 5013504 | tf_op jit(solution)/shard_map/all_gather | solution.py:96
  224.5 221.5 %all-gather.24.cloned.1.call-start = ((), (), s32[]{:S(2)}) async-start(), calls=%async_computation.17 | async-start | bytes 6291456 | tf_op jit(solution)/shard_map/all_gather | solution.py:112
  227.9 274.4 %all-gather.22.cloned.1.call-start = ((), (), s32[]{:S(2)}) async-start(), calls=%async_computation.15 | async-start | bytes 5013504 | tf_op jit(solution)/shard_map/all_gather | solution.py:97
  228.7 392.9 %reduce-scatter.13.cloned.1.call-start = ((), (), s32[]{:S(2)}) async-start(), calls=%async_computation.18 | async-start | bytes 6291456 | tf_op jit(solution)/shard_map/reduce_scatter | solution.py:122
  538.3 16.1 %copy-start.37 = (bf16[2048,2304]{1,0:T(8,128)(2,1)S(1)}, bf16[2048,2304]{1,0:T(8,128)(2,1)}, u32[]{:S(2)}) copy-start(bf16[2048,2304]{1,0:T(8,128)(2,1)} %get-tuple-element.55) | copy-start | bytes 28311556
  568.6 117.2 %all-gather.26.cloned.1.call-start = ((), (), s32[]{:S(2)}) async-start(), calls=%async_computation.19 | async-start | bytes 6291456 | tf_op jit(solution)/shard_map/all_gather | solution.py:127
  625.8 60.0 %copy-start.11 = (bf16[512,1024]{0,1:T(8,128)(2,1)S(1)}, bf16[512,1024]{0,1:T(8,128)(2,1)}, u32[]{:S(2)}) copy-start(bf16[512,1024]{0,1:T(8,128)(2,1)} %all-gather.14.cloned.1.call-done) | copy-start | bytes 3145732
  628.9 267.0 %all-reduce.8.cloned.1.call-start = ((), (), s32[]{:S(2)}) async-start(), calls=%async_computation.25 | async-start | bytes 16777216
  725.9 227.2 %reduce-scatter.15.cloned.1.call-start = ((), (), s32[]{:S(2)}) async-start(), calls=%async_computation.20 | async-start | bytes 6291456 | tf_op jit(solution)/shard_map/reduce_scatter | solution.py:148
  737.9 273.0 %reduce-scatter.11.cloned.1.call-start = ((), (), s32[]{:S(2)}) async-start(), calls=%async_computation.16 | async-start | bytes 6291456 | tf_op jit(solution)/shard_map/reduce_scatter | solution.py:107
  753.4 373.7 %reduce-scatter.19.cloned.1.call-start = ((), (), s32[]{:S(2)}) async-start(), calls=%async_computation.22 | async-start | bytes 10027008 | tf_op jit(solution)/shard_map/reduce_scatter | solution.py:161
  769.1 473.7 %reduce-scatter.21.cloned.1.call-start = ((), (), s32[]{:S(2)}) async-start(), calls=%async_computation.23 | async-start | bytes 10027008 | tf_op jit(solution)/shard_map/reduce_scatter | solution.py:162
  784.9 574.2 %reduce-scatter.23.cloned.1.call-start = ((), (), s32[]{:S(2)}) async-start(), calls=%async_computation.24 | async-start | bytes 10027008 | tf_op jit(solution)/shard_map/reduce_scatter | solution.py:163
  800.4 152.7 %copy-start.21 = (f32[1024]{0:T(1024)S(1)}, f32[1024]{0:T(1024)}, u32[]{:S(2)}) copy-start(f32[1024]{0:T(1024)} %copy-done.20) | copy-start | bytes 12292
  800.4 152.7 %copy-start.22 = (f32[1024]{0:T(1024)S(1)}, f32[1024]{0:T(1024)}, u32[]{:S(2)}) copy-start(f32[1024]{0:T(1024)} %param.16) | copy-start | bytes 12292
  800.4 624.1 %reduce-scatter.17.cloned.1.call-start = ((), (), s32[]{:S(2)}) async-start(), calls=%async_computation.21 | async-start | bytes 2228224 | tf_op jit(solution)/shard_map/reduce_scatter | solution.py:160
  (27 other events, 135.5 us)
Sparse Core Ops, SparseCore 0:
  13.0 59.4 all-gather.9
  75.2 45.1 all-gather.11
  123.2 36.7 all-gather.13
  165.7 53.2 reduce-scatter.8
  222.0 53.2 all-gather.17
  277.3 55.2 all-gather.15
  335.7 53.2 all-gather.19
  390.6 55.2 all-gather.23
  449.1 53.2 all-gather.21
  568.8 52.8 reduce-scatter.12
  629.1 56.7 all-gather.25
  726.0 169.9 all-reduce.7
  898.9 54.1 reduce-scatter.14
  955.3 55.5 reduce-scatter.10
  1015.9 111.1 reduce-scatter.18
  1131.6 111.1 reduce-scatter.20
  1247.9 111.1 reduce-scatter.22
  1363.2 61.2 reduce-scatter.16
where the time goes:
time: 1440 us; the launch traced here: 1430 us
  waiting for transfers between devices  1090 us (76%)
  matrix products  214 us (15%)
  other arithmetic  48.1 us (3%)
  blocking collectives  40.7 us (3%)
  local copies, waits for them, and re-layouts  22.5 us (2%)
  between operations  16 us (1%)
    reduce_scatter x1, waiting for transfers between devices, body(): lax.psum_scatter(grad_wdown, 'dp', scatter_dimension=1, tiled=True)  116 us
    reduce_scatter x1, waiting for transfers between devices, body(): lax.psum_scatter(grad_wup, 'dp', scatter_dimension=0, tiled=True)  116 us
    reduce_scatter x1, waiting for transfers between devices, body(): lax.psum_scatter(grad_wgate, 'dp', scatter_dimension=0, tiled=True)  109 us
    unnamed x19, waiting for transfers between devices  87.9 us
    dot_general x4, matrix products, dot_nt(): lax.dot_general(left, right, (((1,), (1,)), ((), ())), preferred_element_...  77 us
    reduce_scatter x1, waiting for transfers between devices, body(): lax.psum_scatter(grad_wout, 'dp', scatter_dimension=1, tiled=True)  65.5 us
    all_gather x1, waiting for transfers between devices, body(): normed_two_all = lax.all_gather(normed_two, 'tensor', axis=0, tiled=True)  57.4 us
    all_gather x1, waiting for transfers between devices, body(): normed_all = lax.all_gather(normed, 'tensor', axis=0, tiled=True)  56.9 us
  transfers between devices with their start and end apart: 18, of which 18 were waited for; matrix products, arithmetic and copies ran while one was open for 11% of the time, Pallas kernels for 0%

commit v1 on v0

v1 whole, which is shorter than its diff:
```python
import jax
import jax.numpy as jnp
from jax import lax
from jax.sharding import PartitionSpec as P

SLOTS = 1024
EPS = 1e-05
AXES = ("dp", "tensor")
PIECES = 3
BF = jnp.bfloat16
F32 = jnp.float32


def dot_nn(left, right):
    return jnp.dot(left, right, preferred_element_type=F32)


def dot_tn(left, right):
    return lax.dot_general(left, right, (((0,), (0,)), ((), ())), preferred_element_type=F32)


def dot_nt(left, right):
    return lax.dot_general(left, right, (((1,), (1,)), ((), ())), preferred_element_type=F32)


class Links:
    def __init__(self, dp, tp):
        self.dp, self.tp, self.zs = dp, tp, dp // 4

    def swap(self, value, z=0, x=0, c=0, y=0):
        flip = (z * 2 + x) * 2 + c
        pairs = [
            (q * self.tp + t, (q ^ flip) * self.tp + (t ^ y))
            for q in range(self.dp)
            for t in range(self.tp)
        ]
        return lax.ppermute(value, AXES, pairs)

    def gather(self, own):
        parts = [own] + [self.swap(own, z=z) for z in range(1, self.zs)]
        mine = jnp.concatenate(parts, axis=1)
        half = mine.shape[1] // 2
        from_x, from_y = self.swap(mine, x=1), self.swap(mine, y=1)
        corner = jnp.concatenate(
            [self.swap(from_x[:, :half], y=1), self.swap(from_y[:, half:], x=1)], axis=1
        )
        grid = [[mine, from_y], [from_x, corner]]
        twin = [[self.swap(item, c=1) for item in row] for row in grid]
        return jnp.concatenate(
            [jnp.concatenate(row, axis=2) for row in grid + twin], axis=1
        )

    def scatter(self, full):
        kinds, depth, width = full.shape
        rows, cols = depth // 4, width // 2
        half, block = rows // 2, rows // self.zs

        def cell(core, x, y):
            at = (core * 2 + x) * rows
            return full[:, at : at + rows, y * cols : (y + 1) * cols]

        def both(x, y):
            return cell(0, x, y).astype(F32) + self.swap(cell(1, x, y), c=1).astype(F32)

        corner = both(1, 1).astype(BF)
        side_x, side_y, mine = both(1, 0), both(0, 1), both(0, 0)
        got_x = self.swap(corner[:, :half], x=1).astype(F32)
        got_y = self.swap(corner[:, half:], y=1).astype(F32)
        send_y = jnp.concatenate([side_y[:, :half] + got_x, side_y[:, half:]], axis=1).astype(BF)
        send_x = jnp.concatenate([side_x[:, :half], side_x[:, half:] + got_y], axis=1).astype(BF)
        total = (
            mine + self.swap(send_x, x=1).astype(F32) + self.swap(send_y, y=1).astype(F32)
        )
        out = total[:, :block]
        for z in range(1, self.zs):
            part = total[:, z * block : (z + 1) * block].astype(BF)
            out = out + self.swap(part, z=z).astype(F32)
        return out

    def sum_all(self, value):
        value = value + self.swap(value, c=1)
        value = value + self.swap(value, x=1)
        value = value + self.swap(value, y=1)
        step = 1
        while step < self.zs:
            value = value + self.swap(value, z=step)
            step *= 2
        return value

    def relative_blocks(self):
        q = lax.axis_index("dp")
        place = jnp.arange(self.dp)
        core, x, z = place // (2 * self.zs), place // self.zs % 2, place % self.zs
        return q ^ ((z * 2 + x) * 2 + core)


def shift_down(values, shift, position):
    moved = jnp.concatenate(
        [jnp.zeros((shift, values.shape[1]), values.dtype), values[:-shift]], axis=0
    )
    return jnp.where((position >= shift)[:, None], moved, jnp.zeros_like(moved))


def shift_up(values, shift):
    return jnp.concatenate(
        [values[shift:], jnp.zeros((shift, values.shape[1]), values.dtype)], axis=0
    )


def norm_stats(values):
    inverse = lax.rsqrt(jnp.mean(values * values, axis=-1, keepdims=True) + EPS)
    return (inverse, values * inverse)


def norm_back(grad_normed, gain, inverse, unit):
    scaled = grad_normed * gain
    return inverse * (scaled - unit * jnp.mean(scaled * unit, axis=-1, keepdims=True))


def body(
    tokens,
    lengths,
    in_proj,
    conv_weight,
    out_proj,
    norm_gain,
    ffn_gain,
    w_gate,
    w_up,
    w_down,
    cotangent,
):
    rows, width = tokens.shape
    links = Links(lax.axis_size("dp"), lax.axis_size("tensor"))
    rank = lax.axis_index("tensor")
    kernel = conv_weight.shape[0]
    half = in_proj.shape[2]
    hidden_half = w_gate.shape[1]
    chunk = hidden_half // PIECES
    block = width // links.dp

    mixer_own = jnp.concatenate(
        [in_proj.astype(BF), out_proj.T.astype(BF)[None]], axis=0
    )
    ffn_own = jnp.stack([w_gate.astype(BF), w_up.astype(BF), w_down.T.astype(BF)])
    mixer_w = links.gather(mixer_own)
    ffn_w = [
        links.gather(ffn_own[:, :, p * chunk : (p + 1) * chunk]) for p in range(PIECES)
    ]

    blocks = links.relative_blocks()
    feature = jnp.repeat(blocks, block) * block + jnp.tile(jnp.arange(block), links.dp)
    order = (jnp.arange(width)[:, None] == feature[None, :]).astype(BF)
    tokens_f = dot_nn(tokens, order)
    cot = dot_nn(cotangent, order)
    gain_one = jnp.take(norm_gain.reshape(links.dp, block), blocks, axis=0).reshape(width)
    gain_two = jnp.take(ffn_gain.reshape(links.dp, block), blocks, axis=0).reshape(width)
    conv = jnp.where(rank == 0, conv_weight, jnp.roll(conv_weight, half, axis=1))

    count = rows // SLOTS
    own_lengths = lax.dynamic_slice_in_dim(lengths, rank * count, count)
    position = jnp.tile(jnp.arange(SLOTS, dtype=jnp.int32), count)
    alive = (position < jnp.repeat(own_lengths, SLOTS)).astype(F32)[:, None]

    inverse_one, unit_one = norm_stats(tokens_f)
    normed = (unit_one * gain_one).astype(BF)
    b_part, c_part, x_part = [dot_nn(normed, mixer_w[k]) for k in range(3)]
    gated = b_part * x_part * alive
    mixed = conv[0] * gated
    for shift in range(1, kernel):
        mixed = mixed + conv[shift] * shift_down(gated, shift, position)
    branch = (c_part * mixed).astype(BF)
    hidden = tokens_f + dot_nt(branch, mixer_w[3])
    inverse_two, unit_two = norm_stats(hidden)
    normed_two = (unit_two * gain_two).astype(BF)
    grad_out = cot * alive
    grad_ffn = grad_out.astype(BF)

    ffn_out = 0.0
    grad_normed_two = 0.0
    ffn_shards = []
    for w in ffn_w:
        gate = dot_nn(normed_two, w[0])
        upward = dot_nn(normed_two, w[1])
        grad_active = dot_nn(grad_ffn, w[2])
        sigma = jax.nn.sigmoid(gate)
        active = (gate * sigma * upward).astype(BF)
        grad_gate_rows = (grad_active * upward * sigma * (1.0 + gate * (1.0 - sigma))).astype(BF)
        grad_up_rows = (grad_active * gate * sigma).astype(BF)
        ffn_out = ffn_out + dot_nt(active, w[2])
        grads = jnp.stack(
            [
                dot_tn(normed_two, grad_gate_rows).astype(BF),
                dot_tn(normed_two, grad_up_rows).astype(BF),
                dot_tn(grad_ffn, active).astype(BF),
            ]
        )
        ffn_shards.append(links.scatter(grads))
        grad_normed_two = (
            grad_normed_two + dot_nt(grad_gate_rows, w[0]) + dot_nt(grad_up_rows, w[1])
        )
    result = dot_nt((hidden + ffn_out).astype(BF), order).astype(BF)

    gain_two_part = jnp.sum(grad_normed_two * unit_two, axis=0)
    grad_hidden = grad_out + norm_back(grad_normed_two, gain_two, inverse_two, unit_two)
    grad_mix = grad_hidden.astype(BF)
    grad_branch = dot_nn(grad_mix, mixer_w[3])
    grad_wout = dot_tn(grad_mix, branch)
    grad_c = grad_branch * mixed
    grad_mixed = grad_branch * c_part
    tap_grads = [jnp.sum(grad_mixed * gated, axis=0)]
    grad_gated = conv[0] * grad_mixed
    for shift in range(1, kernel):
        masked = jnp.where((position >= shift)[:, None], grad_mixed, jnp.zeros_like(grad_mixed))
        tap_grads.append(jnp.sum(grad_mixed * shift_down(gated, shift, position), axis=0))
        grad_gated = grad_gated + conv[shift] * shift_up(masked, shift)
    grad_gated = grad_gated * alive
    grad_project = [
        item.astype(BF) for item in (grad_gated * x_part, grad_c, grad_gated * b_part)
    ]
    mixer_shard = links.scatter(
        jnp.stack(
            [dot_tn(normed, item).astype(BF) for item in grad_project] + [grad_wout.astype(BF)]
        )
    )
    grad_normed = sum(dot_nt(item, mixer_w[k]) for k, item in enumerate(grad_project))
    gain_one_part = jnp.sum(grad_normed * unit_one, axis=0)
    grad_tokens = grad_hidden + norm_back(grad_normed, gain_one, inverse_one, unit_one)
    high = grad_tokens.astype(BF)
    rest = grad_tokens - high.astype(F32)
    middle = rest.astype(BF)
    low = (rest - middle.astype(F32)).astype(BF)
    grad_tokens = dot_nt(high, order) + (dot_nt(middle, order) + dot_nt(low, order))

    q = lax.axis_index("dp")
    apart = jnp.arange(links.dp) ^ q
    place = ((apart % 2) * 2 + apart // 2 % 2) * links.zs + apart // 4
    taps = jnp.stack(tap_grads)
    taps = jnp.where(rank == 0, taps, jnp.roll(taps, half, axis=1))
    gains = jnp.stack([gain_one_part, gain_two_part]).reshape(2, links.dp, block)
    gains = jnp.take(gains, place, axis=1).reshape(2, width)
    sums = links.sum_all(jnp.concatenate([gains, taps], axis=0))

    ffn_shard = jnp.concatenate(ffn_shards, axis=2)
    return (
        result,
        grad_tokens,
        mixer_shard[:3],
        sums[2:],
        mixer_shard[3].T,
        sums[0],
        sums[1],
        ffn_shard[0],
        ffn_shard[1],
        ffn_shard[2].T,
    )


def solution(mesh):
    rows = P(("dp", "tensor"), None)
    in_specs = (
        rows,
        P("dp"),
        P(None, "dp", "tensor"),
        P(),
        P("tensor", "dp"),
        P(),
        P(),
        P("dp", "tensor"),
        P("dp", "tensor"),
        P("tensor", "dp"),
        rows,
    )
    out_specs = (
        rows,
        rows,
        P(None, "dp", "tensor"),
        P(),
        P("tensor", "dp"),
        P(),
        P(),
        P("dp", "tensor"),
        P("dp", "tensor"),
        P("tensor", "dp"),
    )
    return jax.shard_map(body, mesh=mesh, in_specs=in_specs, out_specs=out_specs, check_vma=False)
```

time: 1440 us -> 933 us (0.65)
  waiting for transfers between devices: 1090 us -> 248 us
  other arithmetic: 48.1 us -> 207 us
  starting transfers between devices: 1.6 us -> 136 us
  local copies, waits for them, and re-layouts: 22.5 us -> 72.7 us
  matrix products: 214 us -> 260 us
  blocking collectives: 40.7 us -> 0 us
    reduce_scatter x8 -> x0, waiting for transfers between devices: 580 us -> none  [the longest x1 116 us: body(): lax.psum_scatter(grad_wdown, 'dp', scatter_dimension=1, tiled=True)]
    all_gather x9 -> x0, waiting for transfers between devices: 421 us -> none  [the longest x1 57.4 us: body(): normed_two_all = lax.all_gather(normed_two, 'tensor', axis=0, tiled=True)]
    ppermute x0 -> x93, waiting for transfers between devices: none -> 248 us  [swap(): return lax.ppermute(value, AXES, pairs)]
    concatenate x0 -> x19, other arithmetic: none -> 142 us  [the longest x4 125 us: gather(): jnp.concatenate([jnp.concatenate(row, axis=2) for row in grid + twin], ax...]
    ppermute x0 -> x93, starting transfers between devices: none -> 136 us  [swap(): return lax.ppermute(value, AXES, pairs)]
    unnamed x19 -> x0, waiting for transfers between devices: 87.9 us -> none
    psum x1 -> x0, blocking collectives: 40.7 us -> none  [body(): lax.psum((gain_one_part, gain_two_part, conv_full), ('dp', 'tensor'))]
    slice x1 -> x35, local copies, waits for them, and re-layouts: 0.9 us -> 39.9 us  [the longest x4 9 us: cell(): return full[:, at:at + rows, y * cols:(y + 1) * cols]]
  transfers between devices with their start and end apart: 18 -> 93, of which waited for: 18 -> 34; matrix products, arithmetic and copies ran while one was open for 11% -> 40% of each run, Pallas kernels for 0% -> 0%
where the time goes in v1:
time: 933 us; the launch traced here: 926 us
  matrix products  260 us (28%)
  waiting for transfers between devices  248 us (27%)
  other arithmetic  207 us (22%)
  starting transfers between devices  136 us (15%)
  local copies, waits for them, and re-layouts  72.7 us (8%)
    ppermute x93, waiting for transfers between devices, swap(): return lax.ppermute(value, AXES, pairs)  248 us
    ppermute x93, starting transfers between devices, swap(): return lax.ppermute(value, AXES, pairs)  136 us
    concatenate x4, other arithmetic, gather(): jnp.concatenate([jnp.concatenate(row, axis=2) for row in grid + twin], ax...  125 us
    dot_general x16, matrix products, dot_nt(): lax.dot_general(left, right, (((1,), (1,)), ((), ())), preferred_element_...  102 us
    dot_general x15, matrix products, dot_nn(): return jnp.dot(left, right, preferred_element_type=F32)  94.3 us
    dot_general x13, matrix products, dot_tn(): lax.dot_general(left, right, (((0,), (0,)), ((), ())), preferred_element_...  64.4 us
    unnamed x248, local copies, waits for them, and re-layouts  20.8 us
  transfers between devices with their start and end apart: 93, of which 34 were waited for; matrix products, arithmetic and copies ran while one was open for 40% of the time, Pallas kernels for 0%

profile of v1, /device:TPU:0, one launch (start us, length us, event | category | flops | bytes accessed | tf_op | source)
XLA Modules:
  0.0 925.7 jit_solution(5869925618887262321)
XLA Ops:
  13.8 8.4 collective-permute-done.2
  22.2 23.6 %collective-permute-start = (bf16[4,64,512]{2,1,0:T(8,128)(2,1)}, bf16[4,64,512]{2,1,0:T(8,128)(2,1)}, u32[]{:S(2)}, u32[]{:S(2)}) collective-permute-start(bf16[4,64,512]{2,1,0:T(8,128)(2,1)} %pad_maximum_fusion.18), channel_id=1, source_target_pairs={{0,8},{1,9},{2,10},{3,11},{4,12},{5,13},{6,14},{7,15},{8,0},{9,1},... | collective-permute-start | bytes 786440 | tf_op jit(solution)/shard_map/ppermute | solution.py:37
  53.9 10.9 %collective-permute-start.22 = (bf16[3,64,768]{2,1,0:T(8,128)(2,1)S(1)}, bf16[3,64,768]{2,1,0:T(8,128)(2,1)}, u32[]{:S(2)}, u32[]{:S(2)}) collective-permute-start(bf16[3,64,768]{2,1,0:T(8,128)(2,1)S(1)} %get-tuple-element.93), channel_id=1, source_target_pairs={{0,8},{1,9},{2,10},{3,11},{4,12},{5,13},{6,14},{7,15},{8,0},{9,1},... | collective-permute-start | bytes 884744 | tf_op jit(solution)/shard_map/ppermute | solution.py:37
  84.4 9.0 collective-permute-done.13
  93.4 10.6 %collective-permute-start.11 = (bf16[3,64,768]{2,1,0:T(8,128)(2,1)S(1)}, bf16[3,64,768]{2,1,0:T(8,128)(2,1)}, u32[]{:S(2)}, u32[]{:S(2)}) collective-permute-start(bf16[3,64,768]{2,1,0:T(8,128)(2,1)S(1)} %get-tuple-element.94), channel_id=1, source_target_pairs={{0,8},{1,9},{2,10},{3,11},{4,12},{5,13},{6,14},{7,15},{8,0},{9,1},... | collective-permute-start | bytes 884744 | tf_op jit(solution)/shard_map/ppermute | solution.py:37
  124.5 12.2 %collective-permute-done.36 = bf16[3,256,768]{2,1,0:T(8,128)(2,1)} collective-permute-done((bf16[3,256,768]{2,1,0:T(8,128)(2,1)}, bf16[3,256,768]{2,1,0:T(8,128)(2,1)}, u32[]{:S(2)}, u32[]{:S(2)}) %collective-permute-start.36) | collective-permute-done | bytes 1179680 | tf_op jit(solution)/shard_map/ppermute | solution.py:37
  149.0 12.9 %collective-permute-done.25 = bf16[3,256,768]{2,1,0:T(8,128)(2,1)S(1)} collective-permute-done((bf16[3,256,768]{2,1,0:T(8,128)(2,1)}, bf16[3,256,768]{2,1,0:T(8,128)(2,1)S(1)}, u32[]{:S(2)}, u32[]{:S(2)}) %collective-permute-start.25) | collective-permute-done | bytes 1179680 | tf_op jit(solution)/shard_map/ppermute | solution.py:37
  169.7 17.6 %collective-permute-done.14 = bf16[3,256,768]{2,1,0:T(8,128)(2,1)} collective-permute-done((bf16[3,256,768]{2,1,0:T(8,128)(2,1)}, bf16[3,256,768]{2,1,0:T(8,128)(2,1)}, u32[]{:S(2)}, u32[]{:S(2)}) %collective-permute-start.14) | collective-permute-done | bytes 1179680 | tf_op jit(solution)/shard_map/ppermute | solution.py:37
  188.8 9.7 %collective-permute-done.5 = bf16[4,128,512]{2,1,0:T(8,128)(2,1)} collective-permute-done((bf16[4,128,512]{2,1,0:T(8,128)(2,1)S(1)}, bf16[4,128,512]{2,1,0:T(8,128)(2,1)}, u32[]{:S(2)}, u32[]{:S(2)}) %collective-permute-start.5) | collective-permute-done | bytes 524320 | tf_op jit(solution)/shard_map/ppermute | solution.py:37
  211.6 12.2 %collective-permute-done.27 = bf16[3,128,768]{2,1,0:T(8,128)(2,1)} collective-permute-done((bf16[3,128,768]{2,1,0:T(8,128)(2,1)}, bf16[3,128,768]{2,1,0:T(8,128)(2,1)}, u32[]{:S(2)}, u32[]{:S(2)}) %collective-permute-start.27) | collective-permute-done | bytes 589856 | tf_op jit(solution)/shard_map/ppermute | solution.py:37
  226.1 7.1 collective-permute-done.16
  246.9 45.6 %maximum_maximum_fusion.3 = bf16[4,1024,1024]{2,1,0:T(8,128)(2,1)S(1)} fusion(bf16[4,256,512]{2,1,0:T(8,128)(2,1)S(1)} %collective-permute-done.10, bf16[4,256,512]{2,1,0:T(8,128)(2,1)S(1)} %collective-permute-done.9, bf16[4,256,512]{2,1,0:T(8,128)(2,1)S(1)} %collective-permute-done.8, bf16[4,256,512]{2,1,0:T(8,128)(2,1)S(1)} %collective-permute-done.7, ...), kind=kLoop, calls=%fused_computation.9 | loop fusion | flops 100663296 | bytes 16777216 | tf_op jit(solution)/shard_map/concatenate | solution.py:49
  316.4 18.4 %maximum_maximum_fusion.2 = bf16[3,1024,1536]{2,1,0:T(8,128)(2,1)S(1)} fusion(bf16[3,256,768]{2,1,0:T(8,128)(2,1)} %collective-permute-done.43, bf16[3,256,768]{2,1,0:T(8,128)(2,1)} %collective-permute-done.42, bf16[3,256,768]{2,1,0:T(8,128)(2,1)} %collective-permute-done.41, bf16[3,256,768]{2,1,0:T(8,128)(2,1)} %collective-permute-done.40, ...), kind=kLoop, calls=%fused_computation.5 | loop fusion | flops 103809024 | bytes 18874368 | tf_op jit(solution)/shard_map/concatenate | solution.py:49
  346.0 11.4 %multiply_convert_fusion = (bf16[1024,1536]{1,0:T(8,128)(2,1)}, bf16[1024,1536]{1,0:T(8,128)(2,1)}, bf16[1024,1536]{1,0:T(8,128)(2,1)}) fusion(f32[1024,1536]{1,0:T(8,128)} %fusion.35, f32[1024,1536]{1,0:T(8,128)} %fusion.37, bf16[1024,1024]{0,1:T(8,128)(2,1)S(1)} %copy-done.62, bf16[3,1024,1536]{2,1,0:T(8,128)(2,1)S(1)} %maximum_maximum_fusion.2), kind=kOutput, calls=%fused_computation.11 | convolution fusion | flops 3246391296 | bytes 27262976 | tf_op jit(solution)/shard_map/dot_general | solution.py:15
  357.4 6.8 fusion.12
  370.1 43.0 %maximum_maximum_fusion.1 = bf16[3,1024,1536]{2,1,0:T(8,128)(2,1)S(1)} fusion(bf16[3,256,768]{2,1,0:T(8,128)(2,1)} %collective-permute-done.32, bf16[3,256,768]{2,1,0:T(8,128)(2,1)S(1)} %collective-permute-done.31, bf16[3,256,768]{2,1,0:T(8,128)(2,1)} %collective-permute-done.30, bf16[3,256,768]{2,1,0:T(8,128)(2,1)} %collective-permute-done.29, ...), kind=kLoop, calls=%fused_computation.4 | loop fusion | flops 103809024 | bytes 18874368 | tf_op jit(solution)/shard_map/concatenate | solution.py:49
  424.2 11.5 %multiply_convert_fusion.3 = (bf16[1024,1536]{1,0:T(8,128)(2,1)}, bf16[1024,1536]{1,0:T(8,128)(2,1)}, bf16[1024,1536]{1,0:T(8,128)(2,1)}) fusion(f32[1024,1536]{1,0:T(8,128)} %fusion.32, f32[1024,1536]{1,0:T(8,128)} %fusion.31, bf16[1024,1024]{0,1:T(8,128)(2,1)S(1)} %multiply_convert_fusion.12, bf16[3,1024,1536]{2,1,0:T(8,128)(2,1)S(1)} %maximum_maximum_fusion.1), kind=kOutput, calls=%fused_computation.14 | convolution fusion | flops 3246391296 | bytes 27262976 | tf_op jit(solution)/shard_map/dot_general | solution.py:15
  435.7 6.8 fusion.9
  467.3 18.3 %maximum_maximum_fusion = bf16[3,1024,1536]{2,1,0:T(8,128)(2,1)S(1)} fusion(bf16[3,256,768]{2,1,0:T(8,128)(2,1)} %collective-permute-done.21, bf16[3,256,768]{2,1,0:T(8,128)(2,1)S(1)} %collective-permute-done.20, bf16[3,256,768]{2,1,0:T(8,128)(2,1)} %collective-permute-done.19, bf16[3,256,768]{2,1,0:T(8,128)(2,1)S(1)} %collective-permute-done.18, ...), kind=kLoop, calls=%fused_computation.3 | loop fusion | flops 103809024 | bytes 18874368 | tf_op jit(solution)/shard_map/concatenate | solution.py:49
  496.8 10.3 %multiply_convert_fusion.4 = (bf16[1024,1536]{1,0:T(8,128)(2,1)S(1)}, bf16[1024,1536]{1,0:T(8,128)(2,1)}, bf16[1024,1536]{1,0:T(8,128)(2,1)S(1)}) fusion(f32[1024,1536]{1,0:T(8,128)} %fusion.23, f32[1024,1536]{1,0:T(8,128)} %fusion.25, bf16[1024,1024]{0,1:T(8,128)(2,1)S(1)} %copy-done.62, bf16[3,1024,1536]{2,1,0:T(8,128)(2,1)S(1)} %maximum_maximum_fusion), kind=kOutput, calls=%fused_computation.15 | convolution fusion | flops 3246391296 | bytes 27262976 | tf_op jit(solution)/shard_map/dot_general | solution.py:15
  532.3 15.0 %multiply_reduce_fusion.3 = (f32[1024]{0:T(1024)S(1)}, f32[1024]{0:T(1024)S(1)}, f32[1024,1024]{0,1:T(8,128)}) fusion(f32[1024,1024]{0,1:T(8,128)S(1)} %copy-done.8, f32[1024]{0:T(1024)S(1)} %copy-done.91, f32[1024]{0:T(1024)S(1)} %copy-done.89, bf16[1024,1536]{1,0:T(8,128)(2,1)} %get-tuple-element.31, bf16[3,1024,1536]{2,1,0:T(8,128)(2,1)} %copy-done.16, ...), kind=kOutput, calls=%fused_computation.34 | convolution fusion | flops 3232757760 | bytes 35667968 | tf_op jit(solution)/shard_map/dot_general | solution.py:23
  554.5 8.3 multiply_reduce_fusion.2
  627.1 13.7 %fusion.46 = bf16[1024,1024]{1,0:T(8,128)(2,1)} fusion(s32[1024]{0:T(1024)S(1)} %copy-done.104, f32[1024,1024]{0,1:T(8,128)} %copy-done.7, f32[1024,1024]{0,1:T(8,128)} %fusion.27, f32[1024,1024]{0,1:T(8,128)} %fusion.33, bf16[1024,1536]{1,0:T(8,128)(2,1)} %get-tuple-element.33, bf16[3,1024,1536]{2,1,0:T(8,128)(2,1)} %copy-done.16), kind=kOutput, calls=%fused_computation.142 | convolution fusion | flops 5375000576 | bytes 20975616 | tf_op jit(solution)/shard_map/dot_general | solution.py:23
  640.9 10.5 %add_add_fusion = f32[1024,1024]{1,0:T(8,128)} fusion(f32[1024,1024]{1,0:T(8,128)} %fusion.2, f32[1024,1024]{1,0:T(8,128)} %fusion.1, s32[1024]{0:T(1024)S(1)} %copy-done.104, f32[1024,1024]{0,1:T(8,128)} %copy-done.32), kind=kOutput, calls=%fused_computation.36 | convolution fusion | flops 2157969408 | bytes 16781312 | tf_op jit(solution)/shard_map/dot_general | solution.py:23
  740.3 6.8 collective-permute-done.88
  752.0 7.7 collective-permute-done.77
  763.4 19.6 %collective-permute-done.51 = bf16[4,256,512]{2,1,0:T(8,128)(2,1)S(1)} collective-permute-done((bf16[4,256,512]{2,1,0:T(8,128)(2,1)}, bf16[4,256,512]{2,1,0:T(8,128)(2,1)S(1)}, u32[]{:S(2)}, u32[]{:S(2)}) %collective-permute-start.51) | collective-permute-done | bytes 1048608 | tf_op jit(solution)/shard_map/ppermute | solution.py:37
  812.3 8.7 collective-permute-done.53
  827.9 13.0 %collective-permute-done.78 = bf16[3,256,768]{2,1,0:T(8,128)(2,1)S(1)} collective-permute-done((bf16[3,256,768]{2,1,0:T(8,128)(2,1)}, bf16[3,256,768]{2,1,0:T(8,128)(2,1)S(1)}, u32[]{:S(2)}, u32[]{:S(2)}) %collective-permute-start.78) | collective-permute-done | bytes 1179680 | tf_op jit(solution)/shard_map/ppermute | solution.py:37
  861.5 10.7 %collective-permute-done.64 = bf16[3,256,768]{2,1,0:T(8,128)(2,1)S(1)} collective-permute-done((bf16[3,256,768]{2,1,0:T(8,128)(2,1)}, bf16[3,256,768]{2,1,0:T(8,128)(2,1)S(1)}, u32[]{:S(2)}, u32[]{:S(2)}) %collective-permute-start.64) | collective-permute-done | bytes 1179680 | tf_op jit(solution)/shard_map/ppermute | solution.py:37
  887.2 25.3 %collective-permute-done.80 = bf16[3,64,768]{2,1,0:T(8,128)(2,1)S(1)} collective-permute-done((bf16[3,64,768]{2,1,0:T(8,128)(2,1)S(1)}, bf16[3,64,768]{2,1,0:T(8,128)(2,1)S(1)}, u32[]{:S(2)}, u32[]{:S(2)}) %collective-permute-start.80) | collective-permute-done | bytes 294944 | tf_op jit(solution)/shard_map/ppermute | solution.py:37
  912.7 10.6 %collective-permute-done.69 = bf16[3,64,768]{2,1,0:T(8,128)(2,1)S(1)} collective-permute-done((bf16[3,64,768]{2,1,0:T(8,128)(2,1)S(1)}, bf16[3,64,768]{2,1,0:T(8,128)(2,1)S(1)}, u32[]{:S(2)}, u32[]{:S(2)}) %collective-permute-start.69) | collective-permute-done | bytes 294944 | tf_op jit(solution)/shard_map/ppermute | solution.py:37
  (584 shorter events, 467.1 us)
Async XLA Ops:
  9.4 44.4 %collective-permute-start.34 = (bf16[3,64,768]{2,1,0:T(8,128)(2,1)S(1)}, bf16[3,64,768]{2,1,0:T(8,128)(2,1)}, u32[]{:S(2)}, u32[]{:S(2)}) collective-permute-start(bf16[3,64,768]{2,1,0:T(8,128)(2,1)S(1)} %get-tuple-element.92), channel_id=1, source_target_pairs={{0,16},{1,17},{2,18},{3,19},{4,20},{5,21},{6,22},{7,23},{8,24},{9,... | collective-permute-start | bytes 884744 | tf_op jit(solution)/shard_map/ppermute | solution.py:37
  10.4 43.5 %collective-permute-start.33 = (bf16[3,64,768]{2,1,0:T(8,128)(2,1)S(1)}, bf16[3,64,768]{2,1,0:T(8,128)(2,1)}, u32[]{:S(2)}, u32[]{:S(2)}) collective-permute-start(bf16[3,64,768]{2,1,0:T(8,128)(2,1)S(1)} %get-tuple-element.92), channel_id=1, source_target_pairs={{0,8},{1,9},{2,10},{3,11},{4,12},{5,13},{6,14},{7,15},{8,0},{9,1},... | collective-permute-start | bytes 884744 | tf_op jit(solution)/shard_map/ppermute | solution.py:37
  13.8 56.2 %collective-permute-start.1 = (bf16[4,64,512]{2,1,0:T(8,128)(2,1)}, bf16[4,64,512]{2,1,0:T(8,128)(2,1)}, u32[]{:S(2)}, u32[]{:S(2)}) collective-permute-start(bf16[4,64,512]{2,1,0:T(8,128)(2,1)} %pad_maximum_fusion.18), channel_id=1, source_target_pairs={{0,16},{1,17},{2,18},{3,19},{4,20},{5,21},{6,22},{7,23},{8,24},{9,... | collective-permute-start | bytes 786440 | tf_op jit(solution)/shard_map/ppermute | solution.py:37
  22.2 49.2 %collective-permute-start = (bf16[4,64,512]{2,1,0:T(8,128)(2,1)}, bf16[4,64,512]{2,1,0:T(8,128)(2,1)}, u32[]{:S(2)}, u32[]{:S(2)}) collective-permute-start(bf16[4,64,512]{2,1,0:T(8,128)(2,1)} %pad_maximum_fusion.18), channel_id=1, source_target_pairs={{0,8},{1,9},{2,10},{3,11},{4,12},{5,13},{6,14},{7,15},{8,0},{9,1},... | collective-permute-start | bytes 786440 | tf_op jit(solution)/shard_map/ppermute | solution.py:37
  69.9 50.5 %collective-permute-start.37 = (bf16[3,256,768]{2,1,0:T(8,128)(2,1)}, bf16[3,256,768]{2,1,0:T(8,128)(2,1)}, u32[]{:S(2)}, u32[]{:S(2)}) collective-permute-start(bf16[3,256,768]{2,1,0:T(8,128)(2,1)} %pad_maximum_fusion.7), channel_id=1, source_target_pairs={{0,4},{1,5},{2,6},{3,7},{4,0},{5,1},{6,2},{7,3},{8,12},{9,13},{10,... | collective-permute-start | bytes 3538952 | tf_op jit(solution)/shard_map/ppermute | solution.py:37
  73.5 43.9 %collective-permute-start.4 = (bf16[4,256,512]{2,1,0:T(8,128)(2,1)}, bf16[4,256,512]{2,1,0:T(8,128)(2,1)}, u32[]{:S(2)}, u32[]{:S(2)}) collective-permute-start(bf16[4,256,512]{2,1,0:T(8,128)(2,1)} %pad_maximum_fusion.14), channel_id=1, source_target_pairs={{0,4},{1,5},{2,6},{3,7},{4,0},{5,1},{6,2},{7,3},{8,12},{9,13},{10,... | collective-permute-start | bytes 3145736 | tf_op jit(solution)/shard_map/ppermute | solution.py:37
  74.0 44.9 %collective-permute-start.3 = (bf16[4,256,512]{2,1,0:T(8,128)(2,1)}, bf16[4,256,512]{2,1,0:T(8,128)(2,1)}, u32[]{:S(2)}, u32[]{:S(2)}) collective-permute-start(bf16[4,256,512]{2,1,0:T(8,128)(2,1)} %pad_maximum_fusion.14), channel_id=1, source_target_pairs={{0,1},{1,0},{2,3},{3,2},{4,5},{5,4},{6,7},{7,6},{8,9},{9,8},{10,11... | collective-permute-start | bytes 3145736 | tf_op jit(solution)/shard_map/ppermute | solution.py:37
  117.4 44.5 %collective-permute-start.25 = (bf16[3,256,768]{2,1,0:T(8,128)(2,1)}, bf16[3,256,768]{2,1,0:T(8,128)(2,1)S(1)}, u32[]{:S(2)}, u32[]{:S(2)}) collective-permute-start(bf16[3,256,768]{2,1,0:T(8,128)(2,1)} %pad_maximum_fusion.6), channel_id=1, source_target_pairs={{0,1},{1,0},{2,3},{3,2},{4,5},{5,4},{6,7},{7,6},{8,9},{9,8},{10,11... | collective-permute-start | bytes 3538952 | tf_op jit(solution)/shard_map/ppermute | solution.py:37
  118.9 49.3 %collective-permute-start.15 = (bf16[3,256,768]{2,1,0:T(8,128)(2,1)}, bf16[3,256,768]{2,1,0:T(8,128)(2,1)}, u32[]{:S(2)}, u32[]{:S(2)}) collective-permute-start(bf16[3,256,768]{2,1,0:T(8,128)(2,1)} %pad_maximum_fusion.5), channel_id=1, source_target_pairs={{0,4},{1,5},{2,6},{3,7},{4,0},{5,1},{6,2},{7,3},{8,12},{9,13},{10,... | collective-permute-start | bytes 3538952 | tf_op jit(solution)/shard_map/ppermute | solution.py:37
  120.4 66.9 %collective-permute-start.14 = (bf16[3,256,768]{2,1,0:T(8,128)(2,1)}, bf16[3,256,768]{2,1,0:T(8,128)(2,1)}, u32[]{:S(2)}, u32[]{:S(2)}) collective-permute-start(bf16[3,256,768]{2,1,0:T(8,128)(2,1)} %pad_maximum_fusion.5), channel_id=1, source_target_pairs={{0,1},{1,0},{2,3},{3,2},{4,5},{5,4},{6,7},{7,6},{8,9},{9,8},{10,11... | collective-permute-start | bytes 3538952 | tf_op jit(solution)/shard_map/ppermute | solution.py:37
  136.8 61.8 %collective-permute-start.5 = (bf16[4,128,512]{2,1,0:T(8,128)(2,1)S(1)}, bf16[4,128,512]{2,1,0:T(8,128)(2,1)}, u32[]{:S(2)}, u32[]{:S(2)}) collective-permute-start(bf16[4,128,512]{2,1,0:T(8,128)(2,1)S(1)} %slice.506), channel_id=1, source_target_pairs={{0,1},{1,0},{2,3},{3,2},{4,5},{5,4},{6,7},{7,6},{8,9},{9,8},{10,11... | collective-permute-start | bytes 1572872 | tf_op jit(solution)/shard_map/ppermute | solution.py:37
  142.8 59.2 %collective-permute-start.6 = (bf16[4,128,512]{2,1,0:T(8,128)(2,1)}, bf16[4,128,512]{2,1,0:T(8,128)(2,1)}, u32[]{:S(2)}, u32[]{:S(2)}) collective-permute-start(bf16[4,128,512]{2,1,0:T(8,128)(2,1)} %slice.507), channel_id=1, source_target_pairs={{0,4},{1,5},{2,6},{3,7},{4,0},{5,1},{6,2},{7,3},{8,12},{9,13},{10,... | collective-permute-start | bytes 1572872 | tf_op jit(solution)/shard_map/ppermute | solution.py:37
  161.9 49.2 %collective-permute-start.38 = (bf16[3,128,768]{2,1,0:T(8,128)(2,1)}, bf16[3,128,768]{2,1,0:T(8,128)(2,1)S(1)}, u32[]{:S(2)}, u32[]{:S(2)}) collective-permute-start(bf16[3,128,768]{2,1,0:T(8,128)(2,1)} %slice.530), channel_id=1, source_target_pairs={{0,1},{1,0},{2,3},{3,2},{4,5},{5,4},{6,7},{7,6},{8,9},{9,8},{10,11... | collective-permute-start | bytes 1769480 | tf_op jit(solution)/shard_map/ppermute | solution.py:37
  245.3 68.7 %collective-permute-start.40 = (bf16[3,256,768]{2,1,0:T(8,128)(2,1)}, bf16[3,256,768]{2,1,0:T(8,128)(2,1)}, u32[]{:S(2)}, u32[]{:S(2)}) collective-permute-start(bf16[3,256,768]{2,1,0:T(8,128)(2,1)} %pad_maximum_fusion.7), channel_id=1, source_target_pairs={{0,2},{1,3},{2,0},{3,1},{4,6},{5,7},{6,4},{7,5},{8,10},{9,11},{10,... | collective-permute-start | bytes 3538952 | tf_op jit(solution)/shard_map/ppermute | solution.py:37
  245.4 123.9 %collective-permute-start.29 = (bf16[3,256,768]{2,1,0:T(8,128)(2,1)}, bf16[3,256,768]{2,1,0:T(8,128)(2,1)}, u32[]{:S(2)}, u32[]{:S(2)}) collective-permute-start(bf16[3,256,768]{2,1,0:T(8,128)(2,1)} %pad_maximum_fusion.6), channel_id=1, source_target_pairs={{0,2},{1,3},{2,0},{3,1},{4,6},{5,7},{6,4},{7,5},{8,10},{9,11},{10,... | collective-permute-start | bytes 3538952 | tf_op jit(solution)/shard_map/ppermute | solution.py:37
  245.9 68.3 %collective-permute-start.42 = (bf16[3,256,768]{2,1,0:T(8,128)(2,1)}, bf16[3,256,768]{2,1,0:T(8,128)(2,1)}, u32[]{:S(2)}, u32[]{:S(2)}) collective-permute-start(bf16[3,256,768]{2,1,0:T(8,128)(2,1)} %collective-permute-done.37), channel_id=1, source_target_pairs={{0,2},{1,3},{2,0},{3,1},{4,6},{5,7},{6,4},{7,5},{8,10},{9,11},{10,... | collective-permute-start | bytes 3538952 | tf_op jit(solution)/shard_map/ppermute | solution.py:37
  246.0 68.6 %collective-permute-start.41 = (bf16[3,256,768]{2,1,0:T(8,128)(2,1)}, bf16[3,256,768]{2,1,0:T(8,128)(2,1)}, u32[]{:S(2)}, u32[]{:S(2)}) collective-permute-start(bf16[3,256,768]{2,1,0:T(8,128)(2,1)} %collective-permute-done.36), channel_id=1, source_target_pairs={{0,2},{1,3},{2,0},{3,1},{4,6},{5,7},{6,4},{7,5},{8,10},{9,11},{10,... | collective-permute-start | bytes 3538952 | tf_op jit(solution)/shard_map/ppermute | solution.py:37
  246.5 69.0 %collective-permute-start.43 = (bf16[3,256,768]{2,1,0:T(8,128)(2,1)}, bf16[3,256,768]{2,1,0:T(8,128)(2,1)}, u32[]{:S(2)}, u32[]{:S(2)}) collective-permute-start(bf16[3,256,768]{2,1,0:T(8,128)(2,1)} %constant_dynamic-update-slice_fusion.6), channel_id=1, source_target_pairs={{0,2},{1,3},{2,0},{3,1},{4,6},{5,7},{6,4},{7,5},{8,10},{9,11},{10,... | collective-permute-start | bytes 3538952 | tf_op jit(solution)/shard_map/ppermute | solution.py:37
  314.0 153.2 %collective-permute-start.18 = (bf16[3,256,768]{2,1,0:T(8,128)(2,1)}, bf16[3,256,768]{2,1,0:T(8,128)(2,1)S(1)}, u32[]{:S(2)}, u32[]{:S(2)}) collective-permute-start(bf16[3,256,768]{2,1,0:T(8,128)(2,1)} %pad_maximum_fusion.5), channel_id=1, source_target_pairs={{0,2},{1,3},{2,0},{3,1},{4,6},{5,7},{6,4},{7,5},{8,10},{9,11},{10,... | collective-permute-start | bytes 3538952 | tf_op jit(solution)/shard_map/ppermute | solution.py:37
  314.3 55.3 %collective-permute-start.31 = (bf16[3,256,768]{2,1,0:T(8,128)(2,1)S(1)}, bf16[3,256,768]{2,1,0:T(8,128)(2,1)S(1)}, u32[]{:S(2)}, u32[]{:S(2)}) collective-permute-start(bf16[3,256,768]{2,1,0:T(8,128)(2,1)S(1)} %copy-done.42), channel_id=1, source_target_pairs={{0,2},{1,3},{2,0},{3,1},{4,6},{5,7},{6,4},{7,5},{8,10},{9,11},{10,... | collective-permute-start | bytes 3538952 | tf_op jit(solution)/shard_map/ppermute | solution.py:37
  315.3 54.4 %collective-permute-start.30 = (bf16[3,256,768]{2,1,0:T(8,128)(2,1)S(1)}, bf16[3,256,768]{2,1,0:T(8,128)(2,1)}, u32[]{:S(2)}, u32[]{:S(2)}) collective-permute-start(bf16[3,256,768]{2,1,0:T(8,128)(2,1)S(1)} %copy-done.44), channel_id=1, source_target_pairs={{0,2},{1,3},{2,0},{3,1},{4,6},{5,7},{6,4},{7,5},{8,10},{9,11},{10,... | collective-permute-start | bytes 3538952 | tf_op jit(solution)/shard_map/ppermute | solution.py:37
  316.2 53.9 %collective-permute-start.32 = (bf16[3,256,768]{2,1,0:T(8,128)(2,1)S(1)}, bf16[3,256,768]{2,1,0:T(8,128)(2,1)}, u32[]{:S(2)}, u32[]{:S(2)}) collective-permute-start(bf16[3,256,768]{2,1,0:T(8,128)(2,1)S(1)} %copy-done.48), channel_id=1, source_target_pairs={{0,2},{1,3},{2,0},{3,1},{4,6},{5,7},{6,4},{7,5},{8,10},{9,11},{10,... | collective-permute-start | bytes 3538952 | tf_op jit(solution)/shard_map/ppermute | solution.py:37
  369.3 98.0 %collective-permute-start.20 = (bf16[3,256,768]{2,1,0:T(8,128)(2,1)}, bf16[3,256,768]{2,1,0:T(8,128)(2,1)S(1)}, u32[]{:S(2)}, u32[]{:S(2)}) collective-permute-start(bf16[3,256,768]{2,1,0:T(8,128)(2,1)} %collective-permute-done.15), channel_id=1, source_target_pairs={{0,2},{1,3},{2,0},{3,1},{4,6},{5,7},{6,4},{7,5},{8,10},{9,11},{10,... | collective-permute-start | bytes 3538952 | tf_op jit(solution)/shard_map/ppermute | solution.py:37
  369.6 97.7 %collective-permute-start.19 = (bf16[3,256,768]{2,1,0:T(8,128)(2,1)}, bf16[3,256,768]{2,1,0:T(8,128)(2,1)}, u32[]{:S(2)}, u32[]{:S(2)}) collective-permute-start(bf16[3,256,768]{2,1,0:T(8,128)(2,1)} %collective-permute-done.14), channel_id=1, source_target_pairs={{0,2},{1,3},{2,0},{3,1},{4,6},{5,7},{6,4},{7,5},{8,10},{9,11},{10,... | collective-permute-start | bytes 3538952 | tf_op jit(solution)/shard_map/ppermute | solution.py:37
  369.8 97.5 %collective-permute-start.21 = (bf16[3,256,768]{2,1,0:T(8,128)(2,1)S(1)}, bf16[3,256,768]{2,1,0:T(8,128)(2,1)}, u32[]{:S(2)}, u32[]{:S(2)}) collective-permute-start(bf16[3,256,768]{2,1,0:T(8,128)(2,1)S(1)} %copy-done.46), channel_id=1, source_target_pairs={{0,2},{1,3},{2,0},{3,1},{4,6},{5,7},{6,4},{7,5},{8,10},{9,11},{10,... | collective-permute-start | bytes 3538952 | tf_op jit(solution)/shard_map/ppermute | solution.py:37
  616.8 45.7 %collective-permute-start.55 = (f32[5,1024]{1,0:T(8,128)S(1)}, f32[5,1024]{1,0:T(8,128)S(1)}, u32[]{:S(2)}, u32[]{:S(2)}) collective-permute-start(f32[5,1024]{1,0:T(8,128)S(1)} %pad_maximum_fusion.19), channel_id=1, source_target_pairs={{0,2},{1,3},{2,0},{3,1},{4,6},{5,7},{6,4},{7,5},{8,10},{9,11},{10,... | collective-permute-start | bytes 61448 | tf_op jit(solution)/shard_map/ppermute | solution.py:37
  626.3 57.6 %collective-permute-start.49 = (bf16[4,256,512]{2,1,0:T(8,128)(2,1)}, bf16[4,256,512]{2,1,0:T(8,128)(2,1)}, u32[]{:S(2)}, u32[]{:S(2)}) collective-permute-start(bf16[4,256,512]{2,1,0:T(8,128)(2,1)} %get-tuple-element.62), channel_id=1, source_target_pairs={{0,2},{1,3},{2,0},{3,1},{4,6},{5,7},{6,4},{7,5},{8,10},{9,11},{10,... | collective-permute-start | bytes 3145736 | tf_op jit(solution)/shard_map/ppermute | solution.py:37
  626.6 57.8 %collective-permute-start.46 = (bf16[4,256,512]{2,1,0:T(8,128)(2,1)}, bf16[4,256,512]{2,1,0:T(8,128)(2,1)}, u32[]{:S(2)}, u32[]{:S(2)}) collective-permute-start(bf16[4,256,512]{2,1,0:T(8,128)(2,1)} %get-tuple-element.63), channel_id=1, source_target_pairs={{0,2},{1,3},{2,0},{3,1},{4,6},{5,7},{6,4},{7,5},{8,10},{9,11},{10,... | collective-permute-start | bytes 3145736 | tf_op jit(solution)/shard_map/ppermute | solution.py:37
  626.8 61.2 %collective-permute-start.45 = (bf16[4,256,512]{2,1,0:T(8,128)(2,1)}, bf16[4,256,512]{2,1,0:T(8,128)(2,1)}, u32[]{:S(2)}, u32[]{:S(2)}) collective-permute-start(bf16[4,256,512]{2,1,0:T(8,128)(2,1)} %get-tuple-element.64), channel_id=1, source_target_pairs={{0,2},{1,3},{2,0},{3,1},{4,6},{5,7},{6,4},{7,5},{8,10},{9,11},{10,... | collective-permute-start | bytes 3145736 | tf_op jit(solution)/shard_map/ppermute | solution.py:37
  707.6 54.2 %collective-permute-start.44 = (bf16[4,256,512]{2,1,0:T(8,128)(2,1)}, bf16[4,256,512]{2,1,0:T(8,128)(2,1)}, u32[]{:S(2)}, u32[]{:S(2)}) collective-permute-start(bf16[4,256,512]{2,1,0:T(8,128)(2,1)} %get-tuple-element.61), channel_id=1, source_target_pairs={{0,2},{1,3},{2,0},{3,1},{4,6},{5,7},{6,4},{7,5},{8,10},{9,11},{10,... | collective-permute-start | bytes 3145736 | tf_op jit(solution)/shard_map/ppermute | solution.py:37
  761.7 61.5 %collective-permute-start.71 = (bf16[3,256,768]{2,1,0:T(8,128)(2,1)S(1)}, bf16[3,256,768]{2,1,0:T(8,128)(2,1)}, u32[]{:S(2)}, u32[]{:S(2)}) collective-permute-start(bf16[3,256,768]{2,1,0:T(8,128)(2,1)S(1)} %copy-done.67), channel_id=1, source_target_pairs={{0,2},{1,3},{2,0},{3,1},{4,6},{5,7},{6,4},{7,5},{8,10},{9,11},{10,... | collective-permute-start | bytes 3538952 | tf_op jit(solution)/shard_map/ppermute | solution.py:37
  823.7 48.4 %collective-permute-start.64 = (bf16[3,256,768]{2,1,0:T(8,128)(2,1)}, bf16[3,256,768]{2,1,0:T(8,128)(2,1)S(1)}, u32[]{:S(2)}, u32[]{:S(2)}) collective-permute-start(bf16[3,256,768]{2,1,0:T(8,128)(2,1)} %pad_maximum_fusion.8), channel_id=1, source_target_pairs={{0,4},{1,5},{2,6},{3,7},{4,0},{5,1},{6,2},{7,3},{8,12},{9,13},{10,... | collective-permute-start | bytes 3538952 | tf_op jit(solution)/shard_map/ppermute | solution.py:37
  (183 other events, 4090.5 us)

commit v2 on v1

v2 whole, which is shorter than its diff:
```python
import functools

import jax
import jax.numpy as jnp
from jax import lax
from jax.experimental import pallas as pl
from jax.experimental.pallas import tpu as pltpu
from jax.sharding import PartitionSpec as P

SLOTS = 1024
EPS = 1e-05
AXES = ("dp", "tensor")
SIZES = (256, 256, 256, 256, 128)
MIXER_PARTS = 2
MIXER_TILE = 128
ROW_TILE = 256
COST = 4
VMEM = 60 * 2**20
BF = jnp.bfloat16
F32 = jnp.float32
ANYWHERE = pl.BlockSpec(memory_space=pl.ANY)


def dot_nn(left, right):
    return jnp.dot(left, right, preferred_element_type=F32)


def dot_tn(left, right):
    return lax.dot_general(left, right, (((0,), (0,)), ((), ())), preferred_element_type=F32)


def dot_nt(left, right):
    return lax.dot_general(left, right, (((1,), (1,)), ((), ())), preferred_element_type=F32)


class Links:
    def __init__(self, dp, tp):
        self.dp, self.tp, self.zs = dp, tp, dp // 4

    def swap(self, value, x=0, c=0, y=0, z=0):
        flip = (z * 2 + x) * 2 + c
        pairs = [
            (q * self.tp + t, (q ^ flip) * self.tp + (t ^ y))
            for q in range(self.dp)
            for t in range(self.tp)
        ]
        return lax.ppermute(value, AXES, pairs)

    def turn_z(self, value):
        groups = [[z * 4 + rest for z in range(self.zs)] for rest in range(4)]
        return lax.all_to_all(value, "dp", 0, 0, axis_index_groups=groups, tiled=True)

    def gather_z(self, own):
        return self.turn_z(jnp.broadcast_to(own[None], (self.zs, *own.shape)))

    def gather_sides(self, mine):
        return self.swap(mine, x=1), self.swap(mine, y=1)

    def gather_corner(self, from_x, from_y):
        half = self.zs // 2
        return self.swap(from_x[:half], y=1), self.swap(from_y[half:], x=1)

    def sum_all(self, value):
        value = value + self.swap(value, c=1)
        value = value + self.swap(value, x=1)
        value = value + self.swap(value, y=1)
        step = 1
        while step < self.zs:
            value = value + self.swap(value, z=step)
            step *= 2
        return value

    def absolute(self, place):
        q = lax.axis_index("dp")
        core, x, z = place // (2 * self.zs), place // self.zs % 2, place % self.zs
        return z * 4 + ((q % 4) ^ (x * 2 + core))

    def place(self, absolute):
        q = lax.axis_index("dp")
        apart = (absolute % 4) ^ (q % 4)
        return ((apart % 2) * 2 + apart // 2) * self.zs + absolute // 4


def whole_spec(shape, buffers=1):
    return pl.BlockSpec(
        shape, lambda *_: (0,) * len(shape), pipeline_mode=pl.Buffered(buffers)
    )


def params():
    return pltpu.CompilerParams(vmem_limit_bytes=VMEM)


def cost(flops, moved_bytes):
    return pl.CostEstimate(flops=flops, bytes_accessed=moved_bytes, transcendentals=0)


def small_call(kernel, inputs, out_shapes, work):
    columns = inputs[0].shape[-1]

    def spec(shape):
        lead = len(shape) - 1
        return pl.BlockSpec(
            (*shape[:-1], 128), lambda j: (*(0,) * lead, j)
        )

    return pl.pallas_call(
        kernel,
        grid=(columns // 128,),
        in_specs=[spec(item.shape) for item in inputs],
        out_specs=[spec(shape) for shape in out_shapes],
        out_shape=[jax.ShapeDtypeStruct(shape, BF) for shape in out_shapes],
        compiler_params=params(),
        cost_estimate=cost(0, 2 * work),
    )(*inputs)


def join_kernel(mine, from_y, from_x, one, two, out):
    half = one.shape[0]
    out[0] = mine[...]
    out[1] = from_y[...]
    out[2] = from_x[...]
    out[3, :half] = one[...]
    out[3, half:] = two[...]


def join(mine, from_y, from_x, one, two):
    shape = (4, *mine.shape)
    return small_call(
        join_kernel, [mine, from_y, from_x, one, two], [shape], 8 * mine.size
    )[0]


def both_kernel(keep, got, send_x, send_y, rest_x, rest_y, own):
    half = keep.shape[1] // 2

    def total(cell, part):
        return (keep[cell, part].astype(F32) + got[cell, part].astype(F32)).astype(BF)

    low, high = slice(0, half), slice(half, 2 * half)
    send_x[0], send_x[1] = total(3, low), total(2, low)
    send_y[0], send_y[1] = total(3, high), total(1, high)
    rest_x[...], rest_y[...] = total(2, high), total(1, low)
    own[:half], own[half:] = total(0, low), total(0, high)


def both_cores(keep, got):
    _, zs, *rest = keep.shape
    part = (zs // 2, *rest)
    shapes = [(2, *part), (2, *part), part, part, (zs, *rest)]
    return small_call(both_kernel, [keep, got], shapes, 3 * keep.size)


def sides_kernel(rest_x, rest_y, got_x, got_y, send_x, send_y):
    send_x[...] = (rest_x[...].astype(F32) + got_y[0].astype(F32)).astype(BF)
    send_y[...] = (rest_y[...].astype(F32) + got_x[0].astype(F32)).astype(BF)


def add_sides(rest_x, rest_y, got_x, got_y):
    return small_call(
        sides_kernel, [rest_x, rest_y, got_x, got_y], [rest_x.shape] * 2, 8 * rest_x.size
    )


def own_kernel(own, got_x, got_y, side_x, side_y, out):
    half = side_x.shape[0]
    low = own[:half].astype(F32) + got_x[1].astype(F32) + side_y[...].astype(F32)
    high = own[half:].astype(F32) + got_y[1].astype(F32) + side_x[...].astype(F32)
    out[:half] = low.astype(BF)
    out[half:] = high.astype(BF)


def add_own(own, got_x, got_y, side_x, side_y):
    return small_call(
        own_kernel, [own, got_x, got_y, side_x, side_y], [own.shape], 5 * own.size
    )[0]


def ffn_kernel(first, last, ties, *refs):
    feed = iter(refs)
    take = lambda n: [next(feed) for _ in range(n)]
    normed, normed_twin, grad_out, grad_out_twin = take(4)
    mine, from_y, from_x, one, two = take(5)
    before = [] if first else take(4)
    take(ties)
    send_x, send_y, rest_x, rest_y, own = take(5)
    totals = take(4)
    wide, rows_n, rows_g, active, grad_gate, grad_up = take(6)
    step = pl.program_id(0)
    steps = pl.num_programs(0)
    zs, _, kinds, block, tile = mine.shape
    half = zs // 2
    height = normed.shape[0]
    places = [(core, x, z) for core in range(2) for x in range(2) for z in range(zs)]

    @pl.when(step == 0)
    def _():
        for at, (core, x, z) in enumerate(places):
            rows = slice(at * block, (at + 1) * block)
            for k in range(kinds):
                if x == 0:
                    wide[k, rows, :tile] = mine[z, core, k]
                    wide[k, rows, tile:] = from_y[z, core, k]
                else:
                    wide[k, rows, :tile] = from_x[z, core, k]
                    corner = one[z, core, k] if z < half else two[z - half, core, k]
                    wide[k, rows, tile:] = corner

    at = pl.ds(pl.multiple_of(step * height, height), height)

    def work(normed, grad_out, before, totals, turn):
        left = normed[...]
        right = grad_out[...]
        rows_n[at, :] = left
        rows_g[at, :] = right
        gate, upward = dot_nn(left, wide[0]), dot_nn(left, wide[1])
        grad_active = dot_nn(right, wide[2])
        sigma = 1.0 / (1.0 + jnp.exp(-gate))
        silu = gate * sigma
        act = (silu * upward).astype(BF)
        g_up = (grad_active * silu).astype(BF)
        g_gate = (grad_active * upward * (sigma + silu * (1.0 - sigma))).astype(BF)
        active[at, :] = act
        grad_up[at, :] = g_up
        grad_gate[at, :] = g_gate
        ffn = dot_nt(act, wide[2])
        back = dot_nt(g_gate, wide[0]) + dot_nt(g_up, wide[1])
        if not first:
            ffn = ffn + before[0][...]
            back = back + before[1][...]
        if turn:
            ffn, back = other_core_first(ffn), other_core_first(back)
        totals[0][...] = ffn.astype(totals[0].dtype)
        totals[1][...] = back.astype(totals[1].dtype)

    @pl.when(step < steps // 2)
    def _():
        work(normed, grad_out, before[:2], totals[:2], False)

    @pl.when(step >= steps // 2)
    def _():
        work(normed_twin, grad_out_twin, before[2:], totals[2:], last)

    @pl.when(step == steps - 1)
    def _():
        group = 256 // block
        for first_place in range(0, len(places), group):
            rows = slice(first_place * block, (first_place + group) * block)
            for k, (left, right) in enumerate(
                ((rows_n, grad_gate), (rows_n, grad_up), (rows_g, active))
            ):
                value = dot_tn(left[:, rows], right[...]).astype(BF)
                for i in range(group):
                    core, x, z = places[first_place + i]
                    part = value[i * block : (i + 1) * block]
                    low, zh = z < half, z % half
                    near, far = part[:, :tile], part[:, tile:]
                    if x == 0:
                        own[z, core, k] = near
                        if low:
                            rest_y[zh, core, k] = far
                        else:
                            send_y[1, zh, core, k] = far
                    else:
                        if low:
                            send_x[1, zh, core, k] = near
                            send_x[0, zh, core, k] = far
                        else:
                            rest_x[zh, core, k] = near
                            send_y[0, zh, core, k] = far


def ffn_piece(inputs, cells, before, last, ties):
    rows, width = inputs[0].shape
    zs, _, kinds, block, columns = cells[0].shape
    first = before is None
    height = min(ROW_TILE, rows)
    half = rows // height
    near = pl.BlockSpec((height, width), lambda i: (jnp.minimum(i, half - 1), 0))
    far = pl.BlockSpec((height, width), lambda i: (jnp.maximum(i - half, 0), 0))
    operands = [*inputs, *cells, *(() if first else before), *ties]
    part = (zs // 2, 2, kinds, block, columns)
    grads = [(2, *part), (2, *part), part, part, (zs, *part[1:])]
    twin = BF if last else F32
    return pl.pallas_call(
        functools.partial(ffn_kernel, first, last, len(ties)),
        grid=(2 * half,),
        in_specs=[near, far, near, far]
        + [whole_spec(item.shape) for item in cells]
        + ([] if first else [near, near, far, far])
        + [ANYWHERE] * len(ties),
        out_specs=[whole_spec(shape) for shape in grads] + [near, near, far, far],
        out_shape=[jax.ShapeDtypeStruct(shape, BF) for shape in grads]
        + [jax.ShapeDtypeStruct((rows, width), dtype) for dtype in (F32, F32, twin, twin)],
        scratch_shapes=[pltpu.VMEM((kinds, width, 2 * columns), BF)]
        + [pltpu.VMEM((2 * rows, width), BF)] * 2
        + [pltpu.VMEM((2 * rows, 2 * columns), BF)] * 3,
        compiler_params=params(),
        cost_estimate=cost(
            72 * COST * rows * width * columns, 24 * width * columns + 40 * rows * width
        ),
    )(*operands)


def lay_out(near, twin, wide):
    _, zs, kinds, block, tile = near.shape
    for core, cells in enumerate((near, twin)):
        for x in range(2):
            for z in range(zs):
                at = ((core * 2 + x) * zs + z) * block
                for k in range(kinds):
                    for y in range(2):
                        wide[k, at : at + block, y * tile : (y + 1) * tile] = cells[
                            2 * x + y, z, k
                        ]


def cell_specs(cells, tile):
    return [
        pl.BlockSpec((*item.shape[:-1], tile), lambda j: (0, 0, 0, 0, j)) for item in cells
    ]


def other_core_first(values):
    half = values.shape[1] // 2
    return jnp.concatenate([values[:, half:], values[:, :half]], axis=1)


def moved(values, shift, position):
    rows = values.shape[0]
    turned = pltpu.roll(values, shift % rows, 0)
    inside = position >= shift if shift > 0 else position < rows + shift
    return jnp.where(inside, turned, 0.0)


def mixed_of(gated, conv, position):
    total = conv[0:1] * gated
    for shift in range(1, conv.shape[0]):
        total = total + conv[shift : shift + 1] * moved(gated, shift, position)
    return total


def tile_conv(conv):
    return jnp.concatenate([conv[0], conv[1]], axis=1)


def mixer_kernel(first, last, ties, row_tile, *refs):
    feed = iter(refs)
    take = lambda n: [next(feed) for _ in range(n)]
    lengths, normed, tokens, conv, gain = take(5)
    cells = take(2)
    before = [] if first else take(1)
    take(ties)
    project, hidden = take(2)
    normed_two, for_twin = take(2) if last else (None, None)
    wide, branch = take(2)
    step = pl.program_id(0)
    rows = normed.shape[0]
    lay_out(*cells, wide)

    @pl.loop(0, rows // row_tile)
    def _(i):
        at = pl.ds(pl.multiple_of(i * row_tile, row_tile), row_tile)
        left = normed[at, :]
        for k in range(3):
            project[k, at, :] = dot_nn(left, wide[k])

    taps = tile_conv(conv[...])
    for sequence in range(rows // SLOTS):
        at = slice(sequence * SLOTS, (sequence + 1) * SLOTS)
        position = lax.broadcasted_iota(jnp.int32, (SLOTS, wide.shape[2]), 0)
        gated = project[0, at] * project[2, at]
        gated = jnp.where(position < lengths[sequence], gated, 0.0)
        branch[at, :] = (project[1, at] * mixed_of(gated, taps, position)).astype(BF)

    @pl.when(step == 0)
    def _():
        if first:
            hidden[...] = tokens[...].astype(F32)
        else:
            hidden[...] = before[0][...]

    ending = step == pl.num_programs(0) - 1

    @pl.loop(0, rows // row_tile)
    def _(i):
        at = pl.ds(pl.multiple_of(i * row_tile, row_tile), row_tile)
        value = hidden[at, :] + dot_nt(branch[at, :], wide[3])
        hidden[at, :] = value
        if last:

            @pl.when(ending)
            def _():
                unit = norm_stats(value)[1]
                value_two = (unit * gain[...]).astype(BF)
                normed_two[at, :] = value_two
                for_twin[at, :] = other_core_first(value_two)


def mixer_part(lengths, normed, tokens, conv, gain, cells, before, last, ties):
    rows, width = normed.shape
    _, zs, kinds, block, columns = cells[0].shape
    first = before is None
    tile = MIXER_TILE
    whole = whole_spec((rows, width))
    inputs = [lengths, normed, tokens, conv, gain, *cells]
    inputs += ([] if first else [before]) + list(ties)
    outs = [jax.ShapeDtypeStruct((3, rows, 2 * columns), F32), jax.ShapeDtypeStruct((rows, width), F32)]
    out_specs = [pl.BlockSpec((3, rows, 2 * tile), lambda j: (0, 0, j)), whole]
    if last:
        outs += [jax.ShapeDtypeStruct((rows, width), BF)] * 2
        out_specs += [whole] * 2
    return pl.pallas_call(
        functools.partial(mixer_kernel, first, last, len(ties), min(rows, 256)),
        grid=(columns // tile,),
        in_specs=[pl.BlockSpec(memory_space=pltpu.SMEM), whole, whole]
        + [pl.BlockSpec((2, conv.shape[1], tile), lambda j: (0, 0, j)), whole_spec((1, width))]
        + cell_specs(cells, tile)
        + [whole] * (0 if first else 1)
        + [ANYWHERE] * len(ties),
        out_specs=out_specs,
        out_shape=outs,
        scratch_shapes=[
            pltpu.VMEM((kinds, width, 2 * tile), BF),
            pltpu.VMEM((rows, 2 * tile), BF),
        ],
        input_output_aliases={} if first else {7: 1},
        compiler_params=params(),
        cost_estimate=pl.CostEstimate(
            flops=16 * COST * rows * width * columns,
            bytes_accessed=24 * rows * columns + 16 * width * columns + 8 * rows * width,
            transcendentals=0,
        ),
    )(*inputs)


def mixer_back_kernel(first, ties, row_tile, *refs):
    feed = iter(refs)
    take = lambda n: [next(feed) for _ in range(n)]
    lengths, normed, grad_mix, project, conv = take(5)
    cells = take(2)
    before = [] if first else take(1)
    take(ties)
    keep, send, tap_grads, grad_normed = take(4)
    wide, branch, grads, grad_branch = take(4)
    step = pl.program_id(0)
    rows = normed.shape[0]
    _, zs, _, block, tile = cells[0].shape
    lay_out(*cells, wide)

    @pl.when(step == 0)
    def _():
        grad_normed[...] = jnp.zeros_like(grad_normed) if first else before[0][...]

    @pl.loop(0, rows // row_tile)
    def _(i):
        at = pl.ds(pl.multiple_of(i * row_tile, row_tile), row_tile)
        grad_branch[at, :] = dot_nn(grad_mix[at, :], wide[3])

    taps = tile_conv(conv[...])
    count = taps.shape[0]
    sums = [jnp.zeros((1, 2 * tile), F32)] * count
    for sequence in range(rows // SLOTS):
        at = slice(sequence * SLOTS, (sequence + 1) * SLOTS)
        position = lax.broadcasted_iota(jnp.int32, (SLOTS, 2 * tile), 0)
        living = position < lengths[sequence]
        gated = jnp.where(living, project[0, at] * project[2, at], 0.0)
        mixed = taps[0:1] * gated
        g_mixed = grad_branch[at, :] * project[1, at]
        sums[0] = sums[0] + jnp.sum(g_mixed * gated, axis=0, keepdims=True)
        g_gated = taps[0:1] * g_mixed
        for shift in range(1, count):
            lower = moved(gated, shift, position)
            mixed = mixed + taps[shift : shift + 1] * lower
            sums[shift] = sums[shift] + jnp.sum(g_mixed * lower, axis=0, keepdims=True)
            g_gated = g_gated + taps[shift : shift + 1] * moved(g_mixed, -shift, position)
        g_gated = jnp.where(living, g_gated, 0.0)
        branch[at, :] = (project[1, at] * mixed).astype(BF)
        grads[0, at, :] = (g_gated * project[2, at]).astype(BF)
        grads[1, at, :] = (grad_branch[at, :] * mixed).astype(BF)
        grads[2, at, :] = (g_gated * project[0, at]).astype(BF)
    tap_grads[...] = jnp.concatenate(
        sums + [jnp.zeros((8 - count, 2 * tile), F32)], axis=0
    )

    @pl.loop(0, rows // row_tile)
    def _(i):
        at = pl.ds(pl.multiple_of(i * row_tile, row_tile), row_tile)
        value = dot_nt(grads[0, at, :], wide[0]) + dot_nt(grads[1, at, :], wide[1])
        grad_normed[at, :] += value + dot_nt(grads[2, at, :], wide[2])

    depth = zs * block
    for place in range(4):
        at = slice(place * depth, (place + 1) * depth)
        core, x = divmod(place, 2)
        out = send if core else keep
        for k in range(4):
            if k < 3:
                value = dot_tn(normed[:, at], grads[k])
            else:
                value = dot_tn(grad_mix[:, at], branch[...])
            value = value.astype(BF)
            for z in range(zs):
                part = value[z * block : (z + 1) * block]
                out[2 * x, z, k] = part[:, :tile]
                out[2 * x + 1, z, k] = part[:, tile:]


def mixer_back(lengths, normed, grad_mix, project, conv, cells, before, ties):
    rows, width = normed.shape
    _, zs, kinds, block, columns = cells[0].shape
    first = before is None
    tile = MIXER_TILE
    whole = whole_spec((rows, width))
    inputs = [lengths, normed, grad_mix, project, conv, *cells]
    inputs += ([] if first else [before]) + list(ties)
    grads = pl.BlockSpec((4, zs, kinds, block, tile), lambda j: (0, 0, 0, 0, j))
    grad_shape = jax.ShapeDtypeStruct((4, zs, kinds, block, columns), BF)
    return pl.pallas_call(
        functools.partial(mixer_back_kernel, first, len(ties), min(rows, 256)),
        grid=(columns // tile,),
        in_specs=[pl.BlockSpec(memory_space=pltpu.SMEM), whole, whole]
        + [pl.BlockSpec((3, rows, 2 * tile), lambda j: (0, 0, j))]
        + [pl.BlockSpec((2, conv.shape[1], tile), lambda j: (0, 0, j))]
        + cell_specs(cells, tile)
        + [whole] * (0 if first else 1)
        + [ANYWHERE] * len(ties),
        out_specs=[grads, grads, pl.BlockSpec((8, 2 * tile), lambda j: (0, j)), whole],
        out_shape=[
            grad_shape,
            grad_shape,
            jax.ShapeDtypeStruct((8, 2 * columns), F32),
            jax.ShapeDtypeStruct((rows, width), F32),
        ],
        scratch_shapes=[
            pltpu.VMEM((kinds, width, 2 * tile), BF),
            pltpu.VMEM((rows, 2 * tile), BF),
            pltpu.VMEM((3, rows, 2 * tile), BF),
            pltpu.VMEM((rows, 2 * tile), F32),
        ],
        input_output_aliases={} if first else {7: 3},
        compiler_params=params(),
        cost_estimate=pl.CostEstimate(
            flops=32 * COST * rows * width * columns,
            bytes_accessed=24 * rows * columns + 32 * width * columns + 8 * rows * width,
            transcendentals=0,
        ),
    )(*inputs)


def norm_stats(values):
    inverse = lax.rsqrt(jnp.mean(values * values, axis=-1, keepdims=True) + EPS)
    return (inverse, values * inverse)


def norm_back(grad_normed, gain, inverse, unit):
    scaled = grad_normed * gain
    return inverse * (scaled - unit * jnp.mean(scaled * unit, axis=-1, keepdims=True))


def body(
    tokens,
    lengths,
    in_proj,
    conv_weight,
    out_proj,
    norm_gain,
    ffn_gain,
    w_gate,
    w_up,
    w_down,
    cotangent,
):
    rows, width = tokens.shape
    links = Links(lax.axis_size("dp"), lax.axis_size("tensor"))
    rank = lax.axis_index("tensor")
    kernel = conv_weight.shape[0]
    half = in_proj.shape[2]
    hidden_half = w_gate.shape[1]
    block = width // links.dp

    core = lax.axis_index("dp") % 2
    mixer_own = jnp.concatenate([in_proj.astype(BF), out_proj.T.astype(BF)[None]], axis=0)
    ffn_own = jnp.stack([w_gate.astype(BF), w_up.astype(BF), w_down.T.astype(BF)])
    part = half // MIXER_PARTS
    mixer_parts = [mixer_own[:, :, p * part : (p + 1) * part] for p in range(MIXER_PARTS)]
    shared = hidden_half // 2
    mine_of = lax.dynamic_slice_in_dim(ffn_own, core * shared, shared, 2)
    twin_of = lax.dynamic_slice_in_dim(ffn_own, (1 - core) * shared, shared, 2)
    ffn_both = jnp.stack([mine_of, links.swap(twin_of, c=1)])
    starts = [sum(SIZES[:p]) for p in range(len(SIZES))]
    own = mixer_parts + [
        ffn_both[..., at : at + size] for at, size in zip(starts, SIZES)
    ]
    pieces = len(own)
    mine, sides, corner, mixer_cells = {}, {}, {}, {}

    def cells(p):
        from_x, from_y = sides[p]
        return [mine[p], from_y, from_x, *corner[p]]

    def gather_stage(p, stage):
        if stage == 0:
            mine[p] = links.gather_z(own[p])
            return [mine[p]]
        if stage == 1:
            sides[p] = links.gather_sides(mine[p])
            return list(sides[p])
        if stage == 2:
            corner[p] = links.gather_corner(*sides[p])
            return list(corner[p])
        joined = join(*cells(p))
        mixer_cells[p] = [joined, links.swap(joined, c=1)]
        return []

    def gather_slot(p, stage):
        return p if stage == 3 else p + stage - (3 if p < MIXER_PARTS else 2)

    sums = {}

    def sum_stage(p, stage):
        item = sums[p]
        if stage == 1:
            got = links.swap(item["send"], c=1)
            item["parts"] = both_cores(item["keep"], got)
            return [got]
        send_x, send_y, rest_x, rest_y, mine_here = item["parts"]
        if stage == 2:
            item["got"] = links.swap(send_x, x=1), links.swap(send_y, y=1)
            return list(item["got"])
        if stage == 3:
            next_x, next_y = add_sides(rest_x, rest_y, *item["got"])
            item["sides"] = links.swap(next_x, x=1), links.swap(next_y, y=1)
            return list(item["sides"])
        item["z"] = links.turn_z(add_own(mine_here, *item["got"], *item["sides"]))
        return [item["z"]]

    done = set()

    def arrive(slot):
        ties = []
        for p in range(pieces):
            for stage in range(4 if p < MIXER_PARTS else 3):
                if (p, stage) not in done and gather_slot(p, stage) <= slot:
                    done.add((p, stage))
                    ties += gather_stage(p, stage)
        for p in list(sums):
            begin = 1 if p < MIXER_PARTS else 2
            for stage in range(begin, 5):
                due = sums[p]["slot"] + 2 + stage - begin
                if (p, -stage) not in done and due <= slot:
                    done.add((p, -stage))
                    ties += sum_stage(p, stage)
        return ties

    blocks = links.absolute(jnp.arange(links.dp))
    feature = jnp.repeat(blocks, block) * block + jnp.tile(jnp.arange(block), links.dp)
    order = (jnp.arange(width)[:, None] == feature[None, :]).astype(BF)
    tokens_f = dot_nn(tokens, order)
    cot = dot_nn(cotangent, order)
    gain_one = jnp.take(norm_gain.reshape(links.dp, block), blocks, axis=0).reshape(width)
    gain_two = jnp.take(ffn_gain.reshape(links.dp, block), blocks, axis=0).reshape(width)
    conv = jnp.where(rank == 0, conv_weight, jnp.roll(conv_weight, half, axis=1))

    count = rows // SLOTS
    own_lengths = lax.dynamic_slice_in_dim(lengths, rank * count, count)
    position = jnp.tile(jnp.arange(SLOTS, dtype=jnp.int32), count)
    alive = (position < jnp.repeat(own_lengths, SLOTS)).astype(F32)[:, None]
    conv = conv.reshape(kernel, 2, half).transpose(1, 0, 2)

    inverse_one, unit_one = norm_stats(tokens_f)
    normed = (unit_one * gain_one).astype(BF)
    grad_ffn = (cot * alive).astype(BF)
    grad_ffn_twin = links.swap(other_core_first(grad_ffn), c=1)
    tokens_low = tokens_f.astype(BF)

    slot = 0
    hidden, projects = None, []
    for p in range(MIXER_PARTS):
        ties = arrive(slot)
        last = p == MIXER_PARTS - 1
        project, hidden, *rest = mixer_part(
            own_lengths, normed, tokens_low, conv[:, :, p * part : (p + 1) * part],
            gain_two[None], mixer_cells[p], hidden, last, ties,
        )
        projects.append(project)
        slot += 1
    normed_two, for_twin = rest
    inputs = [normed_two, links.swap(for_twin, c=1), grad_ffn, grad_ffn_twin]

    totals = None
    for p in range(MIXER_PARTS, pieces):
        ties = arrive(slot)
        *parts, t0, t1, t2, t3 = ffn_piece(inputs, cells(p), totals, p == pieces - 1, ties)
        totals = [t0, t1, t2, t3]
        sums[p] = dict(parts=parts, slot=slot)
        slot += 1
    grad_normed_two = totals[1] + links.swap(totals[3], c=1).astype(F32)
    ffn_out = totals[0] + links.swap(totals[2], c=1).astype(F32)
    result = dot_nt((hidden + ffn_out).astype(BF), order).astype(BF)

    inverse_two, unit_two = norm_stats(hidden)
    grad_out = grad_ffn.astype(F32)
    gain_two_part = jnp.sum(grad_normed_two * unit_two, axis=0)
    grad_hidden = grad_out + norm_back(grad_normed_two, gain_two, inverse_two, unit_two)
    grad_mix = grad_hidden.astype(BF)
    grad_normed, tap_grads = None, [None] * MIXER_PARTS
    for p in reversed(range(MIXER_PARTS)):
        ties = arrive(slot)
        keep, send, tap_grads[p], grad_normed = mixer_back(
            own_lengths, normed, grad_mix, projects[p], conv[:, :, p * part : (p + 1) * part],
            mixer_cells[p], grad_normed, ties,
        )
        sums[p] = dict(keep=keep, send=send, slot=slot)
        slot += 1
    arrive(slot + 9)
    shards = [jnp.sum(sums[p]["z"].astype(F32), axis=0) for p in range(pieces)]
    mixer_shard = jnp.concatenate(shards[:MIXER_PARTS], axis=2)
    ffn_shard = jnp.concatenate(shards[MIXER_PARTS:], axis=3)
    here, there = ffn_shard[0], links.swap(ffn_shard[1], c=1)
    ffn_shard = jnp.concatenate(
        [jnp.where(core == 0, here, there), jnp.where(core == 0, there, here)], axis=2
    )
    gain_one_part = jnp.sum(grad_normed * unit_one, axis=0)
    grad_tokens = grad_hidden + norm_back(grad_normed, gain_one, inverse_one, unit_one)
    high = grad_tokens.astype(BF)
    rest = grad_tokens - high.astype(F32)
    middle = rest.astype(BF)
    low = (rest - middle.astype(F32)).astype(BF)
    grad_tokens = dot_nt(high, order) + (dot_nt(middle, order) + dot_nt(low, order))

    place = links.place(jnp.arange(links.dp))
    taps = jnp.concatenate(
        [
            item[:kernel].reshape(kernel, part // MIXER_TILE, 2, MIXER_TILE)
            for item in tap_grads
        ],
        axis=1,
    )
    taps = taps.transpose(0, 2, 1, 3).reshape(kernel, width)
    taps = jnp.where(rank == 0, taps, jnp.roll(taps, half, axis=1))
    gains = jnp.stack([gain_one_part, gain_two_part]).reshape(2, links.dp, block)
    gains = jnp.take(gains, place, axis=1).reshape(2, width)
    small = links.sum_all(jnp.concatenate([gains, taps], axis=0))

    return (
        result,
        grad_tokens,
        mixer_shard[:3],
        small[2:],
        mixer_shard[3].T,
        small[0],
        small[1],
        ffn_shard[0],
        ffn_shard[1],
        ffn_shard[2].T,
    )


def solution(mesh):
    rows = P(("dp", "tensor"), None)
    in_specs = (
        rows,
        P("dp"),
        P(None, "dp", "tensor"),
        P(),
        P("tensor", "dp"),
        P(),
        P(),
        P("dp", "tensor"),
        P("dp", "tensor"),
        P("tensor", "dp"),
        rows,
    )
    out_specs = (
        rows,
        rows,
        P(None, "dp", "tensor"),
        P(),
        P("tensor", "dp"),
        P(),
        P(),
        P("dp", "tensor"),
        P("dp", "tensor"),
        P("tensor", "dp"),
    )
    return jax.shard_map(body, mesh=mesh, in_specs=in_specs, out_specs=out_specs, check_vma=False)
```

time: 933 us -> 678 us (0.73)
  Pallas kernels: 0 us -> 275 us
  matrix products: 260 us -> 41.2 us
  other arithmetic: 207 us -> 42.7 us
  waiting for transfers between devices: 248 us -> 127 us
  local copies, waits for them, and re-layouts: 72.7 us -> 53 us
    pallas_call x0 -> x27, Pallas kernels: none -> 275 us  [the longest x5 148 us: ffn_piece(): pl.pallas_call(functools.partial(ffn_kernel, first, last, len(ties)), gri...]
    ppermute x93 -> x71, waiting for transfers between devices: 248 us -> 92.9 us  [swap(): return lax.ppermute(value, AXES, pairs)]
    concatenate x18 -> x3, other arithmetic: 141 us -> 2.61 us  [the longest x1 1.81 us: other_core_first(): return jnp.concatenate([values[:, half:], values[:, :half]], axis=1)]
    dot_general x15 -> x2, matrix products: 94.3 us -> 8.4 us  [dot_nn(): return jnp.dot(left, right, preferred_element_type=F32)]
    ppermute x93 -> x71, starting transfers between devices: 136 us -> 62.2 us  [swap(): return lax.ppermute(value, AXES, pairs)]
    dot_general x16 -> x4, matrix products: 102 us -> 32.8 us  [dot_nt(): lax.dot_general(left, right, (((1,), (1,)), ((), ())), preferred_element_...]
    all_to_all x0 -> x14, starting transfers between devices: none -> 65.9 us  [turn_z(): lax.all_to_all(value, 'dp', 0, 0, axis_index_groups=groups, tiled=True)]
    dot_general x13 -> x0, matrix products: 64.4 us -> none  [dot_tn(): lax.dot_general(left, right, (((0,), (0,)), ((), ())), preferred_element_...]
  transfers between devices with their start and end apart: 93 -> 85, of which waited for: 34 -> 27; matrix products, arithmetic and copies ran while one was open for 40% -> 18% of each run, Pallas kernels for 0% -> 41%
where the time goes in v2:
time: 678 us; the launch traced here: 669 us
  Pallas kernels  275 us (41%)
  starting transfers between devices  128 us (19%)
  waiting for transfers between devices  127 us (19%)
  local copies, waits for them, and re-layouts  53 us (8%)
  other arithmetic  42.7 us (6%)
  matrix products  41.2 us (6%)
    pallas_call x5, Pallas kernels, ffn_piece(): pl.pallas_call(functools.partial(ffn_kernel, first, last, len(ties)), gri...  148 us
    ppermute x71, waiting for transfers between devices, swap(): return lax.ppermute(value, AXES, pairs)  92.9 us
    all_to_all x14, starting transfers between devices, turn_z(): lax.all_to_all(value, 'dp', 0, 0, axis_index_groups=groups, tiled=True)  65.9 us
    ppermute x71, starting transfers between devices, swap(): return lax.ppermute(value, AXES, pairs)  62.2 us
    pallas_call x18, Pallas kernels, small_call(): pl.pallas_call(kernel, grid=(columns // 128,), in_specs=[spec(item.shape)...  46.7 us
    pallas_call x2, Pallas kernels, mixer_back(): pl.pallas_call(functools.partial(mixer_back_kernel, first, len(ties), min...  45.1 us
    pallas_call x2, Pallas kernels, mixer_part(): pl.pallas_call(functools.partial(mixer_kernel, first, last, len(ties), mi...  35.4 us
    all_to_all x14, waiting for transfers between devices, turn_z(): lax.all_to_all(value, 'dp', 0, 0, axis_index_groups=groups, tiled=True)  34 us
  transfers between devices with their start and end apart: 85, of which 27 were waited for; matrix products, arithmetic and copies ran while one was open for 18% of the time, Pallas kernels for 41%

profile of v2, /device:TPU:0, one launch (start us, length us, event | category | flops | bytes accessed | tf_op | source)
XLA Modules:
  0.0 668.7 jit_solution(15720459811673026160)
XLA Ops:
  4.3 6.3 all-to-all-start.1
  14.1 11.1 %all-to-all-done.1.mine.refs_7_ = bf16[4,4,64,256]{3,2,1,0:T(8,128)(2,1)} async-done(((bf16[4,4,64,256]{3,2,1,0:T(8,128)(2,1)}), bf16[4,4,64,256]{3,2,1,0:T(8,128)(2,1)}, u32[]{:S(2)}, u32[]{:S(2)}) %all-to-all-start.1) | async-done | bytes 524320 | tf_op jit(solution)/shard_map/all_to_all | solution.py:51
  54.1 5.3 copy.31
  74.3 6.1 collective-permute-done.1.from_x.refs_13_
  105.9 16.1 %shard_map.188 = (f32[3,1024,512]{2,1,0:T(8,128)}, f32[1024,1024]{1,0:T(8,128)}) custom-call(s32[1]{0:T(128)} %dynamic_slice.11.refs_0_, bf16[1024,1024]{1,0:T(8,128)(2,1)} %fusion.refs_1_, bf16[1024,1024]{1,0:T(8,128)(2,1)} %convert_bitcast_fusion.refs_2_, f32[2,3,256]{2,1,0:T(4,128)} %get-tuple-element.202.refs_3_.refs_4_, ...), custom_call_target="tpu_custom_call" | custom-call | flops 17179869184 | bytes 18874368 | tf_op jit(solution)/shard_map/pallas_call | solution.py:413
  125.5 19.3 %shard_map.189 = (f32[3,1024,512]{2,1,0:T(8,128)}, f32[1024,1024]{1,0:T(8,128)}, bf16[1024,1024]{1,0:T(8,128)(2,1)}, bf16[1024,1024]{1,0:T(8,128)(2,1)}) custom-call(s32[1]{0:T(128)} %dynamic_slice.11.refs_0_, bf16[1024,1024]{1,0:T(8,128)(2,1)} %fusion.refs_1_, bf16[1024,1024]{1,0:T(8,128)(2,1)} %convert_bitcast_fusion.refs_2_, ...), custom_call_target="tpu_custom_call", output_to_operand_aliasing={{1}: (7, {})} | custom-call | flops 17179869184 | bytes 18874368 | tf_op jit(solution)/shard_map/pallas_call | solution.py:413
  155.6 14.7 %all-to-all-done.6.refs_13_.refs_4_ = bf16[4,2,3,64,256]{4,3,2,1,0:T(8,128)(2,1)S(1)} async-done(((bf16[4,2,3,64,256]{4,3,2,1,0:T(8,128)(2,1)}), bf16[4,2,3,64,256]{4,3,2,1,0:T(8,128)(2,1)S(1)}, u32[]{:S(2)}, u32[]{:S(2)}) %all-to-all-start.6) | async-done | bytes 786464 | tf_op jit(solution)/shard_map/all_to_all | solution.py:51
  179.3 28.4 %shard_map.190 = (bf16[2,2,2,3,64,256]{5,4,3,2,1,0:T(8,128)(2,1)}, bf16[2,2,2,3,64,256]{5,4,3,2,1,0:T(8,128)(2,1)}, bf16[2,2,3,64,256]{4,3,2,1,0:T(8,128)(2,1)},...) custom-call(bf16[1024,1024]{1,0:T(8,128)(2,1)} %get-tuple-element.96, ...), custom_call_target="tpu_custom_call" | custom-call | flops 77309411328 | bytes 48234496 | tf_op jit(solution)/shard_map/pallas_call | solution.py:285
  215.5 12.9 %collective-permute-done.33.refs_18_.got_x = bf16[2,2,2,3,64,256]{5,4,3,2,1,0:T(8,128)(2,1)S(1)} collective-permute-done((bf16[2,2,2,3,64,256]{5,4,3,2,1,0:T(8,128)(2,1)}, bf16[2,2,2,3,64,256]{5,4,3,2,1,0:T(8,128)(2,1)S(1)}, u32[]{:S(2)}, u32[]{:S(2)}) %collective-permute-start.33) | collective-permute-done | bytes 786464 | tf_op jit(solution)/shard_map/ppermute | solution.py:47
  234.7 5.1 all-to-all-start.4
  239.8 5.6 collective-permute-done.24.refs_15_.refs_6_
  249.3 5.4 collective-permute-done.29.refs_7_.refs_13_
  256.7 5.4 collective-permute-done.35.refs_17_.side_x
  263.0 31.7 %shard_map.191 = (bf16[2,2,2,3,64,256]{5,4,3,2,1,0:T(8,128)(2,1)}, bf16[2,2,2,3,64,256]{5,4,3,2,1,0:T(8,128)(2,1)}, bf16[2,2,3,64,256]{4,3,2,1,0:T(8,128)(2,1)},...) custom-call(bf16[1024,1024]{1,0:T(8,128)(2,1)} %get-tuple-element.96, ...), custom_call_target="tpu_custom_call" | custom-call | flops 77309411328 | bytes 48234496 | tf_op jit(solution)/shard_map/pallas_call | solution.py:285
  300.6 5.0 all-to-all-start.7
  306.4 31.7 %shard_map.192 = (bf16[2,2,2,3,64,256]{5,4,3,2,1,0:T(8,128)(2,1)}, bf16[2,2,2,3,64,256]{5,4,3,2,1,0:T(8,128)(2,1)}, bf16[2,2,3,64,256]{4,3,2,1,0:T(8,128)(2,1)},...) custom-call(bf16[1024,1024]{1,0:T(8,128)(2,1)} %get-tuple-element.96, ...), custom_call_target="tpu_custom_call" | custom-call | flops 77309411328 | bytes 48234496 | tf_op jit(solution)/shard_map/pallas_call | solution.py:285
  348.5 15.8 %collective-permute-done.39.refs_16_.side_x = bf16[2,2,3,64,256]{4,3,2,1,0:T(8,128)(2,1)S(1)} collective-permute-done((bf16[2,2,3,64,256]{4,3,2,1,0:T(8,128)(2,1)}, bf16[2,2,3,64,256]{4,3,2,1,0:T(8,128)(2,1)S(1)}, u32[]{:S(2)}, u32[]{:S(2)}) %collective-permute-start.39) | collective-permute-done | bytes 393248 | tf_op jit(solution)/shard_map/ppermute | solution.py:47
  377.3 5.3 all-to-all-start.8
  383.8 31.7 %shard_map.194 = (bf16[2,2,2,3,64,256]{5,4,3,2,1,0:T(8,128)(2,1)}, bf16[2,2,2,3,64,256]{5,4,3,2,1,0:T(8,128)(2,1)}, bf16[2,2,3,64,256]{4,3,2,1,0:T(8,128)(2,1)},...) custom-call(bf16[1024,1024]{1,0:T(8,128)(2,1)} %get-tuple-element.96, ...), custom_call_target="tpu_custom_call" | custom-call | flops 77309411328 | bytes 48234496 | tf_op jit(solution)/shard_map/pallas_call | solution.py:285
  421.1 5.1 all-to-all-start.9
  426.2 6.9 %collective-permute-done.47.refs_10_.got_x = bf16[2,2,2,3,64,256]{5,4,3,2,1,0:T(8,128)(2,1)S(1)} collective-permute-done((bf16[2,2,2,3,64,256]{5,4,3,2,1,0:T(8,128)(2,1)}, bf16[2,2,2,3,64,256]{5,4,3,2,1,0:T(8,128)(2,1)S(1)}, u32[]{:S(2)}, u32[]{:S(2)}) %collective-permute-start.47) | collective-permute-done | bytes 786464 | tf_op jit(solution)/shard_map/ppermute | solution.py:47
  449.4 6.1 all-to-all-start.12
  456.3 24.1 %shard_map.197 = (bf16[2,2,2,3,64,128]{5,4,3,2,1,0:T(8,128)(2,1)}, bf16[2,2,2,3,64,128]{5,4,3,2,1,0:T(8,128)(2,1)}, bf16[2,2,3,64,128]{4,3,2,1,0:T(8,128)(2,1)},...) custom-call(bf16[1024,1024]{1,0:T(8,128)(2,1)} %get-tuple-element.96, ...), custom_call_target="tpu_custom_call" | custom-call | flops 38654705664 | bytes 45088768 | tf_op jit(solution)/shard_map/pallas_call | solution.py:285
  481.7 6.7 %collective-permute-done.51.refs_11_.got_x = bf16[2,2,2,3,64,128]{5,4,3,2,1,0:T(8,128)(2,1)S(1)} collective-permute-done((bf16[2,2,2,3,64,128]{5,4,3,2,1,0:T(8,128)(2,1)}, bf16[2,2,2,3,64,128]{5,4,3,2,1,0:T(8,128)(2,1)S(1)}, u32[]{:S(2)}, u32[]{:S(2)}) %collective-permute-start.51) | collective-permute-done | bytes 393248 | tf_op jit(solution)/shard_map/ppermute | solution.py:47
  501.6 5.3 all-to-all-start.13
  529.6 21.9 %shard_map.200 = (bf16[4,4,4,64,256]{4,3,2,1,0:T(8,128)(2,1)}, bf16[4,4,4,64,256]{4,3,2,1,0:T(8,128)(2,1)}, f32[8,512]{1,0:T(8,128)}, f32[1024,1024]{1,0:T(8,128)}) custom-call(s32[1]{0:T(128)} %dynamic_slice.11.refs_0_, bf16[1024,1024]{1,0:T(8,128)(2,1)} %fusion.refs_1_, bf16[1024,1024]{1,0:T(8,128)(2,1)} %get-tuple-element.181.refs_2_, ...), custom_call_target="tpu_custom_call" | custom-call | flops 34359738368 | bytes 23068672 | tf_op jit(solution)/shard_map/pallas_call | solution.py:519
  551.5 23.3 %shard_map.203 = (bf16[4,4,4,64,256]{4,3,2,1,0:T(8,128)(2,1)}, bf16[4,4,4,64,256]{4,3,2,1,0:T(8,128)(2,1)}, f32[8,512]{1,0:T(8,128)}, f32[1024,1024]{1,0:T(8,128)}) custom-call(s32[1]{0:T(128)} %dynamic_slice.11.refs_0_, bf16[1024,1024]{1,0:T(8,128)(2,1)} %fusion.refs_1_, ...), custom_call_target="tpu_custom_call", output_to_operand_aliasing={{3}: (7, {})} | custom-call | flops 34359738368 | bytes 23068672 | tf_op jit(solution)/shard_map/pallas_call | solution.py:519
  583.4 7.0 %fusion.4 = f32[1024,1024]{1,0:T(8,128)} fusion(f32[1024,1024]{1,0:T(8,128)} %get-tuple-element.182, f32[1024,1024]{1,0:T(8,128)} %get-tuple-element.150, f32[1024,1024]{0,1:T(8,128)} %copy.31, f32[1024]{0:T(1024)S(1)} %broadcast_multiply_fusion, f32[1024]{0:T(1024)S(1)} %copy-done.51, f32[1024]{0:T(1024)S(1)} %copy-done.55), kind=kLoop, calls=%fused_computation.11 | loop fusion | flops 6291456 | bytes 16789504 | tf_op jit(solution)/shard_map/add | solution.py:725
  598.0 7.9 %fusion.6 = f32[1024,1024]{1,0:T(8,128)} fusion(f32[1024,1024]{1,0:T(8,128)} %fusion.4, s32[1024]{0:T(1024)S(1)} %copy-done.60), kind=kOutput, calls=%fused_computation.25 | convolution fusion | flops 2155872256 | bytes 8392704 | tf_op jit(solution)/shard_map/dot_general | solution.py:33
  616.5 7.9 %fusion.7 = f32[1024,1024]{1,0:T(8,128)} fusion(f32[1024,1024]{1,0:T(8,128)} %fusion.4, s32[1024]{0:T(1024)S(1)} %copy-done.60), kind=kOutput, calls=%fused_computation.26 | convolution fusion | flops 2152726528 | bytes 8392704 | tf_op jit(solution)/shard_map/dot_general | solution.py:33
  637.0 9.1 %add_add_fusion = f32[1024,1024]{1,0:T(8,128)} fusion(f32[1024,1024]{1,0:T(8,128)} %fusion.7, f32[1024,1024]{1,0:T(8,128)} %fusion.6, s32[1024]{0:T(1024)S(1)} %copy-done.60, f32[1024,1024]{1,0:T(8,128)} %fusion.4), kind=kOutput, calls=%fused_computation.14 | convolution fusion | flops 2151677952 | bytes 16781312 | tf_op jit(solution)/shard_map/dot_general | solution.py:33
  655.6 7.9 %fusion.24 = bf16[1024,1024]{1,0:T(8,128)(2,1)} fusion(s32[1024]{0:T(1024)S(1)} %copy-done.60, f32[1024,1024]{1,0:T(8,128)} %get-tuple-element.95, f32[1024,1024]{1,0:T(8,128)} %get-tuple-element.129, bf16[1024,1024]{1,0:T(8,128)(2,1)} %collective-permute-done.43), kind=kOutput, calls=%fused_computation.47 | convolution fusion | flops 2153775104 | bytes 12587008 | tf_op jit(solution)/shard_map/dot_general | solution.py:33
  (416 shorter events, 264.7 us)
Async XLA Ops:
  12.8 54.3 %collective-permute-start.10 = (bf16[3,64,1152]{2,1,0:T(8,128)(2,1)}, bf16[3,64,1152]{2,1,0:T(8,128)(2,1)S(1)}, u32[]{:S(2)}, u32[]{:S(2)}) collective-permute-start(bf16[3,64,1152]{2,1,0:T(8,128)(2,1)} %get-tuple-element.194), channel_id=1, source_target_pairs={{0,2},{1,3},{2,0},{3,1},{4,6},{5,7},{6,4},{7,5},{8,10},{9,11},{10,... | collective-permute-start | bytes 1327112 | tf_op jit(solution)/shard_map/ppermute | solution.py:47
  27.0 39.0 %all-to-all-start = ((bf16[4,4,64,256]{3,2,1,0:T(8,128)(2,1)}), bf16[4,4,64,256]{3,2,1,0:T(8,128)(2,1)S(1)}, u32[]{:S(2)}, u32[]{:S(2)}) async-start(bf16[4,4,64,256]{3,2,1,0:T(8,128)(2,1)} %broadcast_in_dim.40), calls=%async_computation | async-start | bytes 1048576 | tf_op jit(solution)/shard_map/all_to_all | solution.py:51
  39.5 115.2 %collective-permute-start.14 = (bf16[1024,1024]{1,0:T(8,128)(2,1)}, bf16[1024,1024]{1,0:T(8,128)(2,1)}, u32[]{:S(2)}, u32[]{:S(2)}) collective-permute-start(bf16[1024,1024]{1,0:T(8,128)(2,1)} %pad_maximum_fusion), channel_id=1, source_target_pairs={{0,2},{1,3},{2,0},{3,1},{4,6},{5,7},{6,4},{7,5},{8,10},{9,11},{10,... | collective-permute-start | bytes 6291464 | tf_op jit(solution)/shard_map/ppermute | solution.py:47
  62.1 43.8 %collective-permute-start.9 = (bf16[4,4,4,64,256]{4,3,2,1,0:T(8,128)(2,1)}, bf16[4,4,4,64,256]{4,3,2,1,0:T(8,128)(2,1)}, u32[]{:S(2)}, u32[]{:S(2)}) collective-permute-start(bf16[4,4,4,64,256]{4,3,2,1,0:T(8,128)(2,1)} %shard_map.187.refs_5_), channel_id=1, source_target_pairs={{0,2},{1,3},{2,0},{3,1},{4,6},{5,7},{6,4},{7,5},{8,10},{9,11},{10,... | collective-permute-start | bytes 6291464 | tf_op jit(solution)/shard_map/ppermute | solution.py:47
  68.9 28.8 %all-to-all-start.2 = ((bf16[4,2,3,64,256]{4,3,2,1,0:T(8,128)(2,1)}), bf16[4,2,3,64,256]{4,3,2,1,0:T(8,128)(2,1)S(1)}, u32[]{:S(2)}, u32[]{:S(2)}) async-start(bf16[4,2,3,64,256]{4,3,2,1,0:T(8,128)(2,1)} %broadcast_in_dim.42), calls=%async_computation.2 | async-start | bytes 1572864 | tf_op jit(solution)/shard_map/all_to_all | solution.py:51
  93.1 31.5 %collective-permute-start.4 = (bf16[4,4,4,64,256]{4,3,2,1,0:T(8,128)(2,1)}, bf16[4,4,4,64,256]{4,3,2,1,0:T(8,128)(2,1)}, u32[]{:S(2)}, u32[]{:S(2)}) collective-permute-start(bf16[4,4,4,64,256]{4,3,2,1,0:T(8,128)(2,1)} %shard_map.186.refs_5_), channel_id=1, source_target_pairs={{0,2},{1,3},{2,0},{3,1},{4,6},{5,7},{6,4},{7,5},{8,10},{9,11},{10,... | collective-permute-start | bytes 6291464 | tf_op jit(solution)/shard_map/ppermute | solution.py:47
  144.8 34.5 %collective-permute-start.13 = (bf16[1024,1024]{1,0:T(8,128)(2,1)}, bf16[1024,1024]{1,0:T(8,128)(2,1)}, u32[]{:S(2)}, u32[]{:S(2)}) collective-permute-start(bf16[1024,1024]{1,0:T(8,128)(2,1)} %get-tuple-element.97), channel_id=1, source_target_pairs={{0,2},{1,3},{2,0},{3,1},{4,6},{5,7},{6,4},{7,5},{8,10},{9,11},{10,... | collective-permute-start | bytes 6291464 | tf_op jit(solution)/shard_map/ppermute | solution.py:47
  171.4 62.5 %all-to-all-start.5 = ((bf16[4,2,3,64,256]{4,3,2,1,0:T(8,128)(2,1)}), bf16[4,2,3,64,256]{4,3,2,1,0:T(8,128)(2,1)}, u32[]{:S(2)}, u32[]{:S(2)}) async-start(bf16[4,2,3,64,256]{4,3,2,1,0:T(8,128)(2,1)} %broadcast_in_dim.45), calls=%async_computation.5 | async-start | bytes 1572864 | tf_op jit(solution)/shard_map/all_to_all | solution.py:51
  209.5 35.9 %collective-permute-start.24 = (bf16[4,2,3,64,256]{4,3,2,1,0:T(8,128)(2,1)}, bf16[4,2,3,64,256]{4,3,2,1,0:T(8,128)(2,1)}, u32[]{:S(2)}, u32[]{:S(2)}) collective-permute-start(bf16[4,2,3,64,256]{4,3,2,1,0:T(8,128)(2,1)} %copy-done.30), channel_id=1, source_target_pairs={{0,4},{1,5},{2,6},{3,7},{4,0},{5,1},{6,2},{7,3},{8,12},{9,13},{10,... | collective-permute-start | bytes 2359304 | tf_op jit(solution)/shard_map/ppermute | solution.py:47
  210.7 36.6 %collective-permute-start.23 = (bf16[4,2,3,64,256]{4,3,2,1,0:T(8,128)(2,1)}, bf16[4,2,3,64,256]{4,3,2,1,0:T(8,128)(2,1)}, u32[]{:S(2)}, u32[]{:S(2)}) collective-permute-start(bf16[4,2,3,64,256]{4,3,2,1,0:T(8,128)(2,1)} %copy-done.30), channel_id=1, source_target_pairs={{0,1},{1,0},{2,3},{3,2},{4,5},{5,4},{6,7},{7,6},{8,9},{9,8},{10,11... | collective-permute-start | bytes 2359304 | tf_op jit(solution)/shard_map/ppermute | solution.py:47
  213.6 41.2 %collective-permute-start.29 = (bf16[2,2,3,64,256]{4,3,2,1,0:T(8,128)(2,1)}, bf16[2,2,3,64,256]{4,3,2,1,0:T(8,128)(2,1)}, u32[]{:S(2)}, u32[]{:S(2)}) collective-permute-start(bf16[2,2,3,64,256]{4,3,2,1,0:T(8,128)(2,1)} %slice.198), channel_id=1, source_target_pairs={{0,1},{1,0},{2,3},{3,2},{4,5},{5,4},{6,7},{7,6},{8,9},{9,8},{10,11... | collective-permute-start | bytes 1179656 | tf_op jit(solution)/shard_map/ppermute | solution.py:47
  232.7 29.4 %collective-permute-start.35 = (bf16[2,2,3,64,256]{4,3,2,1,0:T(8,128)(2,1)}, bf16[2,2,3,64,256]{4,3,2,1,0:T(8,128)(2,1)S(1)}, u32[]{:S(2)}, u32[]{:S(2)}) collective-permute-start(bf16[2,2,3,64,256]{4,3,2,1,0:T(8,128)(2,1)} %get-tuple-element.114), channel_id=1, source_target_pairs={{0,4},{1,5},{2,6},{3,7},{4,0},{5,1},{6,2},{7,3},{8,12},{9,13},{10,... | collective-permute-start | bytes 1179656 | tf_op jit(solution)/shard_map/ppermute | solution.py:47
  234.7 65.9 %all-to-all-start.4 = ((bf16[4,2,3,64,128]{4,3,2,1,0:T(8,128)(2,1)}), bf16[4,2,3,64,128]{4,3,2,1,0:T(8,128)(2,1)S(1)}, u32[]{:S(2)}, u32[]{:S(2)}) async-start(bf16[4,2,3,64,128]{4,3,2,1,0:T(8,128)(2,1)} %broadcast_in_dim.44), calls=%async_computation.4 | async-start | bytes 786432 | tf_op jit(solution)/shard_map/all_to_all | solution.py:51
  245.4 53.1 %collective-permute-start.19 = (bf16[4,2,3,64,256]{4,3,2,1,0:T(8,128)(2,1)}, bf16[4,2,3,64,256]{4,3,2,1,0:T(8,128)(2,1)S(1)}, u32[]{:S(2)}, u32[]{:S(2)}) collective-permute-start(bf16[4,2,3,64,256]{4,3,2,1,0:T(8,128)(2,1)} %all-to-all-done.5.refs_17_.refs_4_), channel_id=1, source_target_pairs={{0,1},{1,0},{2,3},{3,2},{4,5},{5,4},{6,7},{7,6},{8,9},{9,8},{10,11... | collective-permute-start | bytes 2359304 | tf_op jit(solution)/shard_map/ppermute | solution.py:47
  247.3 58.3 %collective-permute-start.20 = (bf16[4,2,3,64,256]{4,3,2,1,0:T(8,128)(2,1)}, bf16[4,2,3,64,256]{4,3,2,1,0:T(8,128)(2,1)}, u32[]{:S(2)}, u32[]{:S(2)}) collective-permute-start(bf16[4,2,3,64,256]{4,3,2,1,0:T(8,128)(2,1)} %all-to-all-done.5.refs_17_.refs_4_), channel_id=1, source_target_pairs={{0,4},{1,5},{2,6},{3,7},{4,0},{5,1},{6,2},{7,3},{8,12},{9,13},{10,... | collective-permute-start | bytes 2359304 | tf_op jit(solution)/shard_map/ppermute | solution.py:47
  254.7 50.9 %collective-permute-start.25 = (bf16[2,2,3,64,256]{4,3,2,1,0:T(8,128)(2,1)S(1)}, bf16[2,2,3,64,256]{4,3,2,1,0:T(8,128)(2,1)S(1)}, u32[]{:S(2)}, u32[]{:S(2)}) collective-permute-start(bf16[2,2,3,64,256]{4,3,2,1,0:T(8,128)(2,1)S(1)} %slice.196), channel_id=1, source_target_pairs={{0,1},{1,0},{2,3},{3,2},{4,5},{5,4},{6,7},{7,6},{8,9},{9,8},{10,11... | collective-permute-start | bytes 1179656 | tf_op jit(solution)/shard_map/ppermute | solution.py:47
  255.6 50.0 %collective-permute-start.26 = (bf16[2,2,3,64,256]{4,3,2,1,0:T(8,128)(2,1)S(1)}, bf16[2,2,3,64,256]{4,3,2,1,0:T(8,128)(2,1)}, u32[]{:S(2)}, u32[]{:S(2)}) collective-permute-start(bf16[2,2,3,64,256]{4,3,2,1,0:T(8,128)(2,1)S(1)} %slice.197), channel_id=1, source_target_pairs={{0,4},{1,5},{2,6},{3,7},{4,0},{5,1},{6,2},{7,3},{8,12},{9,13},{10,... | collective-permute-start | bytes 1179656 | tf_op jit(solution)/shard_map/ppermute | solution.py:47
  262.1 32.6 %collective-permute-start.36 = (bf16[2,2,3,64,256]{4,3,2,1,0:T(8,128)(2,1)}, bf16[2,2,3,64,256]{4,3,2,1,0:T(8,128)(2,1)S(1)}, u32[]{:S(2)}, u32[]{:S(2)}) collective-permute-start(bf16[2,2,3,64,256]{4,3,2,1,0:T(8,128)(2,1)} %get-tuple-element.115), channel_id=1, source_target_pairs={{0,1},{1,0},{2,3},{3,2},{4,5},{5,4},{6,7},{7,6},{8,9},{9,8},{10,11... | collective-permute-start | bytes 1179656 | tf_op jit(solution)/shard_map/ppermute | solution.py:47
  294.7 45.3 %collective-permute-start.37 = (bf16[2,2,2,3,64,256]{5,4,3,2,1,0:T(8,128)(2,1)}, bf16[2,2,2,3,64,256]{5,4,3,2,1,0:T(8,128)(2,1)S(1)}, u32[]{:S(2)}, u32[]{:S(2)}) collective-permute-start(bf16[2,2,2,3,64,256]{5,4,3,2,1,0:T(8,128)(2,1)} %get-tuple-element.116), channel_id=1, source_target_pairs={{0,4},{1,5},{2,6},{3,7},{4,0},{5,1},{6,2},{7,3},{8,12},{9,13},{10,... | collective-permute-start | bytes 2359304 | tf_op jit(solution)/shard_map/ppermute | solution.py:47
  299.4 40.6 %collective-permute-start.38 = (bf16[2,2,2,3,64,256]{5,4,3,2,1,0:T(8,128)(2,1)}, bf16[2,2,2,3,64,256]{5,4,3,2,1,0:T(8,128)(2,1)}, u32[]{:S(2)}, u32[]{:S(2)}) collective-permute-start(bf16[2,2,2,3,64,256]{5,4,3,2,1,0:T(8,128)(2,1)} %get-tuple-element.117), channel_id=1, source_target_pairs={{0,1},{1,0},{2,3},{3,2},{4,5},{5,4},{6,7},{7,6},{8,9},{9,8},{10,11... | collective-permute-start | bytes 2359304 | tf_op jit(solution)/shard_map/ppermute | solution.py:47
  300.6 76.7 %all-to-all-start.7 = ((bf16[4,2,3,64,256]{4,3,2,1,0:T(8,128)(2,1)}), bf16[4,2,3,64,256]{4,3,2,1,0:T(8,128)(2,1)S(1)}, u32[]{:S(2)}, u32[]{:S(2)}) async-start(bf16[4,2,3,64,256]{4,3,2,1,0:T(8,128)(2,1)} %shard_map.195), calls=%async_computation.7 | async-start | bytes 1572864 | tf_op jit(solution)/shard_map/all_to_all | solution.py:51
  338.0 31.1 %collective-permute-start.41 = (bf16[2,2,2,3,64,256]{5,4,3,2,1,0:T(8,128)(2,1)}, bf16[2,2,2,3,64,256]{5,4,3,2,1,0:T(8,128)(2,1)S(1)}, u32[]{:S(2)}, u32[]{:S(2)}) collective-permute-start(bf16[2,2,2,3,64,256]{5,4,3,2,1,0:T(8,128)(2,1)} %get-tuple-element.127), channel_id=1, source_target_pairs={{0,4},{1,5},{2,6},{3,7},{4,0},{5,1},{6,2},{7,3},{8,12},{9,13},{10,... | collective-permute-start | bytes 2359304 | tf_op jit(solution)/shard_map/ppermute | solution.py:47
  339.1 33.8 %collective-permute-start.42 = (bf16[2,2,2,3,64,256]{5,4,3,2,1,0:T(8,128)(2,1)}, bf16[2,2,2,3,64,256]{5,4,3,2,1,0:T(8,128)(2,1)S(1)}, u32[]{:S(2)}, u32[]{:S(2)}) collective-permute-start(bf16[2,2,2,3,64,256]{5,4,3,2,1,0:T(8,128)(2,1)} %get-tuple-element.128), channel_id=1, source_target_pairs={{0,1},{1,0},{2,3},{3,2},{4,5},{5,4},{6,7},{7,6},{8,9},{9,8},{10,11... | collective-permute-start | bytes 2359304 | tf_op jit(solution)/shard_map/ppermute | solution.py:47
  345.5 37.1 %collective-permute-start.15 = (bf16[4,2,3,64,128]{4,3,2,1,0:T(8,128)(2,1)}, bf16[4,2,3,64,128]{4,3,2,1,0:T(8,128)(2,1)}, u32[]{:S(2)}, u32[]{:S(2)}) collective-permute-start(bf16[4,2,3,64,128]{4,3,2,1,0:T(8,128)(2,1)} %copy-done.36), channel_id=1, source_target_pairs={{0,1},{1,0},{2,3},{3,2},{4,5},{5,4},{6,7},{7,6},{8,9},{9,8},{10,11... | collective-permute-start | bytes 1179656 | tf_op jit(solution)/shard_map/ppermute | solution.py:47
  376.3 41.3 %collective-permute-start.45 = (bf16[2,2,3,64,256]{4,3,2,1,0:T(8,128)(2,1)}, bf16[2,2,3,64,256]{4,3,2,1,0:T(8,128)(2,1)}, u32[]{:S(2)}, u32[]{:S(2)}) collective-permute-start(bf16[2,2,3,64,256]{4,3,2,1,0:T(8,128)(2,1)} %get-tuple-element.138), channel_id=1, source_target_pairs={{0,4},{1,5},{2,6},{3,7},{4,0},{5,1},{6,2},{7,3},{8,12},{9,13},{10,... | collective-permute-start | bytes 1179656 | tf_op jit(solution)/shard_map/ppermute | solution.py:47
  377.3 43.8 %all-to-all-start.8 = ((bf16[4,2,3,64,256]{4,3,2,1,0:T(8,128)(2,1)}), bf16[4,2,3,64,256]{4,3,2,1,0:T(8,128)(2,1)S(1)}, u32[]{:S(2)}, u32[]{:S(2)}) async-start(bf16[4,2,3,64,256]{4,3,2,1,0:T(8,128)(2,1)} %shard_map.198), calls=%async_computation.8 | async-start | bytes 1572864 | tf_op jit(solution)/shard_map/all_to_all | solution.py:51
  382.7 34.9 %collective-permute-start.46 = (bf16[2,2,3,64,256]{4,3,2,1,0:T(8,128)(2,1)}, bf16[2,2,3,64,256]{4,3,2,1,0:T(8,128)(2,1)S(1)}, u32[]{:S(2)}, u32[]{:S(2)}) collective-permute-start(bf16[2,2,3,64,256]{4,3,2,1,0:T(8,128)(2,1)} %get-tuple-element.139), channel_id=1, source_target_pairs={{0,1},{1,0},{2,3},{3,2},{4,5},{5,4},{6,7},{7,6},{8,9},{9,8},{10,11... | collective-permute-start | bytes 1179656 | tf_op jit(solution)/shard_map/ppermute | solution.py:47
  449.4 52.2 %all-to-all-start.12 = ((bf16[4,2,3,64,256]{4,3,2,1,0:T(8,128)(2,1)}), bf16[4,2,3,64,256]{4,3,2,1,0:T(8,128)(2,1)}, u32[]{:S(2)}, u32[]{:S(2)}) async-start(bf16[4,2,3,64,256]{4,3,2,1,0:T(8,128)(2,1)} %shard_map.210), calls=%async_computation.12 | async-start | bytes 1572864 | tf_op jit(solution)/shard_map/all_to_all | solution.py:51
  494.3 30.2 %collective-permute-start.44 = (bf16[1024,1024]{1,0:T(8,128)(2,1)}, bf16[1024,1024]{1,0:T(8,128)(2,1)S(1)}, u32[]{:S(2)}, u32[]{:S(2)}) collective-permute-start(bf16[1024,1024]{1,0:T(8,128)(2,1)} %get-tuple-element.132), channel_id=1, source_target_pairs={{0,2},{1,3},{2,0},{3,1},{4,6},{5,7},{6,4},{7,5},{8,10},{9,11},{10,... | collective-permute-start | bytes 6291464 | tf_op jit(solution)/shard_map/ppermute | solution.py:47
  520.8 134.8 %collective-permute-start.43 = (bf16[1024,1024]{1,0:T(8,128)(2,1)}, bf16[1024,1024]{1,0:T(8,128)(2,1)}, u32[]{:S(2)}, u32[]{:S(2)}) collective-permute-start(bf16[1024,1024]{1,0:T(8,128)(2,1)} %get-tuple-element.130), channel_id=1, source_target_pairs={{0,2},{1,3},{2,0},{3,1},{4,6},{5,7},{6,4},{7,5},{8,10},{9,11},{10,... | collective-permute-start | bytes 6291464 | tf_op jit(solution)/shard_map/ppermute | solution.py:47
  551.5 40.1 %collective-permute-start.58 = (bf16[4,4,4,64,256]{4,3,2,1,0:T(8,128)(2,1)}, bf16[4,4,4,64,256]{4,3,2,1,0:T(8,128)(2,1)S(1)}, u32[]{:S(2)}, u32[]{:S(2)}) collective-permute-start(bf16[4,4,4,64,256]{4,3,2,1,0:T(8,128)(2,1)} %get-tuple-element.161), channel_id=1, source_target_pairs={{0,2},{1,3},{2,0},{3,1},{4,6},{5,7},{6,4},{7,5},{8,10},{9,11},{10,... | collective-permute-start | bytes 6291464 | tf_op jit(solution)/shard_map/ppermute | solution.py:47
  574.8 31.1 %collective-permute-start.53 = (bf16[4,4,4,64,256]{4,3,2,1,0:T(8,128)(2,1)}, bf16[4,4,4,64,256]{4,3,2,1,0:T(8,128)(2,1)}, u32[]{:S(2)}, u32[]{:S(2)}) collective-permute-start(bf16[4,4,4,64,256]{4,3,2,1,0:T(8,128)(2,1)} %get-tuple-element.152), channel_id=1, source_target_pairs={{0,2},{1,3},{2,0},{3,1},{4,6},{5,7},{6,4},{7,5},{8,10},{9,11},{10,... | collective-permute-start | bytes 6291464 | tf_op jit(solution)/shard_map/ppermute | solution.py:47
  (122 other events, 1478.4 us)

commit v3 on v2

--- a/solution.py
+++ b/solution.py
@@ -10,10 +10,8 @@
 SLOTS = 1024
 EPS = 1e-05
 AXES = ("dp", "tensor")
-SIZES = (256, 256, 256, 256, 128)
-MIXER_PARTS = 2
-MIXER_TILE = 128
 ROW_TILE = 256
+SIZES = (256, 256, 384, 256)
 COST = 4
 VMEM = 60 * 2**20
 BF = jnp.bfloat16
@@ -50,8 +48,8 @@
         groups = [[z * 4 + rest for z in range(self.zs)] for rest in range(4)]
         return lax.all_to_all(value, "dp", 0, 0, axis_index_groups=groups, tiled=True)
 
-    def gather_z(self, own):
-        return self.turn_z(jnp.broadcast_to(own[None], (self.zs, *own.shape)))
+    def spread(self, own):
+        return jnp.broadcast_to(own[None], (self.zs, *own.shape))
 
     def gather_sides(self, mine):
         return self.swap(mine, x=1), self.swap(mine, y=1)
@@ -60,10 +58,12 @@
         half = self.zs // 2
         return self.swap(from_x[:half], y=1), self.swap(from_y[half:], x=1)
 
-    def sum_all(self, value):
+    def sum_chip(self, value):
         value = value + self.swap(value, c=1)
+        return value + self.swap(value, y=1)
+
+    def sum_rest(self, value):
         value = value + self.swap(value, x=1)
-        value = value + self.swap(value, y=1)
         step = 1
         while step < self.zs:
             value = value + self.swap(value, z=step)
@@ -115,6 +115,22 @@
     )(*inputs)
 
 
+def gate(values):
+    def nothing(*refs):
+        del refs
+
+    count = len(values)
+    return pl.pallas_call(
+        nothing,
+        in_specs=[ANYWHERE] * count,
+        out_specs=[ANYWHERE] * count,
+        out_shape=[jax.ShapeDtypeStruct(item.shape, item.dtype) for item in values],
+        input_output_aliases={i: i for i in range(count)},
+        compiler_params=params(),
+        cost_estimate=cost(0, 1024),
+    )(*values)
+
+
 def join_kernel(mine, from_y, from_x, one, two, out):
     half = one.shape[0]
     out[0] = mine[...]
@@ -158,7 +174,10 @@
 
 def add_sides(rest_x, rest_y, got_x, got_y):
     return small_call(
-        sides_kernel, [rest_x, rest_y, got_x, got_y], [rest_x.shape] * 2, 8 * rest_x.size
+        sides_kernel,
+        [rest_x, rest_y, got_x, got_y],
+        [rest_x.shape] * 2,
+        8 * rest_x.size,
     )
 
 
@@ -315,9 +334,10 @@
                         ]
 
 
-def cell_specs(cells, tile):
+def cell_specs(cells, tile, skip=0):
     return [
-        pl.BlockSpec((*item.shape[:-1], tile), lambda j: (0, 0, 0, 0, j)) for item in cells
+        pl.BlockSpec((*item.shape[:-1], tile), lambda j: (0, 0, 0, 0, j + skip))
+        for item in cells
     ]
 
 
@@ -397,11 +417,10 @@
                 for_twin[at, :] = other_core_first(value_two)
 
 
-def mixer_part(lengths, normed, tokens, conv, gain, cells, before, last, ties):
+def mixer_part(lengths, normed, tokens, conv, gain, cells, before, last, ties, tile):
     rows, width = normed.shape
     _, zs, kinds, block, columns = cells[0].shape
     first = before is None
-    tile = MIXER_TILE
     whole = whole_spec((rows, width))
     inputs = [lengths, normed, tokens, conv, gain, *cells]
     inputs += ([] if first else [before]) + list(ties)
@@ -506,11 +525,12 @@
                 out[2 * x + 1, z, k] = part[:, tile:]
 
 
-def mixer_back(lengths, normed, grad_mix, project, conv, cells, before, ties):
+def mixer_back(lengths, normed, grad_mix, project, conv, cells, before, ties, tile, part, parts):
     rows, width = normed.shape
     _, zs, kinds, block, columns = cells[0].shape
+    columns = columns // parts
+    skip = part * (columns // tile)
     first = before is None
-    tile = MIXER_TILE
     whole = whole_spec((rows, width))
     inputs = [lengths, normed, grad_mix, project, conv, *cells]
     inputs += ([] if first else [before]) + list(ties)
@@ -520,9 +540,9 @@
         functools.partial(mixer_back_kernel, first, len(ties), min(rows, 256)),
         grid=(columns // tile,),
         in_specs=[pl.BlockSpec(memory_space=pltpu.SMEM), whole, whole]
-        + [pl.BlockSpec((3, rows, 2 * tile), lambda j: (0, 0, j))]
-        + [pl.BlockSpec((2, conv.shape[1], tile), lambda j: (0, 0, j))]
-        + cell_specs(cells, tile)
+        + [pl.BlockSpec((3, rows, 2 * tile), lambda j: (0, 0, j + skip))]
+        + [pl.BlockSpec((2, conv.shape[1], tile), lambda j: (0, 0, j + skip))]
+        + cell_specs(cells, tile, skip)
         + [whole] * (0 if first else 1)
         + [ANYWHERE] * len(ties),
         out_specs=[grads, grads, pl.BlockSpec((8, 2 * tile), lambda j: (0, j)), whole],
@@ -548,6 +568,112 @@
     )(*inputs)
 
 
+def reorder(source, target, flip, inward):
+    width = source.shape[1]
+    for case in range(4):
+
+        @pl.when(flip == case)
+        def _():
+            count = SHARDS[0]
+            block, zs = width // count, count // 4
+            for place in range(count):
+                core, x, z = place // (2 * zs), place // zs % 2, place % zs
+                absolute = z * 4 + (case ^ (x * 2 + core))
+                here = slice(place * block, (place + 1) * block)
+                there = slice(absolute * block, (absolute + 1) * block)
+                if inward:
+                    target[:, here] = source[:, there]
+                else:
+                    target[:, there] = source[:, here]
+
+
+def row_call(kernel, flip, inputs, outs, sums=0, ties=()):
+    rows, width = next(item.shape for item in inputs if item.shape[0] > 1)
+    height = min(ROW_TILE, rows)
+    tiled = pl.BlockSpec((height, width), lambda i: (i, 0))
+    scalar = pl.BlockSpec(memory_space=pltpu.SMEM)
+    specs = [
+        scalar if item.ndim == 1 else tiled if item.shape[0] > 1 else whole_spec((1, width))
+        for item in inputs
+    ]
+    count = len(inputs) + 1
+
+    def body(*refs):
+        kernel(*refs[:count], *refs[count + len(ties) :])
+
+    return pl.pallas_call(
+        body,
+        grid=(rows // height,),
+        in_specs=[scalar] + specs + [ANYWHERE] * len(ties),
+        out_specs=[tiled] * len(outs) + [whole_spec((8, width))] * sums,
+        out_shape=[jax.ShapeDtypeStruct((rows, width), dtype) for dtype in outs]
+        + [jax.ShapeDtypeStruct((8, width), F32)] * sums,
+        scratch_shapes=[pltpu.VMEM((height, width), F32)] * 2,
+        compiler_params=params(),
+        cost_estimate=cost(20 * rows * width, 12 * rows * width),
+    )(flip, *inputs, *ties)
+
+
+def enter_kernel(flip, lengths, tokens, cotangent, gain, low, normed, grad, for_twin, one, two):
+    one[...] = tokens[...].astype(F32)
+    reorder(one, two, flip[0], True)
+    value = two[...]
+    low[...] = value.astype(BF)
+    normed[...] = (norm_stats(value)[1] * gain[...]).astype(BF)
+    one[...] = cotangent[...].astype(F32)
+    reorder(one, two, flip[0], True)
+    height = value.shape[0]
+    first = pl.program_id(0) * height
+    position = first % SLOTS + lax.broadcasted_iota(jnp.int32, value.shape, 0)
+    value = jnp.where(position < lengths[first // SLOTS], two[...], 0.0).astype(BF)
+    grad[...] = value
+    for_twin[...] = other_core_first(value)
+
+
+def add_up(total, values):
+    part = jnp.sum(values.reshape(-1, 8, values.shape[1]), axis=0)
+
+    @pl.when(pl.program_id(0) == 0)
+    def _():
+        total[...] = part
+
+    @pl.when(pl.program_id(0) > 0)
+    def _():
+        total[...] += part
+
+
+def between_kernel(flip, mine, twin, hidden, grad_out, gain, mix, grad_hidden, total, one, two):
+    grad = mine[...] + twin[...].astype(F32)
+    inverse, unit = norm_stats(hidden[...])
+    value = grad_out[...].astype(F32) + norm_back(grad, gain[...], inverse, unit)
+    mix[...] = value.astype(BF)
+    grad_hidden[...] = value
+    add_up(total, grad * unit)
+
+
+def leave_kernel(flip, grad, tokens, grad_hidden, gain, out, total, one, two):
+    inverse, unit = norm_stats(tokens[...].astype(F32))
+    value = grad[...]
+    one[...] = grad_hidden[...] + norm_back(value, gain[...], inverse, unit)
+    reorder(one, out, flip[0], False)
+    add_up(total, value * unit)
+
+
+def result_kernel(flip, hidden, mine, twin, out, one, two):
+    one[...] = hidden[...] + mine[...] + twin[...].astype(F32)
+    reorder(one, two, flip[0], False)
+    out[...] = two[...].astype(BF)
+
+
+SHARDS = [16]
+
+
+def ffn_sizes(columns, rows):
+    if rows <= 1024 and columns == sum(SIZES):
+        return SIZES
+    return (128,) * (columns // 128)
+
+
 def norm_stats(values):
     inverse = lax.rsqrt(jnp.mean(values * values, axis=-1, keepdims=True) + EPS)
     return (inverse, values * inverse)
@@ -582,167 +708,172 @@
     core = lax.axis_index("dp") % 2
     mixer_own = jnp.concatenate([in_proj.astype(BF), out_proj.T.astype(BF)[None]], axis=0)
     ffn_own = jnp.stack([w_gate.astype(BF), w_up.astype(BF), w_down.T.astype(BF)])
-    part = half // MIXER_PARTS
-    mixer_parts = [mixer_own[:, :, p * part : (p + 1) * part] for p in range(MIXER_PARTS)]
+    tile = 256 if half % 512 == 0 and rows <= 1024 else 128
     shared = hidden_half // 2
     mine_of = lax.dynamic_slice_in_dim(ffn_own, core * shared, shared, 2)
     twin_of = lax.dynamic_slice_in_dim(ffn_own, (1 - core) * shared, shared, 2)
     ffn_both = jnp.stack([mine_of, links.swap(twin_of, c=1)])
-    starts = [sum(SIZES[:p]) for p in range(len(SIZES))]
-    own = mixer_parts + [
-        ffn_both[..., at : at + size] for at, size in zip(starts, SIZES)
-    ]
+    sizes = ffn_sizes(shared, rows)
+    starts = [sum(sizes[:p]) for p in range(len(sizes))]
+    own = [mixer_own] + [ffn_both[..., at : at + size] for at, size in zip(starts, sizes)]
+    own = [links.spread(item) for item in own]
     pieces = len(own)
-    mine, sides, corner, mixer_cells = {}, {}, {}, {}
+    last = pieces - 1
+    mine, sides, corner = {}, {}, {}
 
     def cells(p):
         from_x, from_y = sides[p]
         return [mine[p], from_y, from_x, *corner[p]]
 
-    def gather_stage(p, stage):
-        if stage == 0:
-            mine[p] = links.gather_z(own[p])
-            return [mine[p]]
-        if stage == 1:
+    sums = {}
+
+    def start(stage, p):
+        if stage == "z":
+            mine[p] = links.turn_z(own[p])
+            return mine, p
+        if stage == "sides":
             sides[p] = links.gather_sides(mine[p])
-            return list(sides[p])
-        if stage == 2:
+            return sides, p
+        if stage == "corner":
             corner[p] = links.gather_corner(*sides[p])
-            return list(corner[p])
-        joined = join(*cells(p))
-        mixer_cells[p] = [joined, links.swap(joined, c=1)]
-        return []
-
-    def gather_slot(p, stage):
-        return p if stage == 3 else p + stage - (3 if p < MIXER_PARTS else 2)
-
-    sums = {}
-
-    def sum_stage(p, stage):
+            return corner, p
         item = sums[p]
-        if stage == 1:
-            got = links.swap(item["send"], c=1)
-            item["parts"] = both_cores(item["keep"], got)
-            return [got]
-        send_x, send_y, rest_x, rest_y, mine_here = item["parts"]
-        if stage == 2:
-            item["got"] = links.swap(send_x, x=1), links.swap(send_y, y=1)
-            return list(item["got"])
-        if stage == 3:
-            next_x, next_y = add_sides(rest_x, rest_y, *item["got"])
+        if stage == "sum core":
+            item["got"] = links.swap(item["send"], c=1)
+            return item, "got"
+        if stage == "sum corner":
+            if "keep" in item:
+                item["parts"] = both_cores(item["keep"], item["got"])
+            send_x, send_y = item["parts"][:2]
+            item["corner"] = links.swap(send_x, x=1), links.swap(send_y, y=1)
+            return item, "corner"
+        rest_x, rest_y, here = item["parts"][2:]
+        if stage == "sum sides":
+            next_x, next_y = add_sides(rest_x, rest_y, *item["corner"])
             item["sides"] = links.swap(next_x, x=1), links.swap(next_y, y=1)
-            return list(item["sides"])
-        item["z"] = links.turn_z(add_own(mine_here, *item["got"], *item["sides"]))
-        return [item["z"]]
-
-    done = set()
-
-    def arrive(slot):
-        ties = []
-        for p in range(pieces):
-            for stage in range(4 if p < MIXER_PARTS else 3):
-                if (p, stage) not in done and gather_slot(p, stage) <= slot:
-                    done.add((p, stage))
-                    ties += gather_stage(p, stage)
-        for p in list(sums):
-            begin = 1 if p < MIXER_PARTS else 2
-            for stage in range(begin, 5):
-                due = sums[p]["slot"] + 2 + stage - begin
-                if (p, -stage) not in done and due <= slot:
-                    done.add((p, -stage))
-                    ties += sum_stage(p, stage)
-        return ties
+            return item, "sides"
+        item["z"] = links.turn_z(add_own(here, *item["corner"], *item["sides"]))
+        return item, "z"
+
+    def close(kept, places):
+        kept, tree = jax.tree.flatten([kept, [store[key] for store, key in places]])
+        kept, arrived = jax.tree.unflatten(tree, gate(kept))
+        for (store, key), value in zip(places, arrived):
+            store[key] = value
+        return kept
 
     blocks = links.absolute(jnp.arange(links.dp))
-    feature = jnp.repeat(blocks, block) * block + jnp.tile(jnp.arange(block), links.dp)
-    order = (jnp.arange(width)[:, None] == feature[None, :]).astype(BF)
-    tokens_f = dot_nn(tokens, order)
-    cot = dot_nn(cotangent, order)
-    gain_one = jnp.take(norm_gain.reshape(links.dp, block), blocks, axis=0).reshape(width)
-    gain_two = jnp.take(ffn_gain.reshape(links.dp, block), blocks, axis=0).reshape(width)
+    gain_one = jnp.take(norm_gain.reshape(links.dp, block), blocks, axis=0).reshape(1, width)
+    gain_two = jnp.take(ffn_gain.reshape(links.dp, block), blocks, axis=0).reshape(1, width)
     conv = jnp.where(rank == 0, conv_weight, jnp.roll(conv_weight, half, axis=1))
-
+    conv = conv.reshape(kernel, 2, half).transpose(1, 0, 2)
     count = rows // SLOTS
     own_lengths = lax.dynamic_slice_in_dim(lengths, rank * count, count)
-    position = jnp.tile(jnp.arange(SLOTS, dtype=jnp.int32), count)
-    alive = (position < jnp.repeat(own_lengths, SLOTS)).astype(F32)[:, None]
-    conv = conv.reshape(kernel, 2, half).transpose(1, 0, 2)
-
-    inverse_one, unit_one = norm_stats(tokens_f)
-    normed = (unit_one * gain_one).astype(BF)
-    grad_ffn = (cot * alive).astype(BF)
-    grad_ffn_twin = links.swap(other_core_first(grad_ffn), c=1)
-    tokens_low = tokens_f.astype(BF)
-
-    slot = 0
-    hidden, projects = None, []
-    for p in range(MIXER_PARTS):
-        ties = arrive(slot)
-        last = p == MIXER_PARTS - 1
-        project, hidden, *rest = mixer_part(
-            own_lengths, normed, tokens_low, conv[:, :, p * part : (p + 1) * part],
-            gain_two[None], mixer_cells[p], hidden, last, ties,
+    flip = (lax.axis_index("dp") % 4)[None]
+    SHARDS[0] = links.dp
+    tokens_low, normed, grad_ffn, for_twin_grad = row_call(
+        enter_kernel, flip, [own_lengths, tokens, cotangent, gain_one], [BF] * 4, ties=own[1:]
+    )
+
+    places = [start("z", 0)]
+    normed, for_twin_grad, own = close([normed, for_twin_grad, own], places)
+    grad_ffn_twin = links.swap(for_twin_grad, c=1)
+    places = [start("sides", 0), start("z", 1)]
+    own[2:3], mine[0] = close([own[2:3], mine[0]], places)
+    places = [start("corner", 0), start("z", 2)]
+    own[3:4], mine[1] = close([own[3:4], mine[1]], places)
+    joined = join(*cells(0))
+    mixer_cells = [joined, links.swap(joined, c=1)]
+
+    places = [start("sides", 1), start("sides", 2), start("z", 3)]
+    project, hidden, normed_two, for_twin = mixer_part(
+        own_lengths, normed, tokens_low, conv, gain_two, mixer_cells, None, True, [], tile
+    )
+    normed_two, for_twin, own[4:5] = close([normed_two, for_twin, own[4:5]], places)
+    start("corner", 1)
+    inputs = [normed_two, links.swap(for_twin, c=1), grad_ffn, grad_ffn_twin]
+
+    totals = None
+    for p in range(1, pieces):
+        places = []
+        for stage, q in (("corner", p + 1), ("sides", p + 2), ("z", p + 3)):
+            if q < pieces:
+                places.append(start(stage, q))
+        for stage, q in (("sum z", p - 4), ("sum sides", p - 3), ("sum corner", p - 2)):
+            if q > 0:
+                places.append(start(stage, q))
+        *parts, t0, t1, t2, t3 = ffn_piece(inputs, cells(p), totals, p == last, [])
+        parts, totals = close([parts, [t0, t1, t2, t3]], places)
+        sums[p] = dict(parts=parts)
+    grad_mix, grad_hidden, gain_two_part = row_call(
+        between_kernel,
+        flip,
+        [totals[1], links.swap(totals[3], c=1), hidden, grad_ffn, gain_two],
+        [BF, F32],
+        1,
+    )
+    places = [
+        start("sum z", last - 3),
+        start("sum sides", last - 2),
+        start("sum corner", last - 1),
+    ]
+    parts = 2 if half % 256 == 0 else 1
+    names = [f"mixer {p}" for p in range(parts)]
+    grad_normed, taps = None, []
+    for p, name in enumerate(names):
+        if p:
+            places = [start("sum core", names[0])]
+        if p == parts - 1:
+            later = [start("sum z", last - 2), start("sum sides", last - 1)]
+            later.append(start("sum corner", last))
+            places += later
+        keep, send, tap_grads, grad_normed = mixer_back(
+            own_lengths, normed, grad_mix, project, conv, mixer_cells, grad_normed, [],
+            tile, p, parts,
         )
-        projects.append(project)
-        slot += 1
-    normed_two, for_twin = rest
-    inputs = [normed_two, links.swap(for_twin, c=1), grad_ffn, grad_ffn_twin]
-
-    totals = None
-    for p in range(MIXER_PARTS, pieces):
-        ties = arrive(slot)
-        *parts, t0, t1, t2, t3 = ffn_piece(inputs, cells(p), totals, p == pieces - 1, ties)
-        totals = [t0, t1, t2, t3]
-        sums[p] = dict(parts=parts, slot=slot)
-        slot += 1
-    grad_normed_two = totals[1] + links.swap(totals[3], c=1).astype(F32)
-    ffn_out = totals[0] + links.swap(totals[2], c=1).astype(F32)
-    result = dot_nt((hidden + ffn_out).astype(BF), order).astype(BF)
-
-    inverse_two, unit_two = norm_stats(hidden)
-    grad_out = grad_ffn.astype(F32)
-    gain_two_part = jnp.sum(grad_normed_two * unit_two, axis=0)
-    grad_hidden = grad_out + norm_back(grad_normed_two, gain_two, inverse_two, unit_two)
-    grad_mix = grad_hidden.astype(BF)
-    grad_normed, tap_grads = None, [None] * MIXER_PARTS
-    for p in reversed(range(MIXER_PARTS)):
-        ties = arrive(slot)
-        keep, send, tap_grads[p], grad_normed = mixer_back(
-            own_lengths, normed, grad_mix, projects[p], conv[:, :, p * part : (p + 1) * part],
-            mixer_cells[p], grad_normed, ties,
+        keep, send, tap_grads, grad_normed, totals[0], totals[2] = close(
+            [keep, send, tap_grads, grad_normed, totals[0], totals[2]], places
         )
-        sums[p] = dict(keep=keep, send=send, slot=slot)
-        slot += 1
-    arrive(slot + 9)
-    shards = [jnp.sum(sums[p]["z"].astype(F32), axis=0) for p in range(pieces)]
-    mixer_shard = jnp.concatenate(shards[:MIXER_PARTS], axis=2)
-    ffn_shard = jnp.concatenate(shards[MIXER_PARTS:], axis=3)
+        taps.append(tap_grads)
+        sums[name] = dict(keep=keep, send=send)
+    places = [start("sum core", names[-1]), start("sum z", last - 1), start("sum sides", last)]
+    if parts > 1:
+        places.append(start("sum corner", names[0]))
+    grad_tokens, gain_one_part = row_call(
+        leave_kernel, flip, [grad_normed, tokens_low, grad_hidden, gain_one], [F32], 1
+    )
+    item = sums[names[-1]]
+    grad_tokens, gain_one_part, item["keep"] = close(
+        [grad_tokens, gain_one_part, item["keep"]], places
+    )
+
+    place = links.place(jnp.arange(links.dp))
+    taps = jnp.concatenate(taps, axis=1)[:kernel].reshape(kernel, -1, 2, tile)
+    taps = taps.transpose(0, 2, 1, 3).reshape(kernel, width)
+    taps = jnp.where(rank == 0, taps, jnp.roll(taps, half, axis=1))
+    gains = jnp.stack([gain_one_part.sum(0), gain_two_part.sum(0)])
+    gains = jnp.take(gains.reshape(2, links.dp, block), place, axis=1).reshape(2, width)
+    small = links.sum_chip(jnp.concatenate([gains, taps], axis=0))
+
+    places = [start("sum corner", names[-1]), start("sum z", last)]
+    if parts > 1:
+        places.append(start("sum sides", names[0]))
+    result = row_call(
+        result_kernel, flip, [hidden, totals[0], links.swap(totals[2], c=1)], [BF]
+    )[0]
+    result, small = close([result, small], places)
+    places = [start("sum sides", names[-1])]
+    if parts > 1:
+        places.append(start("sum z", names[0]))
+    (small,) = close([links.sum_rest(small)], places)
+    start("sum z", names[-1])
+    shard = lambda p: jnp.sum(sums[p]["z"].astype(F32), axis=0)
+    mixer_shard = jnp.concatenate([shard(name) for name in names], axis=2)
+    ffn_shard = jnp.concatenate([shard(p) for p in range(1, pieces)], axis=3)
     here, there = ffn_shard[0], links.swap(ffn_shard[1], c=1)
     ffn_shard = jnp.concatenate(
         [jnp.where(core == 0, here, there), jnp.where(core == 0, there, here)], axis=2
     )
-    gain_one_part = jnp.sum(grad_normed * unit_one, axis=0)
-    grad_tokens = grad_hidden + norm_back(grad_normed, gain_one, inverse_one, unit_one)
-    high = grad_tokens.astype(BF)
-    rest = grad_tokens - high.astype(F32)
-    middle = rest.astype(BF)
-    low = (rest - middle.astype(F32)).astype(BF)
-    grad_tokens = dot_nt(high, order) + (dot_nt(middle, order) + dot_nt(low, order))
-
-    place = links.place(jnp.arange(links.dp))
-    taps = jnp.concatenate(
-        [
-            item[:kernel].reshape(kernel, part // MIXER_TILE, 2, MIXER_TILE)
-            for item in tap_grads
-        ],
-        axis=1,
-    )
-    taps = taps.transpose(0, 2, 1, 3).reshape(kernel, width)
-    taps = jnp.where(rank == 0, taps, jnp.roll(taps, half, axis=1))
-    gains = jnp.stack([gain_one_part, gain_two_part]).reshape(2, links.dp, block)
-    gains = jnp.take(gains, place, axis=1).reshape(2, width)
-    small = links.sum_all(jnp.concatenate([gains, taps], axis=0))
-
     return (
         result,
         grad_tokens,

time: 678 us -> 543 us (0.80)
  matrix products: 41.2 us -> 0 us
  waiting for transfers between devices: 127 us -> 87.2 us
  other arithmetic: 42.7 us -> 17.4 us
  starting transfers between devices: 128 us -> 107 us
  local copies, waits for them, and re-layouts: 53 us -> 41.5 us
    dot_general x6 -> x0, matrix products: 41.2 us -> none  [the longest x4 32.8 us: dot_nt(): lax.dot_general(left, right, (((1,), (1,)), ((), ())), preferred_element_...]
    pallas_call x0 -> x17, Pallas kernels: none -> 31.7 us  [the longest x4 31.6 us: row_call(): pl.pallas_call(body, grid=(rows // height,), in_specs=[scalar] + specs +...]
    ppermute x71 -> x58, waiting for transfers between devices: 92.9 us -> 65.8 us  [swap(): return lax.ppermute(value, AXES, pairs)]
    pallas_call x5 -> x4, Pallas kernels: 148 us -> 135 us  [ffn_piece(): pl.pallas_call(functools.partial(ffn_kernel, first, last, len(ties)), gri...]
    all_to_all x14 -> x11, starting transfers between devices: 65.9 us -> 53.3 us  [turn_z(): lax.all_to_all(value, 'dp', 0, 0, axis_index_groups=groups, tiled=True)]
    all_to_all x14 -> x11, waiting for transfers between devices: 34 us -> 21.5 us  [turn_z(): lax.all_to_all(value, 'dp', 0, 0, axis_index_groups=groups, tiled=True)]
    convert_element_type x4 -> x0, other arithmetic: 11.9 us -> none  [the longest x1 3.93 us: body(): normed = (unit_one * gain_one).astype(BF)]
    pallas_call x2 -> x1, Pallas kernels: 35.4 us -> 25 us  [mixer_part(): pl.pallas_call(functools.partial(mixer_kernel, first, last, len(ties), mi...]
  transfers between devices with their start and end apart: 85 -> 69, of which waited for: 27 -> 17; matrix products, arithmetic and copies ran while one was open for 18% -> 7% of each run, Pallas kernels for 41% -> 51%
where the time goes in v3:
time: 543 us; the launch traced here: 534 us
  Pallas kernels  279 us (51%)
  starting transfers between devices  107 us (20%)
  waiting for transfers between devices  87.2 us (16%)
  local copies, waits for them, and re-layouts  41.5 us (8%)
  other arithmetic  17.4 us (3%)
    pallas_call x4, Pallas kernels, ffn_piece(): pl.pallas_call(functools.partial(ffn_kernel, first, last, len(ties)), gri...  135 us
    ppermute x58, waiting for transfers between devices, swap(): return lax.ppermute(value, AXES, pairs)  65.8 us
    ppermute x58, starting transfers between devices, swap(): return lax.ppermute(value, AXES, pairs)  53.7 us
    all_to_all x11, starting transfers between devices, turn_z(): lax.all_to_all(value, 'dp', 0, 0, axis_index_groups=groups, tiled=True)  53.3 us
    pallas_call x15, Pallas kernels, small_call(): pl.pallas_call(kernel, grid=(columns // 128,), in_specs=[spec(item.shape)...  44.4 us
    pallas_call x2, Pallas kernels, mixer_back(): pl.pallas_call(functools.partial(mixer_back_kernel, first, len(ties), min...  43.1 us
    pallas_call x4, Pallas kernels, row_call(): pl.pallas_call(body, grid=(rows // height,), in_specs=[scalar] + specs +...  31.6 us
    pallas_call x1, Pallas kernels, mixer_part(): pl.pallas_call(functools.partial(mixer_kernel, first, last, len(ties), mi...  25 us
  transfers between devices with their start and end apart: 69, of which 17 were waited for; matrix products, arithmetic and copies ran while one was open for 7% of the time, Pallas kernels for 51%

profile of v3, /device:TPU:0, one launch (start us, length us, event | category | flops | bytes accessed | tf_op | source)
XLA Modules:
  0.0 534.2 jit_solution(8150770454188911901)
XLA Ops:
  3.8 6.4 %all-to-all-start = ((bf16[4,4,64,512]{3,2,1,0:T(8,128)(2,1)}), bf16[4,4,64,512]{3,2,1,0:T(8,128)(2,1)S(1)}, u32[]{:S(2)}, u32[]{:S(2)}) async-start(bf16[4,4,64,512]{3,2,1,0:T(8,128)(2,1)} %broadcast_in_dim.65.refs_2_), calls=%async_computation | async-start | bytes 2097152 | tf_op jit(solution)/shard_map/all_to_all | solution.py:49
  18.5 8.5 %shard_map.186 = (bf16[1024,1024]{1,0:T(8,128)(2,1)}, bf16[1024,1024]{1,0:T(8,128)(2,1)}, bf16[1024,1024]{1,0:T(8,128)(2,1)}, bf16[1024,1024]{1,0:T(8,128)(2,1)}) custom-call(s32[1]{0:T(128)} %bitcast.refs_0_, s32[1]{0:T(128)} %dynamic_slice.9.refs_1_.refs_0_, bf16[1024,1024]{1,0:T(8,128)(2,1)} %refs_2_.1, bf16[1024,1024]{1,0:T(8,128)(2,1)} %refs_3_.1, ...), custom_call_target="tpu_custom_call" | custom-call | flops 20971520 | bytes 12582912 | tf_op jit(solution)/shard_map/pallas_call | solution.py:604
  27.0 9.0 %all-to-all-done.refs_7_ = bf16[4,4,64,512]{3,2,1,0:T(8,128)(2,1)S(1)} async-done(((bf16[4,4,64,512]{3,2,1,0:T(8,128)(2,1)}), bf16[4,4,64,512]{3,2,1,0:T(8,128)(2,1)S(1)}, u32[]{:S(2)}, u32[]{:S(2)}) %all-to-all-start) | async-done | bytes 1048608 | tf_op jit(solution)/shard_map/all_to_all | solution.py:49
  43.5 21.3 %collective-permute-done.1.refs_2_ = bf16[4,4,64,512]{3,2,1,0:T(8,128)(2,1)S(1)} collective-permute-done((bf16[4,4,64,512]{3,2,1,0:T(8,128)(2,1)}, bf16[4,4,64,512]{3,2,1,0:T(8,128)(2,1)S(1)}, u32[]{:S(2)}, u32[]{:S(2)}) %collective-permute-start.1) | collective-permute-done | bytes 1048608 | tf_op jit(solution)/shard_map/ppermute | solution.py:45
  67.3 4.8 all-to-all-start.2
  75.5 8.9 %collective-permute-done.3.refs_2_ = bf16[2,4,64,512]{3,2,1,0:T(8,128)(2,1)S(1)} collective-permute-done((bf16[2,4,64,512]{3,2,1,0:T(8,128)(2,1)S(1)}, bf16[2,4,64,512]{3,2,1,0:T(8,128)(2,1)S(1)}, u32[]{:S(2)}, u32[]{:S(2)}) %collective-permute-start.3) | collective-permute-done | bytes 524320 | tf_op jit(solution)/shard_map/ppermute | solution.py:45
  85.8 4.2 all-to-all-done.2.refs_4_
  90.9 4.9 shard_map.190.refs_5_
  105.3 25.0 %shard_map.191 = (f32[3,1024,1024]{2,1,0:T(8,128)}, f32[1024,1024]{1,0:T(8,128)}, bf16[1024,1024]{1,0:T(8,128)(2,1)}, bf16[1024,1024]{1,0:T(8,128)(2,1)}) custom-call(s32[1]{0:T(128)} %dynamic_slice.9.refs_1_.refs_0_, bf16[1024,1024]{1,0:T(8,128)(2,1)} %get-tuple-element.213.refs_1_, bf16[1024,1024]{1,0:T(8,128)(2,1)} %get-tuple-element.214.refs_2_, ...), custom_call_target="tpu_custom_call" | custom-call | flops 34359738368 | bytes 29360128 | tf_op jit(solution)/shard_map/pallas_call | solution.py:432
  146.2 4.0 all-to-all-start.4
  154.1 28.4 %shard_map.193 = (bf16[2,2,2,3,64,256]{5,4,3,2,1,0:T(8,128)(2,1)}, bf16[2,2,2,3,64,256]{5,4,3,2,1,0:T(8,128)(2,1)}, bf16[2,2,3,64,256]{4,3,2,1,0:T(8,128)(2,1)},...) custom-call(bf16[1024,1024]{1,0:T(8,128)(2,1)} %get-tuple-element.23, ...), custom_call_target="tpu_custom_call" | custom-call | flops 77309411328 | bytes 48234496 | tf_op jit(solution)/shard_map/pallas_call | solution.py:304
  182.5 3.7 collective-permute-done.14.refs_9_
  196.8 31.8 %shard_map.195 = (bf16[2,2,2,3,64,256]{5,4,3,2,1,0:T(8,128)(2,1)}, bf16[2,2,2,3,64,256]{5,4,3,2,1,0:T(8,128)(2,1)}, bf16[2,2,3,64,256]{4,3,2,1,0:T(8,128)(2,1)},...) custom-call(bf16[1024,1024]{1,0:T(8,128)(2,1)} %get-tuple-element.23, ...), custom_call_target="tpu_custom_call" | custom-call | flops 77309411328 | bytes 48234496 | tf_op jit(solution)/shard_map/pallas_call | solution.py:304
  236.2 43.7 %shard_map.197 = (bf16[2,2,2,3,64,384]{5,4,3,2,1,0:T(8,128)(2,1)}, bf16[2,2,2,3,64,384]{5,4,3,2,1,0:T(8,128)(2,1)}, bf16[2,2,3,64,384]{4,3,2,1,0:T(8,128)(2,1)},...) custom-call(bf16[1024,1024]{1,0:T(8,128)(2,1)} %get-tuple-element.23, ...), custom_call_target="tpu_custom_call" | custom-call | flops 115964116992 | bytes 51380224 | tf_op jit(solution)/shard_map/pallas_call | solution.py:304
  286.2 30.9 %shard_map.199 = (bf16[2,2,2,3,64,256]{5,4,3,2,1,0:T(8,128)(2,1)}, bf16[2,2,2,3,64,256]{5,4,3,2,1,0:T(8,128)(2,1)}, bf16[2,2,3,64,256]{4,3,2,1,0:T(8,128)(2,1)},...) custom-call(bf16[1024,1024]{1,0:T(8,128)(2,1)} %get-tuple-element.23, ...), custom_call_target="tpu_custom_call" | custom-call | flops 77309411328 | bytes 48234496 | tf_op jit(solution)/shard_map/pallas_call | solution.py:304
  327.7 5.0 all-to-all-start.5
  333.9 8.4 %shard_map.202 = (bf16[1024,1024]{1,0:T(8,128)(2,1)}, f32[1024,1024]{1,0:T(8,128)}, f32[8,1024]{1,0:T(8,128)}) custom-call(s32[1]{0:T(128)} %bitcast.refs_0_, f32[1024,1024]{1,0:T(8,128)} %get-tuple-element.312.refs_1_, bf16[1024,1024]{1,0:T(8,128)(2,1)} %collective-permute-done.30.refs_2_, f32[1024,1024]{1,0:T(8,128)} %get-tuple-element.226.refs_3_.refs_1_, ...), custom_call_target="tpu_custom_call" | custom-call | flops 20971520 | bytes 12582912 | tf_op jit(solution)/shard_map/pallas_call | solution.py:604
  342.3 20.9 %shard_map.203 = (bf16[4,4,4,64,256]{4,3,2,1,0:T(8,128)(2,1)}, bf16[4,4,4,64,256]{4,3,2,1,0:T(8,128)(2,1)}, f32[8,512]{1,0:T(8,128)}, f32[1024,1024]{1,0:T(8,128)}) custom-call(s32[1]{0:T(128)} %dynamic_slice.9.refs_1_.refs_0_, bf16[1024,1024]{1,0:T(8,128)(2,1)} %get-tuple-element.213.refs_1_, bf16[1024,1024]{1,0:T(8,128)(2,1)} %get-tuple-element.314.refs_2_, ...), custom_call_target="tpu_custom_call" | custom-call | flops 34359738368 | bytes 23068672 | tf_op jit(solution)/shard_map/pallas_call | solution.py:539
  365.6 3.8 shard_map.209
  374.5 5.3 all-to-all-start.6
  379.9 22.2 %shard_map.207 = (bf16[4,4,4,64,256]{4,3,2,1,0:T(8,128)(2,1)}, bf16[4,4,4,64,256]{4,3,2,1,0:T(8,128)(2,1)}, f32[8,512]{1,0:T(8,128)}, f32[1024,1024]{1,0:T(8,128)}) custom-call(s32[1]{0:T(128)} %dynamic_slice.9.refs_1_.refs_0_, bf16[1024,1024]{1,0:T(8,128)(2,1)} %get-tuple-element.213.refs_1_, ...), custom_call_target="tpu_custom_call", output_to_operand_aliasing={{3}: (7, {})} | custom-call | flops 34359738368 | bytes 23068672 | tf_op jit(solution)/shard_map/pallas_call | solution.py:539
  404.4 4.2 shard_map.213
  408.5 5.5 %all-to-all-start.7 = ((bf16[4,2,3,64,384]{4,3,2,1,0:T(8,128)(2,1)}), bf16[4,2,3,64,384]{4,3,2,1,0:T(8,128)(2,1)S(1)}, u32[]{:S(2)}, u32[]{:S(2)}) async-start(bf16[4,2,3,64,384]{4,3,2,1,0:T(8,128)(2,1)} %shard_map.213), calls=%async_computation.7 | async-start | bytes 2359296 | tf_op jit(solution)/shard_map/all_to_all | solution.py:49
  422.8 6.1 %collective-permute-done.42.refs_5_ = bf16[2,2,3,64,256]{4,3,2,1,0:T(8,128)(2,1)} collective-permute-done((bf16[2,2,3,64,256]{4,3,2,1,0:T(8,128)(2,1)}, bf16[2,2,3,64,256]{4,3,2,1,0:T(8,128)(2,1)}, u32[]{:S(2)}, u32[]{:S(2)}) %collective-permute-start.42) | collective-permute-done | bytes 393248 | tf_op jit(solution)/shard_map/ppermute | solution.py:45
  431.7 8.2 %shard_map.212 = (f32[1024,1024]{1,0:T(8,128)}, f32[8,1024]{1,0:T(8,128)}) custom-call(s32[1]{0:T(128)} %bitcast.refs_0_, f32[1024,1024]{1,0:T(8,128)} %get-tuple-element.354.refs_1_, bf16[1024,1024]{1,0:T(8,128)(2,1)} %get-tuple-element.214.refs_2_, f32[1024,1024]{1,0:T(8,128)} %get-tuple-element.355.refs_3_, f32[1,1024]{1,0:T(1,128)} %reshape.202.refs_4_), custom_call_target="tpu_custom_call" | custom-call | flops 20971520 | bytes 12582912 | tf_op jit(solution)/shard_map/pallas_call | solution.py:604
  439.8 4.7 collective-permute-done.43.refs_6_
  448.3 5.1 all-to-all-start.8
  467.6 6.5 %shard_map.211.refs_0_ = bf16[1024,1024]{1,0:T(8,128)(2,1)} custom-call(s32[1]{0:T(128)} %bitcast.refs_0_, f32[1024,1024]{1,0:T(8,128)} %get-tuple-element.226.refs_3_.refs_1_, f32[1024,1024]{1,0:T(8,128)} %get-tuple-element.352.refs_2_, bf16[1024,1024]{1,0:T(8,128)(2,1)} %collective-permute-done.40.refs_3_), custom_call_target="tpu_custom_call" | custom-call | flops 20971520 | bytes 12582912 | tf_op jit(solution)/shard_map/pallas_call | solution.py:604
  482.6 4.8 all-to-all-start.9
  494.4 7.0 %collective-permute-done.52 = f32[5,1024]{1,0:T(8,128)S(1)} collective-permute-done((f32[5,1024]{1,0:T(8,128)S(1)}, f32[5,1024]{1,0:T(8,128)S(1)}, u32[]{:S(2)}, u32[]{:S(2)}) %collective-permute-start.52) | collective-permute-done | bytes 20512 | tf_op jit(solution)/shard_map/ppermute | solution.py:45
  514.7 5.4 %all-to-all-start.10 = ((bf16[4,4,64,256]{3,2,1,0:T(8,128)(2,1)}), bf16[4,4,64,256]{3,2,1,0:T(8,128)(2,1)S(1)}, u32[]{:S(2)}, u32[]{:S(2)}) async-start(bf16[4,4,64,256]{3,2,1,0:T(8,128)(2,1)} %shard_map.224), calls=%async_computation.10 | async-start | bytes 1048576 | tf_op jit(solution)/shard_map/all_to_all | solution.py:49
  524.0 8.2 %all-to-all-done.10 = bf16[4,4,64,256]{3,2,1,0:T(8,128)(2,1)S(1)} async-done(((bf16[4,4,64,256]{3,2,1,0:T(8,128)(2,1)}), bf16[4,4,64,256]{3,2,1,0:T(8,128)(2,1)S(1)}, u32[]{:S(2)}, u32[]{:S(2)}) %all-to-all-start.10) | async-done | bytes 524320 | tf_op jit(solution)/shard_map/all_to_all | solution.py:49
  (333 shorter events, 165.4 us)
Async XLA Ops:
  97.1 53.1 %collective-permute-start.11 = (bf16[1024,1024]{1,0:T(8,128)(2,1)}, bf16[1024,1024]{1,0:T(8,128)(2,1)}, u32[]{:S(2)}, u32[]{:S(2)}) collective-permute-start(bf16[1024,1024]{1,0:T(8,128)(2,1)} %get-tuple-element.236), channel_id=1, source_target_pairs={{0,2},{1,3},{2,0},{3,1},{4,6},{5,7},{6,4},{7,5},{8,10},{9,11},{10,... | collective-permute-start | bytes 6291464 | tf_op jit(solution)/shard_map/ppermute | solution.py:45
  97.6 32.7 %collective-permute-start.6 = (bf16[4,2,3,64,256]{4,3,2,1,0:T(8,128)(2,1)S(1)}, bf16[4,2,3,64,256]{4,3,2,1,0:T(8,128)(2,1)}, u32[]{:S(2)}, u32[]{:S(2)}) collective-permute-start(bf16[4,2,3,64,256]{4,3,2,1,0:T(8,128)(2,1)S(1)} %copy-done.11), channel_id=1, source_target_pairs={{0,4},{1,5},{2,6},{3,7},{4,0},{5,1},{6,2},{7,3},{8,12},{9,13},{10,... | collective-permute-start | bytes 2359304 | tf_op jit(solution)/shard_map/ppermute | solution.py:45
  100.0 34.0 %collective-permute-start.8 = (bf16[4,2,3,64,256]{4,3,2,1,0:T(8,128)(2,1)S(1)}, bf16[4,2,3,64,256]{4,3,2,1,0:T(8,128)(2,1)}, u32[]{:S(2)}, u32[]{:S(2)}) collective-permute-start(bf16[4,2,3,64,256]{4,3,2,1,0:T(8,128)(2,1)S(1)} %copy-done.22), channel_id=1, source_target_pairs={{0,4},{1,5},{2,6},{3,7},{4,0},{5,1},{6,2},{7,3},{8,12},{9,13},{10,... | collective-permute-start | bytes 2359304 | tf_op jit(solution)/shard_map/ppermute | solution.py:45
  101.1 33.5 %all-to-all-start.3 = ((bf16[4,2,3,64,384]{4,3,2,1,0:T(8,128)(2,1)}), bf16[4,2,3,64,384]{4,3,2,1,0:T(8,128)(2,1)S(1)}, u32[]{:S(2)}, u32[]{:S(2)}) async-start(bf16[4,2,3,64,384]{4,3,2,1,0:T(8,128)(2,1)} %get-tuple-element.232), calls=%async_computation.3 | async-start | bytes 2359296 | tf_op jit(solution)/shard_map/all_to_all | solution.py:49
  141.8 44.4 %collective-permute-start.16 = (bf16[4,2,3,64,384]{4,3,2,1,0:T(8,128)(2,1)}, bf16[4,2,3,64,384]{4,3,2,1,0:T(8,128)(2,1)S(1)}, u32[]{:S(2)}, u32[]{:S(2)}) collective-permute-start(bf16[4,2,3,64,384]{4,3,2,1,0:T(8,128)(2,1)} %get-tuple-element.250.refs_4_), channel_id=1, source_target_pairs={{0,4},{1,5},{2,6},{3,7},{4,0},{5,1},{6,2},{7,3},{8,12},{9,13},{10,... | collective-permute-start | bytes 3538952 | tf_op jit(solution)/shard_map/ppermute | solution.py:45
  146.2 40.9 %all-to-all-start.4 = ((bf16[4,2,3,64,256]{4,3,2,1,0:T(8,128)(2,1)}), bf16[4,2,3,64,256]{4,3,2,1,0:T(8,128)(2,1)S(1)}, u32[]{:S(2)}, u32[]{:S(2)}) async-start(bf16[4,2,3,64,256]{4,3,2,1,0:T(8,128)(2,1)} %get-tuple-element.251), calls=%async_computation.4 | async-start | bytes 1572864 | tf_op jit(solution)/shard_map/all_to_all | solution.py:49
  150.2 36.9 %collective-permute-start.17 = (bf16[4,2,3,64,384]{4,3,2,1,0:T(8,128)(2,1)S(1)}, bf16[4,2,3,64,384]{4,3,2,1,0:T(8,128)(2,1)}, u32[]{:S(2)}, u32[]{:S(2)}) collective-permute-start(bf16[4,2,3,64,384]{4,3,2,1,0:T(8,128)(2,1)S(1)} %copy-done.17), channel_id=1, source_target_pairs={{0,1},{1,0},{2,3},{3,2},{4,5},{5,4},{6,7},{7,6},{8,9},{9,8},{10,11... | collective-permute-start | bytes 3538952 | tf_op jit(solution)/shard_map/ppermute | solution.py:45
  150.8 35.5 %collective-permute-start.14 = (bf16[2,2,3,64,256]{4,3,2,1,0:T(8,128)(2,1)}, bf16[2,2,3,64,256]{4,3,2,1,0:T(8,128)(2,1)S(1)}, u32[]{:S(2)}, u32[]{:S(2)}) collective-permute-start(bf16[2,2,3,64,256]{4,3,2,1,0:T(8,128)(2,1)} %slice.99), channel_id=1, source_target_pairs={{0,1},{1,0},{2,3},{3,2},{4,5},{5,4},{6,7},{7,6},{8,9},{9,8},{10,11... | collective-permute-start | bytes 1179656 | tf_op jit(solution)/shard_map/ppermute | solution.py:45
  152.9 33.3 %collective-permute-start.15 = (bf16[2,2,3,64,256]{4,3,2,1,0:T(8,128)(2,1)}, bf16[2,2,3,64,256]{4,3,2,1,0:T(8,128)(2,1)S(1)}, u32[]{:S(2)}, u32[]{:S(2)}) collective-permute-start(bf16[2,2,3,64,256]{4,3,2,1,0:T(8,128)(2,1)} %slice.100), channel_id=1, source_target_pairs={{0,4},{1,5},{2,6},{3,7},{4,0},{5,1},{6,2},{7,3},{8,12},{9,13},{10,... | collective-permute-start | bytes 1179656 | tf_op jit(solution)/shard_map/ppermute | solution.py:45
  188.4 40.9 %collective-permute-start.20 = (bf16[4,2,3,64,256]{4,3,2,1,0:T(8,128)(2,1)}, bf16[4,2,3,64,256]{4,3,2,1,0:T(8,128)(2,1)S(1)}, u32[]{:S(2)}, u32[]{:S(2)}) collective-permute-start(bf16[4,2,3,64,256]{4,3,2,1,0:T(8,128)(2,1)} %get-tuple-element.252.refs_4_), channel_id=1, source_target_pairs={{0,4},{1,5},{2,6},{3,7},{4,0},{5,1},{6,2},{7,3},{8,12},{9,13},{10,... | collective-permute-start | bytes 2359304 | tf_op jit(solution)/shard_map/ppermute | solution.py:45
  189.6 39.8 %collective-permute-start.21 = (bf16[4,2,3,64,256]{4,3,2,1,0:T(8,128)(2,1)}, bf16[4,2,3,64,256]{4,3,2,1,0:T(8,128)(2,1)S(1)}, u32[]{:S(2)}, u32[]{:S(2)}) collective-permute-start(bf16[4,2,3,64,256]{4,3,2,1,0:T(8,128)(2,1)} %get-tuple-element.252.refs_4_), channel_id=1, source_target_pairs={{0,1},{1,0},{2,3},{3,2},{4,5},{5,4},{6,7},{7,6},{8,9},{9,8},{10,11... | collective-permute-start | bytes 2359304 | tf_op jit(solution)/shard_map/ppermute | solution.py:45
  191.3 37.3 %collective-permute-start.18 = (bf16[2,2,3,64,384]{4,3,2,1,0:T(8,128)(2,1)S(1)}, bf16[2,2,3,64,384]{4,3,2,1,0:T(8,128)(2,1)S(1)}, u32[]{:S(2)}, u32[]{:S(2)}) collective-permute-start(bf16[2,2,3,64,384]{4,3,2,1,0:T(8,128)(2,1)S(1)} %slice.101), channel_id=1, source_target_pairs={{0,1},{1,0},{2,3},{3,2},{4,5},{5,4},{6,7},{7,6},{8,9},{9,8},{10,11... | collective-permute-start | bytes 1769480 | tf_op jit(solution)/shard_map/ppermute | solution.py:45
  194.8 34.6 %collective-permute-start.19 = (bf16[2,2,3,64,384]{4,3,2,1,0:T(8,128)(2,1)}, bf16[2,2,3,64,384]{4,3,2,1,0:T(8,128)(2,1)}, u32[]{:S(2)}, u32[]{:S(2)}) collective-permute-start(bf16[2,2,3,64,384]{4,3,2,1,0:T(8,128)(2,1)} %slice.102), channel_id=1, source_target_pairs={{0,4},{1,5},{2,6},{3,7},{4,0},{5,1},{6,2},{7,3},{8,12},{9,13},{10,... | collective-permute-start | bytes 1769480 | tf_op jit(solution)/shard_map/ppermute | solution.py:45
  195.6 84.2 %collective-permute-start.24 = (bf16[2,2,2,3,64,256]{5,4,3,2,1,0:T(8,128)(2,1)}, bf16[2,2,2,3,64,256]{5,4,3,2,1,0:T(8,128)(2,1)}, u32[]{:S(2)}, u32[]{:S(2)}) collective-permute-start(bf16[2,2,2,3,64,256]{5,4,3,2,1,0:T(8,128)(2,1)} %get-tuple-element.287), channel_id=1, source_target_pairs={{0,4},{1,5},{2,6},{3,7},{4,0},{5,1},{6,2},{7,3},{8,12},{9,13},{10,... | collective-permute-start | bytes 2359304 | tf_op jit(solution)/shard_map/ppermute | solution.py:45
  228.7 51.9 %collective-permute-start.25 = (bf16[2,2,2,3,64,256]{5,4,3,2,1,0:T(8,128)(2,1)S(1)}, bf16[2,2,2,3,64,256]{5,4,3,2,1,0:T(8,128)(2,1)S(1)}, u32[]{:S(2)}, u32[]{:S(2)}) collective-permute-start(bf16[2,2,2,3,64,256]{5,4,3,2,1,0:T(8,128)(2,1)S(1)} %copy-done.38), channel_id=1, source_target_pairs={{0,1},{1,0},{2,3},{3,2},{4,5},{5,4},{6,7},{7,6},{8,9},{9,8},{10,11... | collective-permute-start | bytes 2359304 | tf_op jit(solution)/shard_map/ppermute | solution.py:45
  231.5 49.0 %collective-permute-start.22 = (bf16[2,2,3,64,256]{4,3,2,1,0:T(8,128)(2,1)S(1)}, bf16[2,2,3,64,256]{4,3,2,1,0:T(8,128)(2,1)}, u32[]{:S(2)}, u32[]{:S(2)}) collective-permute-start(bf16[2,2,3,64,256]{4,3,2,1,0:T(8,128)(2,1)S(1)} %slice.103), channel_id=1, source_target_pairs={{0,1},{1,0},{2,3},{3,2},{4,5},{5,4},{6,7},{7,6},{8,9},{9,8},{10,11... | collective-permute-start | bytes 1179656 | tf_op jit(solution)/shard_map/ppermute | solution.py:45
  234.1 46.5 %collective-permute-start.23 = (bf16[2,2,3,64,256]{4,3,2,1,0:T(8,128)(2,1)S(1)}, bf16[2,2,3,64,256]{4,3,2,1,0:T(8,128)(2,1)}, u32[]{:S(2)}, u32[]{:S(2)}) collective-permute-start(bf16[2,2,3,64,256]{4,3,2,1,0:T(8,128)(2,1)S(1)} %slice.104), channel_id=1, source_target_pairs={{0,4},{1,5},{2,6},{3,7},{4,0},{5,1},{6,2},{7,3},{8,12},{9,13},{10,... | collective-permute-start | bytes 1179656 | tf_op jit(solution)/shard_map/ppermute | solution.py:45
  235.0 82.2 %collective-permute-start.28 = (bf16[2,2,2,3,64,256]{5,4,3,2,1,0:T(8,128)(2,1)}, bf16[2,2,2,3,64,256]{5,4,3,2,1,0:T(8,128)(2,1)}, u32[]{:S(2)}, u32[]{:S(2)}) collective-permute-start(bf16[2,2,2,3,64,256]{5,4,3,2,1,0:T(8,128)(2,1)} %get-tuple-element.310), channel_id=1, source_target_pairs={{0,4},{1,5},{2,6},{3,7},{4,0},{5,1},{6,2},{7,3},{8,12},{9,13},{10,... | collective-permute-start | bytes 2359304 | tf_op jit(solution)/shard_map/ppermute | solution.py:45
  279.9 37.3 %collective-permute-start.29 = (bf16[2,2,2,3,64,256]{5,4,3,2,1,0:T(8,128)(2,1)S(1)}, bf16[2,2,2,3,64,256]{5,4,3,2,1,0:T(8,128)(2,1)S(1)}, u32[]{:S(2)}, u32[]{:S(2)}) collective-permute-start(bf16[2,2,2,3,64,256]{5,4,3,2,1,0:T(8,128)(2,1)S(1)} %copy-done.37), channel_id=1, source_target_pairs={{0,1},{1,0},{2,3},{3,2},{4,5},{5,4},{6,7},{7,6},{8,9},{9,8},{10,11... | collective-permute-start | bytes 2359304 | tf_op jit(solution)/shard_map/ppermute | solution.py:45
  283.9 33.2 %collective-permute-start.26 = (bf16[2,2,3,64,256]{4,3,2,1,0:T(8,128)(2,1)}, bf16[2,2,3,64,256]{4,3,2,1,0:T(8,128)(2,1)S(1)}, u32[]{:S(2)}, u32[]{:S(2)}) collective-permute-start(bf16[2,2,3,64,256]{4,3,2,1,0:T(8,128)(2,1)} %get-tuple-element.308), channel_id=1, source_target_pairs={{0,4},{1,5},{2,6},{3,7},{4,0},{5,1},{6,2},{7,3},{8,12},{9,13},{10,... | collective-permute-start | bytes 1179656 | tf_op jit(solution)/shard_map/ppermute | solution.py:45
  284.8 32.4 %collective-permute-start.27 = (bf16[2,2,3,64,256]{4,3,2,1,0:T(8,128)(2,1)}, bf16[2,2,3,64,256]{4,3,2,1,0:T(8,128)(2,1)S(1)}, u32[]{:S(2)}, u32[]{:S(2)}) collective-permute-start(bf16[2,2,3,64,256]{4,3,2,1,0:T(8,128)(2,1)} %get-tuple-element.309), channel_id=1, source_target_pairs={{0,1},{1,0},{2,3},{3,2},{4,5},{5,4},{6,7},{7,6},{8,9},{9,8},{10,11... | collective-permute-start | bytes 1179656 | tf_op jit(solution)/shard_map/ppermute | solution.py:45
  318.3 45.6 %collective-permute-start.33 = (bf16[2,2,2,3,64,384]{5,4,3,2,1,0:T(8,128)(2,1)}, bf16[2,2,2,3,64,384]{5,4,3,2,1,0:T(8,128)(2,1)S(1)}, u32[]{:S(2)}, u32[]{:S(2)}) collective-permute-start(bf16[2,2,2,3,64,384]{5,4,3,2,1,0:T(8,128)(2,1)} %get-tuple-element.331), channel_id=1, source_target_pairs={{0,4},{1,5},{2,6},{3,7},{4,0},{5,1},{6,2},{7,3},{8,12},{9,13},{10,... | collective-permute-start | bytes 3538952 | tf_op jit(solution)/shard_map/ppermute | solution.py:45
  319.5 44.4 %collective-permute-start.34 = (bf16[2,2,2,3,64,384]{5,4,3,2,1,0:T(8,128)(2,1)}, bf16[2,2,2,3,64,384]{5,4,3,2,1,0:T(8,128)(2,1)S(1)}, u32[]{:S(2)}, u32[]{:S(2)}) collective-permute-start(bf16[2,2,2,3,64,384]{5,4,3,2,1,0:T(8,128)(2,1)} %get-tuple-element.332), channel_id=1, source_target_pairs={{0,1},{1,0},{2,3},{3,2},{4,5},{5,4},{6,7},{7,6},{8,9},{9,8},{10,11... | collective-permute-start | bytes 3538952 | tf_op jit(solution)/shard_map/ppermute | solution.py:45
  322.6 40.7 %collective-permute-start.31 = (bf16[2,2,3,64,256]{4,3,2,1,0:T(8,128)(2,1)}, bf16[2,2,3,64,256]{4,3,2,1,0:T(8,128)(2,1)S(1)}, u32[]{:S(2)}, u32[]{:S(2)}) collective-permute-start(bf16[2,2,3,64,256]{4,3,2,1,0:T(8,128)(2,1)} %get-tuple-element.329), channel_id=1, source_target_pairs={{0,4},{1,5},{2,6},{3,7},{4,0},{5,1},{6,2},{7,3},{8,12},{9,13},{10,... | collective-permute-start | bytes 1179656 | tf_op jit(solution)/shard_map/ppermute | solution.py:45
  323.4 40.5 %collective-permute-start.32 = (bf16[2,2,3,64,256]{4,3,2,1,0:T(8,128)(2,1)}, bf16[2,2,3,64,256]{4,3,2,1,0:T(8,128)(2,1)}, u32[]{:S(2)}, u32[]{:S(2)}) collective-permute-start(bf16[2,2,3,64,256]{4,3,2,1,0:T(8,128)(2,1)} %get-tuple-element.330), channel_id=1, source_target_pairs={{0,1},{1,0},{2,3},{3,2},{4,5},{5,4},{6,7},{7,6},{8,9},{9,8},{10,11... | collective-permute-start | bytes 1179656 | tf_op jit(solution)/shard_map/ppermute | solution.py:45
  327.7 36.2 %all-to-all-start.5 = ((bf16[4,2,3,64,256]{4,3,2,1,0:T(8,128)(2,1)}), bf16[4,2,3,64,256]{4,3,2,1,0:T(8,128)(2,1)S(1)}, u32[]{:S(2)}, u32[]{:S(2)}) async-start(bf16[4,2,3,64,256]{4,3,2,1,0:T(8,128)(2,1)} %shard_map.204), calls=%async_computation.5 | async-start | bytes 1572864 | tf_op jit(solution)/shard_map/all_to_all | solution.py:49
  332.7 69.4 %collective-permute-start.38 = (bf16[2,2,2,3,64,256]{5,4,3,2,1,0:T(8,128)(2,1)}, bf16[2,2,2,3,64,256]{5,4,3,2,1,0:T(8,128)(2,1)}, u32[]{:S(2)}, u32[]{:S(2)}) collective-permute-start(bf16[2,2,2,3,64,256]{5,4,3,2,1,0:T(8,128)(2,1)} %get-tuple-element.350), channel_id=1, source_target_pairs={{0,4},{1,5},{2,6},{3,7},{4,0},{5,1},{6,2},{7,3},{8,12},{9,13},{10,... | collective-permute-start | bytes 2359304 | tf_op jit(solution)/shard_map/ppermute | solution.py:45
  363.2 38.8 %collective-permute-start.39 = (bf16[2,2,2,3,64,256]{5,4,3,2,1,0:T(8,128)(2,1)}, bf16[2,2,2,3,64,256]{5,4,3,2,1,0:T(8,128)(2,1)}, u32[]{:S(2)}, u32[]{:S(2)}) collective-permute-start(bf16[2,2,2,3,64,256]{5,4,3,2,1,0:T(8,128)(2,1)} %get-tuple-element.351), channel_id=1, source_target_pairs={{0,1},{1,0},{2,3},{3,2},{4,5},{5,4},{6,7},{7,6},{8,9},{9,8},{10,11... | collective-permute-start | bytes 2359304 | tf_op jit(solution)/shard_map/ppermute | solution.py:45
  369.4 32.7 %collective-permute-start.36 = (bf16[2,2,3,64,384]{4,3,2,1,0:T(8,128)(2,1)}, bf16[2,2,3,64,384]{4,3,2,1,0:T(8,128)(2,1)S(1)}, u32[]{:S(2)}, u32[]{:S(2)}) collective-permute-start(bf16[2,2,3,64,384]{4,3,2,1,0:T(8,128)(2,1)} %get-tuple-element.348), channel_id=1, source_target_pairs={{0,4},{1,5},{2,6},{3,7},{4,0},{5,1},{6,2},{7,3},{8,12},{9,13},{10,... | collective-permute-start | bytes 1769480 | tf_op jit(solution)/shard_map/ppermute | solution.py:45
  403.9 40.7 %collective-permute-start.41 = (bf16[4,4,4,64,256]{4,3,2,1,0:T(8,128)(2,1)}, bf16[4,4,4,64,256]{4,3,2,1,0:T(8,128)(2,1)}, u32[]{:S(2)}, u32[]{:S(2)}) collective-permute-start(bf16[4,4,4,64,256]{4,3,2,1,0:T(8,128)(2,1)} %get-tuple-element.359), channel_id=1, source_target_pairs={{0,2},{1,3},{2,0},{3,1},{4,6},{5,7},{6,4},{7,5},{8,10},{9,11},{10,... | collective-permute-start | bytes 6291464 | tf_op jit(solution)/shard_map/ppermute | solution.py:45
  408.5 36.0 %all-to-all-start.7 = ((bf16[4,2,3,64,384]{4,3,2,1,0:T(8,128)(2,1)}), bf16[4,2,3,64,384]{4,3,2,1,0:T(8,128)(2,1)S(1)}, u32[]{:S(2)}, u32[]{:S(2)}) async-start(bf16[4,2,3,64,384]{4,3,2,1,0:T(8,128)(2,1)} %shard_map.213), calls=%async_computation.7 | async-start | bytes 2359296 | tf_op jit(solution)/shard_map/all_to_all | solution.py:49
  414.0 52.0 %collective-permute-start.40 = (bf16[1024,1024]{1,0:T(8,128)(2,1)S(1)}, bf16[1024,1024]{1,0:T(8,128)(2,1)}, u32[]{:S(2)}, u32[]{:S(2)}) collective-permute-start(bf16[1024,1024]{1,0:T(8,128)(2,1)S(1)} %copy-done), channel_id=1, source_target_pairs={{0,2},{1,3},{2,0},{3,1},{4,6},{5,7},{6,4},{7,5},{8,10},{9,11},{10,... | collective-permute-start | bytes 6291464 | tf_op jit(solution)/shard_map/ppermute | solution.py:45
  (93 other events, 972.8 us)

commit v4 on v3

--- a/solution.py
+++ b/solution.py
@@ -55,8 +55,8 @@
         return self.swap(mine, x=1), self.swap(mine, y=1)
 
     def gather_corner(self, from_x, from_y):
-        half = self.zs // 2
-        return self.swap(from_x[:half], y=1), self.swap(from_y[half:], x=1)
+        low, high = cut(from_x, from_y)
+        return self.swap(low, y=1), self.swap(high, x=1)
 
     def sum_chip(self, value):
         value = value + self.swap(value, c=1)
@@ -129,6 +129,29 @@
         compiler_params=params(),
         cost_estimate=cost(0, 1024),
     )(*values)
+
+
+def cut_kernel(from_x, from_y, low, high):
+    low[...] = from_x[...]
+    high[...] = from_y[...]
+
+
+def cut(from_x, from_y):
+    half, *rest, columns = from_x.shape
+    half //= 2
+    lead = (0,) * len(rest)
+    block = (half, *rest, 128)
+    low = pl.BlockSpec(block, lambda j: (0, *lead, j))
+    high = pl.BlockSpec(block, lambda j: (1, *lead, j))
+    return pl.pallas_call(
+        cut_kernel,
+        grid=(columns // 128,),
+        in_specs=[low, high],
+        out_specs=[low] * 2,
+        out_shape=[jax.ShapeDtypeStruct((half, *rest, columns), BF)] * 2,
+        compiler_params=params(),
+        cost_estimate=cost(0, 4 * from_x.size),
+    )(from_x, from_y)
 
 
 def join_kernel(mine, from_y, from_x, one, two, out):
@@ -245,8 +268,8 @@
         ffn = dot_nt(act, wide[2])
         back = dot_nt(g_gate, wide[0]) + dot_nt(g_up, wide[1])
         if not first:
-            ffn = ffn + before[0][...]
-            back = back + before[1][...]
+            ffn = ffn + before[0][...].astype(F32)
+            back = back + before[1][...].astype(F32)
         if turn:
             ffn, back = other_core_first(ffn), other_core_first(back)
         totals[0][...] = ffn.astype(totals[0].dtype)
@@ -300,7 +323,7 @@
     operands = [*inputs, *cells, *(() if first else before), *ties]
     part = (zs // 2, 2, kinds, block, columns)
     grads = [(2, *part), (2, *part), part, part, (zs, *part[1:])]
-    twin = BF if last else F32
+    mine = F32 if last else BF
     return pl.pallas_call(
         functools.partial(ffn_kernel, first, last, len(ties)),
         grid=(2 * half,),
@@ -310,7 +333,7 @@
         + [ANYWHERE] * len(ties),
         out_specs=[whole_spec(shape) for shape in grads] + [near, near, far, far],
         out_shape=[jax.ShapeDtypeStruct(shape, BF) for shape in grads]
-        + [jax.ShapeDtypeStruct((rows, width), dtype) for dtype in (F32, F32, twin, twin)],
+        + [jax.ShapeDtypeStruct((rows, width), dtype) for dtype in (mine, mine, BF, BF)],
         scratch_shapes=[pltpu.VMEM((kinds, width, 2 * columns), BF)]
         + [pltpu.VMEM((2 * rows, width), BF)] * 2
         + [pltpu.VMEM((2 * rows, 2 * columns), BF)] * 3,
@@ -642,19 +665,18 @@
         total[...] += part
 
 
-def between_kernel(flip, mine, twin, hidden, grad_out, gain, mix, grad_hidden, total, one, two):
+def between_kernel(flip, mine, twin, hidden, grad_out, gain, mix, total, one, two):
     grad = mine[...] + twin[...].astype(F32)
     inverse, unit = norm_stats(hidden[...])
     value = grad_out[...].astype(F32) + norm_back(grad, gain[...], inverse, unit)
     mix[...] = value.astype(BF)
-    grad_hidden[...] = value
     add_up(total, grad * unit)
 
 
 def leave_kernel(flip, grad, tokens, grad_hidden, gain, out, total, one, two):
     inverse, unit = norm_stats(tokens[...].astype(F32))
     value = grad[...]
-    one[...] = grad_hidden[...] + norm_back(value, gain[...], inverse, unit)
+    one[...] = grad_hidden[...].astype(F32) + norm_back(value, gain[...], inverse, unit)
     reorder(one, out, flip[0], False)
     add_up(total, value * unit)
 
@@ -803,13 +825,16 @@
             if q > 0:
                 places.append(start(stage, q))
         *parts, t0, t1, t2, t3 = ffn_piece(inputs, cells(p), totals, p == last, [])
-        parts, totals = close([parts, [t0, t1, t2, t3]], places)
-        sums[p] = dict(parts=parts)
-    grad_mix, grad_hidden, gain_two_part = row_call(
+        held = sums[p - 1]["parts"][:2] if p > 1 else []
+        parts, totals, held = close([parts, [t0, t1, t2, t3], held], places)
+        if p > 1:
+            sums[p - 1]["parts"][:2] = held
+        sums[p] = dict(parts=list(parts))
+    grad_mix, gain_two_part = row_call(
         between_kernel,
         flip,
         [totals[1], links.swap(totals[3], c=1), hidden, grad_ffn, gain_two],
-        [BF, F32],
+        [BF],
         1,
     )
     places = [
@@ -831,16 +856,19 @@
             own_lengths, normed, grad_mix, project, conv, mixer_cells, grad_normed, [],
             tile, p, parts,
         )
-        keep, send, tap_grads, grad_normed, totals[0], totals[2] = close(
-            [keep, send, tap_grads, grad_normed, totals[0], totals[2]], places
+        held = sums[last]["parts"][:2] if p < parts - 1 else []
+        keep, send, tap_grads, grad_normed, totals[0], totals[2], held = close(
+            [keep, send, tap_grads, grad_normed, totals[0], totals[2], held], places
         )
+        if p < parts - 1:
+            sums[last]["parts"][:2] = held
         taps.append(tap_grads)
         sums[name] = dict(keep=keep, send=send)
     places = [start("sum core", names[-1]), start("sum z", last - 1), start("sum sides", last)]
     if parts > 1:
         places.append(start("sum corner", names[0]))
     grad_tokens, gain_one_part = row_call(
-        leave_kernel, flip, [grad_normed, tokens_low, grad_hidden, gain_one], [F32], 1
+        leave_kernel, flip, [grad_normed, tokens_low, grad_mix, gain_one], [F32], 1
     )
     item = sums[names[-1]]
     grad_tokens, gain_one_part, item["keep"] = close(

time: 543 us -> 533 us (0.982)
  local copies, waits for them, and re-layouts: 41.5 us -> 29 us
  Pallas kernels: 279 us -> 285 us
    slice x10 -> x0, local copies, waits for them, and re-layouts: 13.3 us -> none  [gather_corner(): return (self.swap(from_x[:half], y=1), self.swap(from_y[half:], x=1))]
    pallas_call x0 -> x5, Pallas kernels: none -> 12.7 us  [cut(): pl.pallas_call(cut_kernel, grid=(columns // 128,), in_specs=[low, high],...]
    pallas_call x4, Pallas kernels: 135 us -> 129 us  [ffn_piece(): pl.pallas_call(functools.partial(ffn_kernel, first, last, len(ties)), gri...]
    unnamed x112 -> x120, local copies, waits for them, and re-layouts: 16.4 us -> 17.1 us
  transfers between devices with their start and end apart: 69 -> 69, of which waited for: 17 -> 18; matrix products, arithmetic and copies ran while one was open for 7% -> 4% of each run, Pallas kernels for 51% -> 51%
where the time goes in v4:
time: 533 us; the launch traced here: 525 us
  Pallas kernels  285 us (53%)
  starting transfers between devices  106 us (20%)
  waiting for transfers between devices  85.2 us (16%)
  local copies, waits for them, and re-layouts  29 us (5%)
  other arithmetic  17.5 us (3%)
    pallas_call x4, Pallas kernels, ffn_piece(): pl.pallas_call(functools.partial(ffn_kernel, first, last, len(ties)), gri...  129 us
    ppermute x58, waiting for transfers between devices, swap(): return lax.ppermute(value, AXES, pairs)  66.2 us
    all_to_all x11, starting transfers between devices, turn_z(): lax.all_to_all(value, 'dp', 0, 0, axis_index_groups=groups, tiled=True)  53.6 us
    ppermute x58, starting transfers between devices, swap(): return lax.ppermute(value, AXES, pairs)  52.8 us
    pallas_call x15, Pallas kernels, small_call(): pl.pallas_call(kernel, grid=(columns // 128,), in_specs=[spec(item.shape)...  44.4 us
    pallas_call x2, Pallas kernels, mixer_back(): pl.pallas_call(functools.partial(mixer_back_kernel, first, len(ties), min...  43 us
    pallas_call x4, Pallas kernels, row_call(): pl.pallas_call(body, grid=(rows // height,), in_specs=[scalar] + specs +...  30.2 us
    pallas_call x1, Pallas kernels, mixer_part(): pl.pallas_call(functools.partial(mixer_kernel, first, last, len(ties), mi...  25.1 us
  transfers between devices with their start and end apart: 69, of which 18 were waited for; matrix products, arithmetic and copies ran while one was open for 4% of the time, Pallas kernels for 51%

profile of v4, /device:TPU:0, one launch (start us, length us, event | category | flops | bytes accessed | tf_op | source)
XLA Modules:
  0.0 524.7 jit_solution(10278555262508930652)
XLA Ops:
  3.8 6.4 %all-to-all-start = ((bf16[4,4,64,512]{3,2,1,0:T(8,128)(2,1)}), bf16[4,4,64,512]{3,2,1,0:T(8,128)(2,1)S(1)}, u32[]{:S(2)}, u32[]{:S(2)}) async-start(bf16[4,4,64,512]{3,2,1,0:T(8,128)(2,1)} %broadcast_in_dim.65.refs_2_), calls=%async_computation | async-start | bytes 2097152 | tf_op jit(solution)/shard_map/all_to_all | solution.py:49
  18.6 8.5 %shard_map.186 = (bf16[1024,1024]{1,0:T(8,128)(2,1)}, bf16[1024,1024]{1,0:T(8,128)(2,1)}, bf16[1024,1024]{1,0:T(8,128)(2,1)}, bf16[1024,1024]{1,0:T(8,128)(2,1)}) custom-call(s32[1]{0:T(128)} %bitcast.refs_0_, s32[1]{0:T(128)} %dynamic_slice.9.refs_1_.refs_0_, bf16[1024,1024]{1,0:T(8,128)(2,1)} %refs_2_.1, bf16[1024,1024]{1,0:T(8,128)(2,1)} %refs_3_.1, ...), custom_call_target="tpu_custom_call" | custom-call | flops 20971520 | bytes 12582912 | tf_op jit(solution)/shard_map/pallas_call | solution.py:627
  27.1 8.8 %all-to-all-done.refs_7_ = bf16[4,4,64,512]{3,2,1,0:T(8,128)(2,1)S(1)} async-done(((bf16[4,4,64,512]{3,2,1,0:T(8,128)(2,1)}), bf16[4,4,64,512]{3,2,1,0:T(8,128)(2,1)S(1)}, u32[]{:S(2)}, u32[]{:S(2)}) %all-to-all-start) | async-done | bytes 1048608 | tf_op jit(solution)/shard_map/all_to_all | solution.py:49
  43.6 21.3 %collective-permute-done.1.refs_2_ = bf16[4,4,64,512]{3,2,1,0:T(8,128)(2,1)S(1)} collective-permute-done((bf16[4,4,64,512]{3,2,1,0:T(8,128)(2,1)}, bf16[4,4,64,512]{3,2,1,0:T(8,128)(2,1)S(1)}, u32[]{:S(2)}, u32[]{:S(2)}) %collective-permute-start.1) | collective-permute-done | bytes 1048608 | tf_op jit(solution)/shard_map/ppermute | solution.py:45
  67.3 4.7 all-to-all-start.2
  77.6 9.3 %collective-permute-done.3.refs_2_ = bf16[2,4,64,512]{3,2,1,0:T(8,128)(2,1)S(1)} collective-permute-done((bf16[2,4,64,512]{3,2,1,0:T(8,128)(2,1)}, bf16[2,4,64,512]{3,2,1,0:T(8,128)(2,1)S(1)}, u32[]{:S(2)}, u32[]{:S(2)}) %collective-permute-start.3) | collective-permute-done | bytes 524320 | tf_op jit(solution)/shard_map/ppermute | solution.py:45
  90.0 4.8 shard_map.191.refs_5_
  100.2 3.5 all-to-all-start.3
  104.3 25.1 %shard_map.192 = (f32[3,1024,1024]{2,1,0:T(8,128)}, f32[1024,1024]{1,0:T(8,128)}, bf16[1024,1024]{1,0:T(8,128)(2,1)}, bf16[1024,1024]{1,0:T(8,128)(2,1)}) custom-call(s32[1]{0:T(128)} %dynamic_slice.9.refs_1_.refs_0_, bf16[1024,1024]{1,0:T(8,128)(2,1)} %get-tuple-element.230.refs_1_, bf16[1024,1024]{1,0:T(8,128)(2,1)} %get-tuple-element.231.refs_2_, ...), custom_call_target="tpu_custom_call" | custom-call | flops 34359738368 | bytes 29360128 | tf_op jit(solution)/shard_map/pallas_call | solution.py:455
  129.5 3.6 collective-permute-done.8.refs_5_
  140.3 4.6 all-to-all-start.4
  152.8 27.7 %shard_map.195 = (bf16[2,2,2,3,64,256]{5,4,3,2,1,0:T(8,128)(2,1)}, bf16[2,2,2,3,64,256]{5,4,3,2,1,0:T(8,128)(2,1)}, bf16[2,2,3,64,256]{4,3,2,1,0:T(8,128)(2,1)},...) custom-call(bf16[1024,1024]{1,0:T(8,128)(2,1)} %get-tuple-element.25, ...), custom_call_target="tpu_custom_call" | custom-call | flops 77309411328 | bytes 48234496 | tf_op jit(solution)/shard_map/pallas_call | solution.py:327
  191.8 29.6 %shard_map.198 = (bf16[2,2,2,3,64,256]{5,4,3,2,1,0:T(8,128)(2,1)}, bf16[2,2,2,3,64,256]{5,4,3,2,1,0:T(8,128)(2,1)}, bf16[2,2,3,64,256]{4,3,2,1,0:T(8,128)(2,1)},...) custom-call(bf16[1024,1024]{1,0:T(8,128)(2,1)} %get-tuple-element.25, ...), custom_call_target="tpu_custom_call" | custom-call | flops 77309411328 | bytes 48234496 | tf_op jit(solution)/shard_map/pallas_call | solution.py:327
  229.0 42.3 %shard_map.201 = (bf16[2,2,2,3,64,384]{5,4,3,2,1,0:T(8,128)(2,1)}, bf16[2,2,2,3,64,384]{5,4,3,2,1,0:T(8,128)(2,1)}, bf16[2,2,3,64,384]{4,3,2,1,0:T(8,128)(2,1)},...) custom-call(bf16[1024,1024]{1,0:T(8,128)(2,1)} %get-tuple-element.25, ...), custom_call_target="tpu_custom_call" | custom-call | flops 115964116992 | bytes 51380224 | tf_op jit(solution)/shard_map/pallas_call | solution.py:327
  279.4 29.7 %shard_map.204 = (bf16[2,2,2,3,64,256]{5,4,3,2,1,0:T(8,128)(2,1)}, bf16[2,2,2,3,64,256]{5,4,3,2,1,0:T(8,128)(2,1)}, bf16[2,2,3,64,256]{4,3,2,1,0:T(8,128)(2,1)},...) custom-call(bf16[1024,1024]{1,0:T(8,128)(2,1)} %get-tuple-element.25, ...), custom_call_target="tpu_custom_call" | custom-call | flops 77309411328 | bytes 48234496 | tf_op jit(solution)/shard_map/pallas_call | solution.py:327
  317.5 4.6 all-to-all-start.5
  324.7 7.5 %shard_map.207 = (bf16[1024,1024]{1,0:T(8,128)(2,1)}, f32[8,1024]{1,0:T(8,128)}) custom-call(s32[1]{0:T(128)} %bitcast.refs_0_, f32[1024,1024]{1,0:T(8,128)} %get-tuple-element.345.refs_1_, bf16[1024,1024]{1,0:T(8,128)(2,1)} %collective-permute-done.30.refs_2_, f32[1024,1024]{1,0:T(8,128)} %get-tuple-element.245.refs_3_.refs_1_, ...), custom_call_target="tpu_custom_call" | custom-call | flops 20971520 | bytes 12582912 | tf_op jit(solution)/shard_map/pallas_call | solution.py:627
  332.2 20.9 %shard_map.208 = (bf16[4,4,4,64,256]{4,3,2,1,0:T(8,128)(2,1)}, bf16[4,4,4,64,256]{4,3,2,1,0:T(8,128)(2,1)}, f32[8,512]{1,0:T(8,128)}, f32[1024,1024]{1,0:T(8,128)}) custom-call(s32[1]{0:T(128)} %dynamic_slice.9.refs_1_.refs_0_, bf16[1024,1024]{1,0:T(8,128)(2,1)} %get-tuple-element.230.refs_1_, bf16[1024,1024]{1,0:T(8,128)(2,1)} %get-tuple-element.347.refs_2_.refs_3_, ...), custom_call_target="tpu_custom_call" | custom-call | flops 34359738368 | bytes 23068672 | tf_op jit(solution)/shard_map/pallas_call | solution.py:562
  355.0 3.7 shard_map.214
  363.1 5.3 %all-to-all-start.6 = ((bf16[4,2,3,64,256]{4,3,2,1,0:T(8,128)(2,1)}), bf16[4,2,3,64,256]{4,3,2,1,0:T(8,128)(2,1)S(1)}, u32[]{:S(2)}, u32[]{:S(2)}) async-start(bf16[4,2,3,64,256]{4,3,2,1,0:T(8,128)(2,1)} %shard_map.213), calls=%async_computation.6 | async-start | bytes 1572864 | tf_op jit(solution)/shard_map/all_to_all | solution.py:49
  371.0 22.1 %shard_map.212 = (bf16[4,4,4,64,256]{4,3,2,1,0:T(8,128)(2,1)}, bf16[4,4,4,64,256]{4,3,2,1,0:T(8,128)(2,1)}, f32[8,512]{1,0:T(8,128)}, f32[1024,1024]{1,0:T(8,128)}) custom-call(s32[1]{0:T(128)} %dynamic_slice.9.refs_1_.refs_0_, bf16[1024,1024]{1,0:T(8,128)(2,1)} %get-tuple-element.230.refs_1_, ...), custom_call_target="tpu_custom_call", output_to_operand_aliasing={{3}: (7, {})} | custom-call | flops 34359738368 | bytes 23068672 | tf_op jit(solution)/shard_map/pallas_call | solution.py:562
  394.8 4.2 shard_map.218
  399.0 5.5 %all-to-all-start.7 = ((bf16[4,2,3,64,384]{4,3,2,1,0:T(8,128)(2,1)}), bf16[4,2,3,64,384]{4,3,2,1,0:T(8,128)(2,1)S(1)}, u32[]{:S(2)}, u32[]{:S(2)}) async-start(bf16[4,2,3,64,384]{4,3,2,1,0:T(8,128)(2,1)} %shard_map.218), calls=%async_computation.7 | async-start | bytes 2359296 | tf_op jit(solution)/shard_map/all_to_all | solution.py:49
  413.4 6.2 %collective-permute-done.42.refs_5_ = bf16[2,2,3,64,256]{4,3,2,1,0:T(8,128)(2,1)} collective-permute-done((bf16[2,2,3,64,256]{4,3,2,1,0:T(8,128)(2,1)}, bf16[2,2,3,64,256]{4,3,2,1,0:T(8,128)(2,1)}, u32[]{:S(2)}, u32[]{:S(2)}) %collective-permute-start.42) | collective-permute-done | bytes 393248 | tf_op jit(solution)/shard_map/ppermute | solution.py:45
  422.3 7.5 %shard_map.217 = (f32[1024,1024]{1,0:T(8,128)}, f32[8,1024]{1,0:T(8,128)}) custom-call(s32[1]{0:T(128)} %bitcast.refs_0_, f32[1024,1024]{1,0:T(8,128)} %get-tuple-element.389.refs_1_, bf16[1024,1024]{1,0:T(8,128)(2,1)} %get-tuple-element.231.refs_2_, bf16[1024,1024]{1,0:T(8,128)(2,1)} %get-tuple-element.347.refs_2_.refs_3_, f32[1,1024]{1,0:T(1,128)} %reshape.202.refs_4_), custom_call_target="tpu_custom_call" | custom-call | flops 20971520 | bytes 12582912 | tf_op jit(solution)/shard_map/pallas_call | solution.py:627
  429.8 5.2 collective-permute-done.43.refs_6_
  438.8 5.1 all-to-all-start.8
  458.0 6.5 %shard_map.216.refs_0_ = bf16[1024,1024]{1,0:T(8,128)(2,1)} custom-call(s32[1]{0:T(128)} %bitcast.refs_0_, f32[1024,1024]{1,0:T(8,128)} %get-tuple-element.245.refs_3_.refs_1_, f32[1024,1024]{1,0:T(8,128)} %get-tuple-element.387.refs_2_, bf16[1024,1024]{1,0:T(8,128)(2,1)} %collective-permute-done.40.refs_3_), custom_call_target="tpu_custom_call" | custom-call | flops 20971520 | bytes 12582912 | tf_op jit(solution)/shard_map/pallas_call | solution.py:627
  473.0 4.8 all-to-all-start.9
  484.8 7.1 %collective-permute-done.52 = f32[5,1024]{1,0:T(8,128)S(1)} collective-permute-done((f32[5,1024]{1,0:T(8,128)S(1)}, f32[5,1024]{1,0:T(8,128)S(1)}, u32[]{:S(2)}, u32[]{:S(2)}) %collective-permute-start.52) | collective-permute-done | bytes 20512 | tf_op jit(solution)/shard_map/ppermute | solution.py:45
  505.2 5.4 %all-to-all-start.10 = ((bf16[4,4,64,256]{3,2,1,0:T(8,128)(2,1)}), bf16[4,4,64,256]{3,2,1,0:T(8,128)(2,1)S(1)}, u32[]{:S(2)}, u32[]{:S(2)}) async-start(bf16[4,4,64,256]{3,2,1,0:T(8,128)(2,1)} %shard_map.229), calls=%async_computation.10 | async-start | bytes 1048576 | tf_op jit(solution)/shard_map/all_to_all | solution.py:49
  514.5 8.2 %all-to-all-done.10 = bf16[4,4,64,256]{3,2,1,0:T(8,128)(2,1)S(1)} async-done(((bf16[4,4,64,256]{3,2,1,0:T(8,128)(2,1)}), bf16[4,4,64,256]{3,2,1,0:T(8,128)(2,1)S(1)}, u32[]{:S(2)}, u32[]{:S(2)}) %all-to-all-start.10) | async-done | bytes 524320 | tf_op jit(solution)/shard_map/all_to_all | solution.py:49
  (336 shorter events, 162.6 us)
Async XLA Ops:
  3.8 32.2 %all-to-all-start = ((bf16[4,4,64,512]{3,2,1,0:T(8,128)(2,1)}), bf16[4,4,64,512]{3,2,1,0:T(8,128)(2,1)S(1)}, u32[]{:S(2)}, u32[]{:S(2)}) async-start(bf16[4,4,64,512]{3,2,1,0:T(8,128)(2,1)} %broadcast_in_dim.65.refs_2_), calls=%async_computation | async-start | bytes 2097152 | tf_op jit(solution)/shard_map/all_to_all | solution.py:49
  96.1 50.9 %collective-permute-start.11 = (bf16[1024,1024]{1,0:T(8,128)(2,1)}, bf16[1024,1024]{1,0:T(8,128)(2,1)}, u32[]{:S(2)}, u32[]{:S(2)}) collective-permute-start(bf16[1024,1024]{1,0:T(8,128)(2,1)} %get-tuple-element.255), channel_id=1, source_target_pairs={{0,2},{1,3},{2,0},{3,1},{4,6},{5,7},{6,4},{7,5},{8,10},{9,11},{10,... | collective-permute-start | bytes 6291464 | tf_op jit(solution)/shard_map/ppermute | solution.py:45
  96.6 32.8 %collective-permute-start.6 = (bf16[4,2,3,64,256]{4,3,2,1,0:T(8,128)(2,1)S(1)}, bf16[4,2,3,64,256]{4,3,2,1,0:T(8,128)(2,1)S(1)}, u32[]{:S(2)}, u32[]{:S(2)}) collective-permute-start(bf16[4,2,3,64,256]{4,3,2,1,0:T(8,128)(2,1)S(1)} %copy-done.16), channel_id=1, source_target_pairs={{0,4},{1,5},{2,6},{3,7},{4,0},{5,1},{6,2},{7,3},{8,12},{9,13},{10,... | collective-permute-start | bytes 2359304 | tf_op jit(solution)/shard_map/ppermute | solution.py:45
  97.5 31.9 %collective-permute-start.7 = (bf16[4,2,3,64,256]{4,3,2,1,0:T(8,128)(2,1)S(1)}, bf16[4,2,3,64,256]{4,3,2,1,0:T(8,128)(2,1)}, u32[]{:S(2)}, u32[]{:S(2)}) collective-permute-start(bf16[4,2,3,64,256]{4,3,2,1,0:T(8,128)(2,1)S(1)} %copy-done.16), channel_id=1, source_target_pairs={{0,1},{1,0},{2,3},{3,2},{4,5},{5,4},{6,7},{7,6},{8,9},{9,8},{10,11... | collective-permute-start | bytes 2359304 | tf_op jit(solution)/shard_map/ppermute | solution.py:45
  99.0 34.0 %collective-permute-start.8 = (bf16[4,2,3,64,256]{4,3,2,1,0:T(8,128)(2,1)}, bf16[4,2,3,64,256]{4,3,2,1,0:T(8,128)(2,1)}, u32[]{:S(2)}, u32[]{:S(2)}) collective-permute-start(bf16[4,2,3,64,256]{4,3,2,1,0:T(8,128)(2,1)} %get-tuple-element.250.refs_4_), channel_id=1, source_target_pairs={{0,4},{1,5},{2,6},{3,7},{4,0},{5,1},{6,2},{7,3},{8,12},{9,13},{10,... | collective-permute-start | bytes 2359304 | tf_op jit(solution)/shard_map/ppermute | solution.py:45
  100.2 33.5 %all-to-all-start.3 = ((bf16[4,2,3,64,384]{4,3,2,1,0:T(8,128)(2,1)}), bf16[4,2,3,64,384]{4,3,2,1,0:T(8,128)(2,1)S(1)}, u32[]{:S(2)}, u32[]{:S(2)}) async-start(bf16[4,2,3,64,384]{4,3,2,1,0:T(8,128)(2,1)} %get-tuple-element.251), calls=%async_computation.3 | async-start | bytes 2359296 | tf_op jit(solution)/shard_map/all_to_all | solution.py:49
  139.4 44.0 %collective-permute-start.16 = (bf16[4,2,3,64,384]{4,3,2,1,0:T(8,128)(2,1)}, bf16[4,2,3,64,384]{4,3,2,1,0:T(8,128)(2,1)S(1)}, u32[]{:S(2)}, u32[]{:S(2)}) collective-permute-start(bf16[4,2,3,64,384]{4,3,2,1,0:T(8,128)(2,1)} %get-tuple-element.273.refs_4_), channel_id=1, source_target_pairs={{0,4},{1,5},{2,6},{3,7},{4,0},{5,1},{6,2},{7,3},{8,12},{9,13},{10,... | collective-permute-start | bytes 3538952 | tf_op jit(solution)/shard_map/ppermute | solution.py:45
  140.3 43.1 %all-to-all-start.4 = ((bf16[4,2,3,64,256]{4,3,2,1,0:T(8,128)(2,1)}), bf16[4,2,3,64,256]{4,3,2,1,0:T(8,128)(2,1)}, u32[]{:S(2)}, u32[]{:S(2)}) async-start(bf16[4,2,3,64,256]{4,3,2,1,0:T(8,128)(2,1)} %get-tuple-element.274), calls=%async_computation.4 | async-start | bytes 1572864 | tf_op jit(solution)/shard_map/all_to_all | solution.py:49
  147.0 36.5 %collective-permute-start.17 = (bf16[4,2,3,64,384]{4,3,2,1,0:T(8,128)(2,1)S(1)}, bf16[4,2,3,64,384]{4,3,2,1,0:T(8,128)(2,1)}, u32[]{:S(2)}, u32[]{:S(2)}) collective-permute-start(bf16[4,2,3,64,384]{4,3,2,1,0:T(8,128)(2,1)S(1)} %copy-done.18), channel_id=1, source_target_pairs={{0,1},{1,0},{2,3},{3,2},{4,5},{5,4},{6,7},{7,6},{8,9},{9,8},{10,11... | collective-permute-start | bytes 3538952 | tf_op jit(solution)/shard_map/ppermute | solution.py:45
  149.2 33.8 %collective-permute-start.14 = (bf16[2,2,3,64,256]{4,3,2,1,0:T(8,128)(2,1)}, bf16[2,2,3,64,256]{4,3,2,1,0:T(8,128)(2,1)S(1)}, u32[]{:S(2)}, u32[]{:S(2)}) collective-permute-start(bf16[2,2,3,64,256]{4,3,2,1,0:T(8,128)(2,1)} %get-tuple-element.271), channel_id=1, source_target_pairs={{0,1},{1,0},{2,3},{3,2},{4,5},{5,4},{6,7},{7,6},{8,9},{9,8},{10,11... | collective-permute-start | bytes 1179656 | tf_op jit(solution)/shard_map/ppermute | solution.py:45
  151.7 31.8 %collective-permute-start.15 = (bf16[2,2,3,64,256]{4,3,2,1,0:T(8,128)(2,1)}, bf16[2,2,3,64,256]{4,3,2,1,0:T(8,128)(2,1)S(1)}, u32[]{:S(2)}, u32[]{:S(2)}) collective-permute-start(bf16[2,2,3,64,256]{4,3,2,1,0:T(8,128)(2,1)} %get-tuple-element.272), channel_id=1, source_target_pairs={{0,4},{1,5},{2,6},{3,7},{4,0},{5,1},{6,2},{7,3},{8,12},{9,13},{10,... | collective-permute-start | bytes 1179656 | tf_op jit(solution)/shard_map/ppermute | solution.py:45
  184.6 36.9 %collective-permute-start.20 = (bf16[4,2,3,64,256]{4,3,2,1,0:T(8,128)(2,1)}, bf16[4,2,3,64,256]{4,3,2,1,0:T(8,128)(2,1)S(1)}, u32[]{:S(2)}, u32[]{:S(2)}) collective-permute-start(bf16[4,2,3,64,256]{4,3,2,1,0:T(8,128)(2,1)} %get-tuple-element.275.refs_4_), channel_id=1, source_target_pairs={{0,4},{1,5},{2,6},{3,7},{4,0},{5,1},{6,2},{7,3},{8,12},{9,13},{10,... | collective-permute-start | bytes 2359304 | tf_op jit(solution)/shard_map/ppermute | solution.py:45
  185.7 35.7 %collective-permute-start.21 = (bf16[4,2,3,64,256]{4,3,2,1,0:T(8,128)(2,1)}, bf16[4,2,3,64,256]{4,3,2,1,0:T(8,128)(2,1)S(1)}, u32[]{:S(2)}, u32[]{:S(2)}) collective-permute-start(bf16[4,2,3,64,256]{4,3,2,1,0:T(8,128)(2,1)} %get-tuple-element.275.refs_4_), channel_id=1, source_target_pairs={{0,1},{1,0},{2,3},{3,2},{4,5},{5,4},{6,7},{7,6},{8,9},{9,8},{10,11... | collective-permute-start | bytes 2359304 | tf_op jit(solution)/shard_map/ppermute | solution.py:45
  189.4 32.0 %collective-permute-start.18 = (bf16[2,2,3,64,384]{4,3,2,1,0:T(8,128)(2,1)}, bf16[2,2,3,64,384]{4,3,2,1,0:T(8,128)(2,1)S(1)}, u32[]{:S(2)}, u32[]{:S(2)}) collective-permute-start(bf16[2,2,3,64,384]{4,3,2,1,0:T(8,128)(2,1)} %get-tuple-element.295), channel_id=1, source_target_pairs={{0,1},{1,0},{2,3},{3,2},{4,5},{5,4},{6,7},{7,6},{8,9},{9,8},{10,11... | collective-permute-start | bytes 1769480 | tf_op jit(solution)/shard_map/ppermute | solution.py:45
  225.0 46.3 %collective-permute-start.22 = (bf16[2,2,3,64,256]{4,3,2,1,0:T(8,128)(2,1)}, bf16[2,2,3,64,256]{4,3,2,1,0:T(8,128)(2,1)S(1)}, u32[]{:S(2)}, u32[]{:S(2)}) collective-permute-start(bf16[2,2,3,64,256]{4,3,2,1,0:T(8,128)(2,1)} %get-tuple-element.316), channel_id=1, source_target_pairs={{0,1},{1,0},{2,3},{3,2},{4,5},{5,4},{6,7},{7,6},{8,9},{9,8},{10,11... | collective-permute-start | bytes 1179656 | tf_op jit(solution)/shard_map/ppermute | solution.py:45
  225.5 45.8 %collective-permute-start.23 = (bf16[2,2,3,64,256]{4,3,2,1,0:T(8,128)(2,1)}, bf16[2,2,3,64,256]{4,3,2,1,0:T(8,128)(2,1)S(1)}, u32[]{:S(2)}, u32[]{:S(2)}) collective-permute-start(bf16[2,2,3,64,256]{4,3,2,1,0:T(8,128)(2,1)} %get-tuple-element.317), channel_id=1, source_target_pairs={{0,4},{1,5},{2,6},{3,7},{4,0},{5,1},{6,2},{7,3},{8,12},{9,13},{10,... | collective-permute-start | bytes 1179656 | tf_op jit(solution)/shard_map/ppermute | solution.py:45
  226.6 44.7 %collective-permute-start.24 = (bf16[2,2,2,3,64,256]{5,4,3,2,1,0:T(8,128)(2,1)}, bf16[2,2,2,3,64,256]{5,4,3,2,1,0:T(8,128)(2,1)S(1)}, u32[]{:S(2)}, u32[]{:S(2)}) collective-permute-start(bf16[2,2,2,3,64,256]{5,4,3,2,1,0:T(8,128)(2,1)} %get-tuple-element.318), channel_id=1, source_target_pairs={{0,4},{1,5},{2,6},{3,7},{4,0},{5,1},{6,2},{7,3},{8,12},{9,13},{10,... | collective-permute-start | bytes 2359304 | tf_op jit(solution)/shard_map/ppermute | solution.py:45
  227.5 43.9 %collective-permute-start.25 = (bf16[2,2,2,3,64,256]{5,4,3,2,1,0:T(8,128)(2,1)}, bf16[2,2,2,3,64,256]{5,4,3,2,1,0:T(8,128)(2,1)S(1)}, u32[]{:S(2)}, u32[]{:S(2)}) collective-permute-start(bf16[2,2,2,3,64,256]{5,4,3,2,1,0:T(8,128)(2,1)} %get-tuple-element.319), channel_id=1, source_target_pairs={{0,1},{1,0},{2,3},{3,2},{4,5},{5,4},{6,7},{7,6},{8,9},{9,8},{10,11... | collective-permute-start | bytes 2359304 | tf_op jit(solution)/shard_map/ppermute | solution.py:45
  275.3 33.8 %collective-permute-start.26 = (bf16[2,2,3,64,256]{4,3,2,1,0:T(8,128)(2,1)}, bf16[2,2,3,64,256]{4,3,2,1,0:T(8,128)(2,1)S(1)}, u32[]{:S(2)}, u32[]{:S(2)}) collective-permute-start(bf16[2,2,3,64,256]{4,3,2,1,0:T(8,128)(2,1)} %get-tuple-element.341), channel_id=1, source_target_pairs={{0,4},{1,5},{2,6},{3,7},{4,0},{5,1},{6,2},{7,3},{8,12},{9,13},{10,... | collective-permute-start | bytes 1179656 | tf_op jit(solution)/shard_map/ppermute | solution.py:45
  276.5 32.7 %collective-permute-start.27 = (bf16[2,2,3,64,256]{4,3,2,1,0:T(8,128)(2,1)}, bf16[2,2,3,64,256]{4,3,2,1,0:T(8,128)(2,1)S(1)}, u32[]{:S(2)}, u32[]{:S(2)}) collective-permute-start(bf16[2,2,3,64,256]{4,3,2,1,0:T(8,128)(2,1)} %get-tuple-element.342), channel_id=1, source_target_pairs={{0,1},{1,0},{2,3},{3,2},{4,5},{5,4},{6,7},{7,6},{8,9},{9,8},{10,11... | collective-permute-start | bytes 1179656 | tf_op jit(solution)/shard_map/ppermute | solution.py:45
  277.0 32.2 %collective-permute-start.28 = (bf16[2,2,2,3,64,256]{5,4,3,2,1,0:T(8,128)(2,1)S(1)}, bf16[2,2,2,3,64,256]{5,4,3,2,1,0:T(8,128)(2,1)S(1)}, u32[]{:S(2)}, u32[]{:S(2)}) collective-permute-start(bf16[2,2,2,3,64,256]{5,4,3,2,1,0:T(8,128)(2,1)S(1)} %copy-done.22), channel_id=1, source_target_pairs={{0,4},{1,5},{2,6},{3,7},{4,0},{5,1},{6,2},{7,3},{8,12},{9,13},{10,... | collective-permute-start | bytes 2359304 | tf_op jit(solution)/shard_map/ppermute | solution.py:45
  277.9 31.3 %collective-permute-start.29 = (bf16[2,2,2,3,64,256]{5,4,3,2,1,0:T(8,128)(2,1)S(1)}, bf16[2,2,2,3,64,256]{5,4,3,2,1,0:T(8,128)(2,1)S(1)}, u32[]{:S(2)}, u32[]{:S(2)}) collective-permute-start(bf16[2,2,2,3,64,256]{5,4,3,2,1,0:T(8,128)(2,1)S(1)} %copy-done.23), channel_id=1, source_target_pairs={{0,1},{1,0},{2,3},{3,2},{4,5},{5,4},{6,7},{7,6},{8,9},{9,8},{10,11... | collective-permute-start | bytes 2359304 | tf_op jit(solution)/shard_map/ppermute | solution.py:45
  313.1 40.0 %collective-permute-start.31 = (bf16[2,2,3,64,256]{4,3,2,1,0:T(8,128)(2,1)}, bf16[2,2,3,64,256]{4,3,2,1,0:T(8,128)(2,1)S(1)}, u32[]{:S(2)}, u32[]{:S(2)}) collective-permute-start(bf16[2,2,3,64,256]{4,3,2,1,0:T(8,128)(2,1)} %get-tuple-element.364), channel_id=1, source_target_pairs={{0,4},{1,5},{2,6},{3,7},{4,0},{5,1},{6,2},{7,3},{8,12},{9,13},{10,... | collective-permute-start | bytes 1179656 | tf_op jit(solution)/shard_map/ppermute | solution.py:45
  314.2 38.9 %collective-permute-start.32 = (bf16[2,2,3,64,256]{4,3,2,1,0:T(8,128)(2,1)}, bf16[2,2,3,64,256]{4,3,2,1,0:T(8,128)(2,1)}, u32[]{:S(2)}, u32[]{:S(2)}) collective-permute-start(bf16[2,2,3,64,256]{4,3,2,1,0:T(8,128)(2,1)} %get-tuple-element.365), channel_id=1, source_target_pairs={{0,1},{1,0},{2,3},{3,2},{4,5},{5,4},{6,7},{7,6},{8,9},{9,8},{10,11... | collective-permute-start | bytes 1179656 | tf_op jit(solution)/shard_map/ppermute | solution.py:45
  317.5 35.6 %all-to-all-start.5 = ((bf16[4,2,3,64,256]{4,3,2,1,0:T(8,128)(2,1)}), bf16[4,2,3,64,256]{4,3,2,1,0:T(8,128)(2,1)S(1)}, u32[]{:S(2)}, u32[]{:S(2)}) async-start(bf16[4,2,3,64,256]{4,3,2,1,0:T(8,128)(2,1)} %shard_map.209), calls=%async_computation.5 | async-start | bytes 1572864 | tf_op jit(solution)/shard_map/all_to_all | solution.py:49
  322.2 31.0 %collective-permute-start.33 = (bf16[2,2,2,3,64,384]{5,4,3,2,1,0:T(8,128)(2,1)}, bf16[2,2,2,3,64,384]{5,4,3,2,1,0:T(8,128)(2,1)S(1)}, u32[]{:S(2)}, u32[]{:S(2)}) collective-permute-start(bf16[2,2,2,3,64,384]{5,4,3,2,1,0:T(8,128)(2,1)} %get-tuple-element.366), channel_id=1, source_target_pairs={{0,4},{1,5},{2,6},{3,7},{4,0},{5,1},{6,2},{7,3},{8,12},{9,13},{10,... | collective-permute-start | bytes 3538952 | tf_op jit(solution)/shard_map/ppermute | solution.py:45
  358.7 34.3 %collective-permute-start.36 = (bf16[2,2,3,64,384]{4,3,2,1,0:T(8,128)(2,1)}, bf16[2,2,3,64,384]{4,3,2,1,0:T(8,128)(2,1)S(1)}, u32[]{:S(2)}, u32[]{:S(2)}) collective-permute-start(bf16[2,2,3,64,384]{4,3,2,1,0:T(8,128)(2,1)} %get-tuple-element.383), channel_id=1, source_target_pairs={{0,4},{1,5},{2,6},{3,7},{4,0},{5,1},{6,2},{7,3},{8,12},{9,13},{10,... | collective-permute-start | bytes 1769480 | tf_op jit(solution)/shard_map/ppermute | solution.py:45
  359.9 33.2 %collective-permute-start.37 = (bf16[2,2,3,64,384]{4,3,2,1,0:T(8,128)(2,1)}, bf16[2,2,3,64,384]{4,3,2,1,0:T(8,128)(2,1)}, u32[]{:S(2)}, u32[]{:S(2)}) collective-permute-start(bf16[2,2,3,64,384]{4,3,2,1,0:T(8,128)(2,1)} %get-tuple-element.384), channel_id=1, source_target_pairs={{0,1},{1,0},{2,3},{3,2},{4,5},{5,4},{6,7},{7,6},{8,9},{9,8},{10,11... | collective-permute-start | bytes 1769480 | tf_op jit(solution)/shard_map/ppermute | solution.py:45
  394.8 40.2 %collective-permute-start.41 = (bf16[4,4,4,64,256]{4,3,2,1,0:T(8,128)(2,1)}, bf16[4,4,4,64,256]{4,3,2,1,0:T(8,128)(2,1)}, u32[]{:S(2)}, u32[]{:S(2)}) collective-permute-start(bf16[4,4,4,64,256]{4,3,2,1,0:T(8,128)(2,1)} %get-tuple-element.393), channel_id=1, source_target_pairs={{0,2},{1,3},{2,0},{3,1},{4,6},{5,7},{6,4},{7,5},{8,10},{9,11},{10,... | collective-permute-start | bytes 6291464 | tf_op jit(solution)/shard_map/ppermute | solution.py:45
  399.0 36.0 %all-to-all-start.7 = ((bf16[4,2,3,64,384]{4,3,2,1,0:T(8,128)(2,1)}), bf16[4,2,3,64,384]{4,3,2,1,0:T(8,128)(2,1)S(1)}, u32[]{:S(2)}, u32[]{:S(2)}) async-start(bf16[4,2,3,64,384]{4,3,2,1,0:T(8,128)(2,1)} %shard_map.218), calls=%async_computation.7 | async-start | bytes 2359296 | tf_op jit(solution)/shard_map/all_to_all | solution.py:49
  404.5 52.0 %collective-permute-start.40 = (bf16[1024,1024]{1,0:T(8,128)(2,1)S(1)}, bf16[1024,1024]{1,0:T(8,128)(2,1)}, u32[]{:S(2)}, u32[]{:S(2)}) collective-permute-start(bf16[1024,1024]{1,0:T(8,128)(2,1)S(1)} %copy-done), channel_id=1, source_target_pairs={{0,2},{1,3},{2,0},{3,1},{4,6},{5,7},{6,4},{7,5},{8,10},{9,11},{10,... | collective-permute-start | bytes 6291464 | tf_op jit(solution)/shard_map/ppermute | solution.py:45
  480.1 31.9 %collective-permute-start.57 = (f32[3,64,1152]{2,1,0:T(8,128)}, f32[3,64,1152]{2,1,0:T(8,128)}, u32[]{:S(2)}, u32[]{:S(2)}) collective-permute-start(f32[3,64,1152]{2,1,0:T(8,128)} %slice_bitcast_fusion), channel_id=1, source_target_pairs={{0,2},{1,3},{2,0},{3,1},{4,6},{5,7},{6,4},{7,5},{8,10},{9,11},{10,... | collective-permute-start | bytes 2654216 | tf_op jit(solution)/shard_map/ppermute | solution.py:45
  (97 other events, 878.0 us)

commit v5 on v4

--- a/solution.py
+++ b/solution.py
@@ -64,11 +64,8 @@
 
     def sum_rest(self, value):
         value = value + self.swap(value, x=1)
-        step = 1
-        while step < self.zs:
-            value = value + self.swap(value, z=step)
-            step *= 2
-        return value
+        others = [self.swap(value, z=z) for z in range(1, self.zs)]
+        return functools.reduce(jnp.add, others, value)
 
     def absolute(self, place):
         q = lax.axis_index("dp")
@@ -95,24 +92,47 @@
     return pl.CostEstimate(flops=flops, bytes_accessed=moved_bytes, transcendentals=0)
 
 
-def small_call(kernel, inputs, out_shapes, work):
-    columns = inputs[0].shape[-1]
-
-    def spec(shape):
-        lead = len(shape) - 1
+def small_calls(jobs):
+    tiles = [inputs[0].shape[-1] // 128 for _, inputs, _ in jobs]
+
+    def spec(shape, count):
+        zeros = (0,) * (len(shape) - 1)
         return pl.BlockSpec(
-            (*shape[:-1], 128), lambda j: (*(0,) * lead, j)
+            (*shape[:-1], 128), lambda j: (*zeros, jnp.minimum(j, count - 1))
         )
 
-    return pl.pallas_call(
-        kernel,
-        grid=(columns // 128,),
-        in_specs=[spec(item.shape) for item in inputs],
-        out_specs=[spec(shape) for shape in out_shapes],
-        out_shape=[jax.ShapeDtypeStruct(shape, BF) for shape in out_shapes],
+    n_in = [len(inputs) for _, inputs, _ in jobs]
+    n_out = [len(shapes) for _, _, shapes in jobs]
+
+    def body(*refs):
+        ins, outs = list(refs[: sum(n_in)]), list(refs[sum(n_in) :])
+        for (kernel, _, _), count, i, o in zip(jobs, tiles, n_in, n_out):
+            here, ins = ins[:i], ins[i:]
+            there, outs = outs[:o], outs[o:]
+
+            @pl.when(pl.program_id(0) < count)
+            def _():
+                kernel(*here, *there)
+
+    arrays = [item for _, inputs, _ in jobs for item in inputs]
+    out = pl.pallas_call(
+        body,
+        grid=(max(tiles),),
+        in_specs=[
+            spec(item.shape, count) for (_, inputs, _), count in zip(jobs, tiles) for item in inputs
+        ],
+        out_specs=[
+            spec(shape, count) for (_, _, shapes), count in zip(jobs, tiles) for shape in shapes
+        ],
+        out_shape=[jax.ShapeDtypeStruct(shape, BF) for _, _, shapes in jobs for shape in shapes],
         compiler_params=params(),
-        cost_estimate=cost(0, 2 * work),
-    )(*inputs)
+        cost_estimate=cost(0, 4 * sum(item.size for item in arrays)),
+    )(*arrays)
+    result = []
+    for o in n_out:
+        result.append(out[:o])
+        out = out[o:]
+    return result
 
 
 def gate(values):
@@ -164,10 +184,8 @@
 
 
 def join(mine, from_y, from_x, one, two):
-    shape = (4, *mine.shape)
-    return small_call(
-        join_kernel, [mine, from_y, from_x, one, two], [shape], 8 * mine.size
-    )[0]
+    job = (join_kernel, [mine, from_y, from_x, one, two], [(4, *mine.shape)])
+    return small_calls([job])[0][0]
 
 
 def both_kernel(keep, got, send_x, send_y, rest_x, rest_y, own):
@@ -187,7 +205,7 @@
     _, zs, *rest = keep.shape
     part = (zs // 2, *rest)
     shapes = [(2, *part), (2, *part), part, part, (zs, *rest)]
-    return small_call(both_kernel, [keep, got], shapes, 3 * keep.size)
+    return both_kernel, [keep, got], shapes
 
 
 def sides_kernel(rest_x, rest_y, got_x, got_y, send_x, send_y):
@@ -196,12 +214,7 @@
 
 
 def add_sides(rest_x, rest_y, got_x, got_y):
-    return small_call(
-        sides_kernel,
-        [rest_x, rest_y, got_x, got_y],
-        [rest_x.shape] * 2,
-        8 * rest_x.size,
-    )
+    return sides_kernel, [rest_x, rest_y, got_x, got_y], [rest_x.shape] * 2
 
 
 def own_kernel(own, got_x, got_y, side_x, side_y, out):
@@ -213,9 +226,7 @@
 
 
 def add_own(own, got_x, got_y, side_x, side_y):
-    return small_call(
-        own_kernel, [own, got_x, got_y, side_x, side_y], [own.shape], 5 * own.size
-    )[0]
+    return own_kernel, [own, got_x, got_y, side_x, side_y], [own.shape]
 
 
 def ffn_kernel(first, last, ties, *refs):
@@ -763,19 +774,36 @@
         if stage == "sum core":
             item["got"] = links.swap(item["send"], c=1)
             return item, "got"
-        if stage == "sum corner":
-            if "keep" in item:
-                item["parts"] = both_cores(item["keep"], item["got"])
-            send_x, send_y = item["parts"][:2]
-            item["corner"] = links.swap(send_x, x=1), links.swap(send_y, y=1)
-            return item, "corner"
-        rest_x, rest_y, here = item["parts"][2:]
-        if stage == "sum sides":
-            next_x, next_y = add_sides(rest_x, rest_y, *item["corner"])
-            item["sides"] = links.swap(next_x, x=1), links.swap(next_y, y=1)
-            return item, "sides"
-        item["z"] = links.turn_z(add_own(here, *item["corner"], *item["sides"]))
-        return item, "z"
+        raise ValueError(stage)
+
+    def add(*steps):
+        jobs, keys = [], []
+        for stage, p in steps:
+            item = sums[p]
+            if stage == "sum sides":
+                jobs.append(add_sides(*item["parts"][2:4], *item["corner"]))
+                keys.append((item, "next"))
+            elif stage == "sum z":
+                jobs.append(add_own(item["parts"][4], *item["corner"], *item["sides"]))
+                keys.append((item, "total"))
+            elif "keep" in item:
+                jobs.append(both_cores(item["keep"], item["got"]))
+                keys.append((item, "parts"))
+        if jobs:
+            for (item, key), out in zip(keys, small_calls(jobs)):
+                item[key] = out
+        places = []
+        for stage, p in steps:
+            item = sums[p]
+            if stage == "sum z":
+                item["z"] = links.turn_z(item["total"][0])
+                places.append((item, "z"))
+                continue
+            pair = item["next"] if stage == "sum sides" else item["parts"][:2]
+            key = stage[4:]
+            item[key] = links.swap(pair[0], x=1), links.swap(pair[1], y=1)
+            places.append((item, key))
+        return places
 
     def close(kept, places):
         kept, tree = jax.tree.flatten([kept, [store[key] for store, key in places]])
@@ -821,15 +849,15 @@
         for stage, q in (("corner", p + 1), ("sides", p + 2), ("z", p + 3)):
             if q < pieces:
                 places.append(start(stage, q))
-        for stage, q in (("sum z", p - 4), ("sum sides", p - 3), ("sum corner", p - 2)):
-            if q > 0:
-                places.append(start(stage, q))
+        steps = (("sum z", p - 4), ("sum sides", p - 3), ("sum corner", p - 2))
+        places += add(*[step for step in steps if step[1] > 0])
         *parts, t0, t1, t2, t3 = ffn_piece(inputs, cells(p), totals, p == last, [])
         held = sums[p - 1]["parts"][:2] if p > 1 else []
         parts, totals, held = close([parts, [t0, t1, t2, t3], held], places)
         if p > 1:
             sums[p - 1]["parts"][:2] = held
         sums[p] = dict(parts=list(parts))
+    ffn_twin = links.swap(totals[2], c=1)
     grad_mix, gain_two_part = row_call(
         between_kernel,
         flip,
@@ -837,11 +865,7 @@
         [BF],
         1,
     )
-    places = [
-        start("sum z", last - 3),
-        start("sum sides", last - 2),
-        start("sum corner", last - 1),
-    ]
+    places = add(("sum z", last - 3), ("sum sides", last - 2), ("sum corner", last - 1))
     parts = 2 if half % 256 == 0 else 1
     names = [f"mixer {p}" for p in range(parts)]
     grad_normed, taps = None, []
@@ -849,24 +873,24 @@
         if p:
             places = [start("sum core", names[0])]
         if p == parts - 1:
-            later = [start("sum z", last - 2), start("sum sides", last - 1)]
-            later.append(start("sum corner", last))
-            places += later
+            places += add(("sum z", last - 2), ("sum sides", last - 1), ("sum corner", last))
         keep, send, tap_grads, grad_normed = mixer_back(
             own_lengths, normed, grad_mix, project, conv, mixer_cells, grad_normed, [],
             tile, p, parts,
         )
         held = sums[last]["parts"][:2] if p < parts - 1 else []
-        keep, send, tap_grads, grad_normed, totals[0], totals[2], held = close(
-            [keep, send, tap_grads, grad_normed, totals[0], totals[2], held], places
+        keep, send, tap_grads, grad_normed, ffn_twin, held = close(
+            [keep, send, tap_grads, grad_normed, ffn_twin, held], places
         )
         if p < parts - 1:
             sums[last]["parts"][:2] = held
         taps.append(tap_grads)
         sums[name] = dict(keep=keep, send=send)
-    places = [start("sum core", names[-1]), start("sum z", last - 1), start("sum sides", last)]
+    places = [start("sum core", names[-1])]
+    steps = [("sum z", last - 1), ("sum sides", last)]
     if parts > 1:
-        places.append(start("sum corner", names[0]))
+        steps.append(("sum corner", names[0]))
+    places += add(*steps)[1:]
     grad_tokens, gain_one_part = row_call(
         leave_kernel, flip, [grad_normed, tokens_low, grad_mix, gain_one], [F32], 1
     )
@@ -883,18 +907,20 @@
     gains = jnp.take(gains.reshape(2, links.dp, block), place, axis=1).reshape(2, width)
     small = links.sum_chip(jnp.concatenate([gains, taps], axis=0))
 
-    places = [start("sum corner", names[-1]), start("sum z", last)]
+    steps = [("sum corner", names[-1]), ("sum z", last)]
     if parts > 1:
-        places.append(start("sum sides", names[0]))
+        steps.append(("sum sides", names[0]))
+    places = add(*steps)
     result = row_call(
-        result_kernel, flip, [hidden, totals[0], links.swap(totals[2], c=1)], [BF]
+        result_kernel, flip, [hidden, totals[0], ffn_twin], [BF]
     )[0]
     result, small = close([result, small], places)
-    places = [start("sum sides", names[-1])]
+    steps = [("sum sides", names[-1])]
     if parts > 1:
-        places.append(start("sum z", names[0]))
+        steps.append(("sum z", names[0]))
+    places = add(*steps)
     (small,) = close([links.sum_rest(small)], places)
-    start("sum z", names[-1])
+    add(("sum z", names[-1]))
     shard = lambda p: jnp.sum(sums[p]["z"].astype(F32), axis=0)
     mixer_shard = jnp.concatenate([shard(name) for name in names], axis=2)
     ffn_shard = jnp.concatenate([shard(p) for p in range(1, pieces)], axis=3)

time: 533 us -> 523 us (0.981)
  Pallas kernels: 285 us -> 273 us
    pallas_call x15 -> x8, Pallas kernels: 44.4 us -> 33.1 us  [small_calls(): pl.pallas_call(body, grid=(max(tiles),), in_specs=[spec(item.shape, count...]
    ppermute x58 -> x59, starting transfers between devices: 52.8 us -> 56 us  [swap(): return lax.ppermute(value, AXES, pairs)]
    ppermute x58 -> x59, waiting for transfers between devices: 66.2 us -> 67.7 us  [swap(): return lax.ppermute(value, AXES, pairs)]
    unnamed x120 -> x124, local copies, waits for them, and re-layouts: 17.1 us -> 17.3 us
  transfers between devices with their start and end apart: 69 -> 70, of which waited for: 18 -> 21; matrix products, arithmetic and copies ran while one was open for 4% -> 4% of each run, Pallas kernels for 51% -> 50%
where the time goes in v5:
time: 523 us; the launch traced here: 515 us
  Pallas kernels  273 us (52%)
  starting transfers between devices  106 us (20%)
  waiting for transfers between devices  87 us (17%)
  local copies, waits for them, and re-layouts  29.2 us (6%)
  other arithmetic  16.9 us (3%)
    pallas_call x4, Pallas kernels, ffn_piece(): pl.pallas_call(functools.partial(ffn_kernel, first, last, len(ties)), gri...  129 us
    ppermute x59, waiting for transfers between devices, swap(): return lax.ppermute(value, AXES, pairs)  67.7 us
    ppermute x59, starting transfers between devices, swap(): return lax.ppermute(value, AXES, pairs)  56 us
    all_to_all x11, starting transfers between devices, turn_z(): lax.all_to_all(value, 'dp', 0, 0, axis_index_groups=groups, tiled=True)  50.4 us
    pallas_call x2, Pallas kernels, mixer_back(): pl.pallas_call(functools.partial(mixer_back_kernel, first, len(ties), min...  43.1 us
    pallas_call x8, Pallas kernels, small_calls(): pl.pallas_call(body, grid=(max(tiles),), in_specs=[spec(item.shape, count...  33.1 us
    pallas_call x4, Pallas kernels, row_call(): pl.pallas_call(body, grid=(rows // height,), in_specs=[scalar] + specs +...  30 us
    pallas_call x1, Pallas kernels, mixer_part(): pl.pallas_call(functools.partial(mixer_kernel, first, last, len(ties), mi...  25.1 us
  transfers between devices with their start and end apart: 70, of which 21 were waited for; matrix products, arithmetic and copies ran while one was open for 4% of the time, Pallas kernels for 50%

profile of v5, /device:TPU:0, one launch (start us, length us, event | category | flops | bytes accessed | tf_op | source)
XLA Modules:
  0.0 514.8 jit_solution(12087703553042192870)
XLA Ops:
  3.8 6.4 %all-to-all-start = ((bf16[4,4,64,512]{3,2,1,0:T(8,128)(2,1)}), bf16[4,4,64,512]{3,2,1,0:T(8,128)(2,1)S(1)}, u32[]{:S(2)}, u32[]{:S(2)}) async-start(bf16[4,4,64,512]{3,2,1,0:T(8,128)(2,1)} %broadcast_in_dim.65.refs_2_), calls=%async_computation | async-start | bytes 2097152 | tf_op jit(solution)/shard_map/all_to_all | solution.py:49
  18.6 8.6 %shard_map.186 = (bf16[1024,1024]{1,0:T(8,128)(2,1)}, bf16[1024,1024]{1,0:T(8,128)(2,1)}, bf16[1024,1024]{1,0:T(8,128)(2,1)}, bf16[1024,1024]{1,0:T(8,128)(2,1)}) custom-call(s32[1]{0:T(128)} %bitcast.refs_0_, s32[1]{0:T(128)} %dynamic_slice.9.refs_1_.refs_0_, bf16[1024,1024]{1,0:T(8,128)(2,1)} %refs_2_.1, bf16[1024,1024]{1,0:T(8,128)(2,1)} %refs_3_.1, ...), custom_call_target="tpu_custom_call" | custom-call | flops 20971520 | bytes 12582912 | tf_op jit(solution)/shard_map/pallas_call | solution.py:638
  27.2 8.8 %all-to-all-done.refs_7_ = bf16[4,4,64,512]{3,2,1,0:T(8,128)(2,1)S(1)} async-done(((bf16[4,4,64,512]{3,2,1,0:T(8,128)(2,1)}), bf16[4,4,64,512]{3,2,1,0:T(8,128)(2,1)S(1)}, u32[]{:S(2)}, u32[]{:S(2)}) %all-to-all-start) | async-done | bytes 1048608 | tf_op jit(solution)/shard_map/all_to_all | solution.py:49
  43.6 21.3 %collective-permute-done.1.refs_2_ = bf16[4,4,64,512]{3,2,1,0:T(8,128)(2,1)S(1)} collective-permute-done((bf16[4,4,64,512]{3,2,1,0:T(8,128)(2,1)}, bf16[4,4,64,512]{3,2,1,0:T(8,128)(2,1)S(1)}, u32[]{:S(2)}, u32[]{:S(2)}) %collective-permute-start.1) | collective-permute-done | bytes 1048608 | tf_op jit(solution)/shard_map/ppermute | solution.py:45
  67.3 4.7 all-to-all-start.2
  77.7 9.2 %collective-permute-done.3.refs_2_ = bf16[2,4,64,512]{3,2,1,0:T(8,128)(2,1)S(1)} collective-permute-done((bf16[2,4,64,512]{3,2,1,0:T(8,128)(2,1)}, bf16[2,4,64,512]{3,2,1,0:T(8,128)(2,1)S(1)}, u32[]{:S(2)}, u32[]{:S(2)}) %collective-permute-start.3) | collective-permute-done | bytes 524320 | tf_op jit(solution)/shard_map/ppermute | solution.py:45
  90.0 4.8 shard_map.191.refs_5_
  100.2 3.5 all-to-all-start.3
  104.3 25.1 %shard_map.192 = (f32[3,1024,1024]{2,1,0:T(8,128)}, f32[1024,1024]{1,0:T(8,128)}, bf16[1024,1024]{1,0:T(8,128)(2,1)}, bf16[1024,1024]{1,0:T(8,128)(2,1)}) custom-call(s32[1]{0:T(128)} %dynamic_slice.9.refs_1_.refs_0_, bf16[1024,1024]{1,0:T(8,128)(2,1)} %get-tuple-element.232.refs_1_, bf16[1024,1024]{1,0:T(8,128)(2,1)} %get-tuple-element.233.refs_2_, ...), custom_call_target="tpu_custom_call" | custom-call | flops 34359738368 | bytes 29360128 | tf_op jit(solution)/shard_map/pallas_call | solution.py:466
  129.5 3.6 collective-permute-done.8.refs_5_
  140.4 3.8 all-to-all-start.4
  151.7 27.8 %shard_map.195 = (bf16[2,2,2,3,64,256]{5,4,3,2,1,0:T(8,128)(2,1)}, bf16[2,2,2,3,64,256]{5,4,3,2,1,0:T(8,128)(2,1)}, bf16[2,2,3,64,256]{4,3,2,1,0:T(8,128)(2,1)},...) custom-call(bf16[1024,1024]{1,0:T(8,128)(2,1)} %get-tuple-element.25, ...), custom_call_target="tpu_custom_call" | custom-call | flops 77309411328 | bytes 48234496 | tf_op jit(solution)/shard_map/pallas_call | solution.py:338
  192.2 29.9 %shard_map.198 = (bf16[2,2,2,3,64,256]{5,4,3,2,1,0:T(8,128)(2,1)}, bf16[2,2,2,3,64,256]{5,4,3,2,1,0:T(8,128)(2,1)}, bf16[2,2,3,64,256]{4,3,2,1,0:T(8,128)(2,1)},...) custom-call(bf16[1024,1024]{1,0:T(8,128)(2,1)} %get-tuple-element.25, ...), custom_call_target="tpu_custom_call" | custom-call | flops 77309411328 | bytes 48234496 | tf_op jit(solution)/shard_map/pallas_call | solution.py:338
  229.8 42.0 %shard_map.201 = (bf16[2,2,2,3,64,384]{5,4,3,2,1,0:T(8,128)(2,1)}, bf16[2,2,2,3,64,384]{5,4,3,2,1,0:T(8,128)(2,1)}, bf16[2,2,3,64,384]{4,3,2,1,0:T(8,128)(2,1)},...) custom-call(bf16[1024,1024]{1,0:T(8,128)(2,1)} %get-tuple-element.25, ...), custom_call_target="tpu_custom_call" | custom-call | flops 115964116992 | bytes 51380224 | tf_op jit(solution)/shard_map/pallas_call | solution.py:338
  280.0 29.8 %shard_map.204 = (bf16[2,2,2,3,64,256]{5,4,3,2,1,0:T(8,128)(2,1)}, bf16[2,2,2,3,64,256]{5,4,3,2,1,0:T(8,128)(2,1)}, bf16[2,2,3,64,256]{4,3,2,1,0:T(8,128)(2,1)},...) custom-call(bf16[1024,1024]{1,0:T(8,128)(2,1)} %get-tuple-element.25, ...), custom_call_target="tpu_custom_call" | custom-call | flops 77309411328 | bytes 48234496 | tf_op jit(solution)/shard_map/pallas_call | solution.py:338
  311.2 3.8 shard_map.209
  316.9 4.6 all-to-all-start.5
  323.7 7.3 %shard_map.207 = (bf16[1024,1024]{1,0:T(8,128)(2,1)}, f32[8,1024]{1,0:T(8,128)}) custom-call(s32[1]{0:T(128)} %bitcast.refs_0_, f32[1024,1024]{1,0:T(8,128)} %get-tuple-element.348.refs_1_, bf16[1024,1024]{1,0:T(8,128)(2,1)} %collective-permute-done.30.refs_2_, f32[1024,1024]{1,0:T(8,128)} %get-tuple-element.247.refs_3_.refs_1_, ...), custom_call_target="tpu_custom_call" | custom-call | flops 20971520 | bytes 12582912 | tf_op jit(solution)/shard_map/pallas_call | solution.py:638
  331.1 21.0 %shard_map.208 = (bf16[4,4,4,64,256]{4,3,2,1,0:T(8,128)(2,1)}, bf16[4,4,4,64,256]{4,3,2,1,0:T(8,128)(2,1)}, f32[8,512]{1,0:T(8,128)}, f32[1024,1024]{1,0:T(8,128)}) custom-call(s32[1]{0:T(128)} %dynamic_slice.9.refs_1_.refs_0_, bf16[1024,1024]{1,0:T(8,128)(2,1)} %get-tuple-element.232.refs_1_, bf16[1024,1024]{1,0:T(8,128)(2,1)} %get-tuple-element.350.refs_2_.refs_3_, ...), custom_call_target="tpu_custom_call" | custom-call | flops 34359738368 | bytes 23068672 | tf_op jit(solution)/shard_map/pallas_call | solution.py:573
  354.2 4.7 shard_map.212
  360.9 4.9 all-to-all-start.6
  368.0 22.2 %shard_map.211 = (bf16[4,4,4,64,256]{4,3,2,1,0:T(8,128)(2,1)}, bf16[4,4,4,64,256]{4,3,2,1,0:T(8,128)(2,1)}, f32[8,512]{1,0:T(8,128)}, f32[1024,1024]{1,0:T(8,128)}) custom-call(s32[1]{0:T(128)} %dynamic_slice.9.refs_1_.refs_0_, bf16[1024,1024]{1,0:T(8,128)(2,1)} %get-tuple-element.232.refs_1_, ...), custom_call_target="tpu_custom_call", output_to_operand_aliasing={{3}: (7, {})} | custom-call | flops 34359738368 | bytes 23068672 | tf_op jit(solution)/shard_map/pallas_call | solution.py:573
  393.3 6.6 %shard_map.216 = (bf16[4,2,3,64,384]{4,3,2,1,0:T(8,128)(2,1)}, bf16[2,2,3,64,256]{4,3,2,1,0:T(8,128)(2,1)}, bf16[2,2,3,64,256]{4,3,2,1,0:T(8,128)(2,1)}, bf16[2,...) custom-call(bf16[4,2,3,64,384]{4,3,2,1,0:T(8,128)(2,1)} %get-tuple-e, ...), custom_call_target="tpu_custom_call" | custom-call | bytes 22544384 | tf_op jit(solution)/shard_map/pallas_call | solution.py:118
  399.9 5.4 %all-to-all-start.10 = ((bf16[4,2,3,64,384]{4,3,2,1,0:T(8,128)(2,1)}), bf16[4,2,3,64,384]{4,3,2,1,0:T(8,128)(2,1)}, u32[]{:S(2)}, u32[]{:S(2)}) async-start(bf16[4,2,3,64,384]{4,3,2,1,0:T(8,128)(2,1)} %get-tuple-element.447), calls=%async_computation.10 | async-start | bytes 2359296 | tf_op jit(solution)/shard_map/all_to_all | solution.py:49
  411.9 7.6 %shard_map.215 = (f32[1024,1024]{1,0:T(8,128)}, f32[8,1024]{1,0:T(8,128)}) custom-call(s32[1]{0:T(128)} %bitcast.refs_0_, f32[1024,1024]{1,0:T(8,128)} %get-tuple-element.391.refs_1_, bf16[1024,1024]{1,0:T(8,128)(2,1)} %get-tuple-element.233.refs_2_, bf16[1024,1024]{1,0:T(8,128)(2,1)} %get-tuple-element.350.refs_2_.refs_3_, f32[1,1024]{1,0:T(1,128)} %reshape.202.refs_4_), custom_call_target="tpu_custom_call" | custom-call | flops 20971520 | bytes 12582912 | tf_op jit(solution)/shard_map/pallas_call | solution.py:638
  419.4 8.8 %collective-permute-done.42.refs_4_ = bf16[2,2,3,64,256]{4,3,2,1,0:T(8,128)(2,1)} collective-permute-done((bf16[2,2,3,64,256]{4,3,2,1,0:T(8,128)(2,1)}, bf16[2,2,3,64,256]{4,3,2,1,0:T(8,128)(2,1)}, u32[]{:S(2)}, u32[]{:S(2)}) %collective-permute-start.42) | collective-permute-done | bytes 393248 | tf_op jit(solution)/shard_map/ppermute | solution.py:45
  430.5 5.2 %shard_map.218 = (bf16[2,2,4,64,256]{4,3,2,1,0:T(8,128)(2,1)}, bf16[2,2,4,64,256]{4,3,2,1,0:T(8,128)(2,1)}, bf16[2,4,64,256]{3,2,1,0:T(8,128)(2,1)}, bf16[2,4,64...) custom-call(bf16[4,4,4,64,256]{4,3,2,1,0:T(8,128)(2,1)} %get-tuple-e, ...), custom_call_target="tpu_custom_call" | custom-call | bytes 17825792 | tf_op jit(solution)/shard_map/pallas_call | solution.py:118
  435.7 5.0 all-to-all-start.7
  444.5 6.6 %shard_map.214.refs_0_ = bf16[1024,1024]{1,0:T(8,128)(2,1)} custom-call(s32[1]{0:T(128)} %bitcast.refs_0_, f32[1024,1024]{1,0:T(8,128)} %get-tuple-element.247.refs_3_.refs_1_, f32[1024,1024]{1,0:T(8,128)} %get-tuple-element.347.refs_2_, bf16[1024,1024]{1,0:T(8,128)(2,1)} %get-tuple-element.390.refs_3_), custom_call_target="tpu_custom_call" | custom-call | flops 20971520 | bytes 12582912 | tf_op jit(solution)/shard_map/pallas_call | solution.py:638
  455.7 5.5 %collective-permute-done.47 = f32[5,1024]{1,0:T(8,128)S(1)} collective-permute-done((f32[5,1024]{1,0:T(8,128)S(1)}, f32[5,1024]{1,0:T(8,128)S(1)}, u32[]{:S(2)}, u32[]{:S(2)}) %collective-permute-start.47) | collective-permute-done | bytes 20512 | tf_op jit(solution)/shard_map/ppermute | solution.py:45
  469.0 5.1 all-to-all-start.8
  504.5 8.5 %all-to-all-done.9 = bf16[4,4,64,256]{3,2,1,0:T(8,128)(2,1)S(1)} async-done(((bf16[4,4,64,256]{3,2,1,0:T(8,128)(2,1)}), bf16[4,4,64,256]{3,2,1,0:T(8,128)(2,1)S(1)}, u32[]{:S(2)}, u32[]{:S(2)}) %all-to-all-start.9) | async-done | bytes 524320 | tf_op jit(solution)/shard_map/all_to_all | solution.py:49
  (334 shorter events, 151.1 us)
Async XLA Ops:
  3.8 32.2 %all-to-all-start = ((bf16[4,4,64,512]{3,2,1,0:T(8,128)(2,1)}), bf16[4,4,64,512]{3,2,1,0:T(8,128)(2,1)S(1)}, u32[]{:S(2)}, u32[]{:S(2)}) async-start(bf16[4,4,64,512]{3,2,1,0:T(8,128)(2,1)} %broadcast_in_dim.65.refs_2_), calls=%async_computation | async-start | bytes 2097152 | tf_op jit(solution)/shard_map/all_to_all | solution.py:49
  96.1 50.1 %collective-permute-start.11 = (bf16[1024,1024]{1,0:T(8,128)(2,1)}, bf16[1024,1024]{1,0:T(8,128)(2,1)}, u32[]{:S(2)}, u32[]{:S(2)}) collective-permute-start(bf16[1024,1024]{1,0:T(8,128)(2,1)} %get-tuple-element.257), channel_id=1, source_target_pairs={{0,2},{1,3},{2,0},{3,1},{4,6},{5,7},{6,4},{7,5},{8,10},{9,11},{10,... | collective-permute-start | bytes 6291464 | tf_op jit(solution)/shard_map/ppermute | solution.py:45
  96.7 32.8 %collective-permute-start.6 = (bf16[4,2,3,64,256]{4,3,2,1,0:T(8,128)(2,1)S(1)}, bf16[4,2,3,64,256]{4,3,2,1,0:T(8,128)(2,1)S(1)}, u32[]{:S(2)}, u32[]{:S(2)}) collective-permute-start(bf16[4,2,3,64,256]{4,3,2,1,0:T(8,128)(2,1)S(1)} %copy-done.15), channel_id=1, source_target_pairs={{0,4},{1,5},{2,6},{3,7},{4,0},{5,1},{6,2},{7,3},{8,12},{9,13},{10,... | collective-permute-start | bytes 2359304 | tf_op jit(solution)/shard_map/ppermute | solution.py:45
  97.6 31.8 %collective-permute-start.7 = (bf16[4,2,3,64,256]{4,3,2,1,0:T(8,128)(2,1)S(1)}, bf16[4,2,3,64,256]{4,3,2,1,0:T(8,128)(2,1)}, u32[]{:S(2)}, u32[]{:S(2)}) collective-permute-start(bf16[4,2,3,64,256]{4,3,2,1,0:T(8,128)(2,1)S(1)} %copy-done.15), channel_id=1, source_target_pairs={{0,1},{1,0},{2,3},{3,2},{4,5},{5,4},{6,7},{7,6},{8,9},{9,8},{10,11... | collective-permute-start | bytes 2359304 | tf_op jit(solution)/shard_map/ppermute | solution.py:45
  99.1 33.9 %collective-permute-start.8 = (bf16[4,2,3,64,256]{4,3,2,1,0:T(8,128)(2,1)}, bf16[4,2,3,64,256]{4,3,2,1,0:T(8,128)(2,1)}, u32[]{:S(2)}, u32[]{:S(2)}) collective-permute-start(bf16[4,2,3,64,256]{4,3,2,1,0:T(8,128)(2,1)} %get-tuple-element.252.refs_4_), channel_id=1, source_target_pairs={{0,4},{1,5},{2,6},{3,7},{4,0},{5,1},{6,2},{7,3},{8,12},{9,13},{10,... | collective-permute-start | bytes 2359304 | tf_op jit(solution)/shard_map/ppermute | solution.py:45
  100.2 33.6 %all-to-all-start.3 = ((bf16[4,2,3,64,384]{4,3,2,1,0:T(8,128)(2,1)}), bf16[4,2,3,64,384]{4,3,2,1,0:T(8,128)(2,1)S(1)}, u32[]{:S(2)}, u32[]{:S(2)}) async-start(bf16[4,2,3,64,384]{4,3,2,1,0:T(8,128)(2,1)} %get-tuple-element.253), calls=%async_computation.3 | async-start | bytes 2359296 | tf_op jit(solution)/shard_map/all_to_all | solution.py:49
  139.5 44.2 %collective-permute-start.16 = (bf16[4,2,3,64,384]{4,3,2,1,0:T(8,128)(2,1)}, bf16[4,2,3,64,384]{4,3,2,1,0:T(8,128)(2,1)S(1)}, u32[]{:S(2)}, u32[]{:S(2)}) collective-permute-start(bf16[4,2,3,64,384]{4,3,2,1,0:T(8,128)(2,1)} %get-tuple-element.275.refs_4_), channel_id=1, source_target_pairs={{0,4},{1,5},{2,6},{3,7},{4,0},{5,1},{6,2},{7,3},{8,12},{9,13},{10,... | collective-permute-start | bytes 3538952 | tf_op jit(solution)/shard_map/ppermute | solution.py:45
  140.4 43.3 %all-to-all-start.4 = ((bf16[4,2,3,64,256]{4,3,2,1,0:T(8,128)(2,1)}), bf16[4,2,3,64,256]{4,3,2,1,0:T(8,128)(2,1)S(1)}, u32[]{:S(2)}, u32[]{:S(2)}) async-start(bf16[4,2,3,64,256]{4,3,2,1,0:T(8,128)(2,1)} %get-tuple-element.276), calls=%async_computation.4 | async-start | bytes 1572864 | tf_op jit(solution)/shard_map/all_to_all | solution.py:49
  146.2 37.4 %collective-permute-start.17 = (bf16[4,2,3,64,384]{4,3,2,1,0:T(8,128)(2,1)S(1)}, bf16[4,2,3,64,384]{4,3,2,1,0:T(8,128)(2,1)}, u32[]{:S(2)}, u32[]{:S(2)}) collective-permute-start(bf16[4,2,3,64,384]{4,3,2,1,0:T(8,128)(2,1)S(1)} %copy-done.17), channel_id=1, source_target_pairs={{0,1},{1,0},{2,3},{3,2},{4,5},{5,4},{6,7},{7,6},{8,9},{9,8},{10,11... | collective-permute-start | bytes 3538952 | tf_op jit(solution)/shard_map/ppermute | solution.py:45
  148.7 33.6 %collective-permute-start.14 = (bf16[2,2,3,64,256]{4,3,2,1,0:T(8,128)(2,1)}, bf16[2,2,3,64,256]{4,3,2,1,0:T(8,128)(2,1)S(1)}, u32[]{:S(2)}, u32[]{:S(2)}) collective-permute-start(bf16[2,2,3,64,256]{4,3,2,1,0:T(8,128)(2,1)} %get-tuple-element.273), channel_id=1, source_target_pairs={{0,1},{1,0},{2,3},{3,2},{4,5},{5,4},{6,7},{7,6},{8,9},{9,8},{10,11... | collective-permute-start | bytes 1179656 | tf_op jit(solution)/shard_map/ppermute | solution.py:45
  150.7 33.0 %collective-permute-start.15 = (bf16[2,2,3,64,256]{4,3,2,1,0:T(8,128)(2,1)}, bf16[2,2,3,64,256]{4,3,2,1,0:T(8,128)(2,1)}, u32[]{:S(2)}, u32[]{:S(2)}) collective-permute-start(bf16[2,2,3,64,256]{4,3,2,1,0:T(8,128)(2,1)} %get-tuple-element.274), channel_id=1, source_target_pairs={{0,4},{1,5},{2,6},{3,7},{4,0},{5,1},{6,2},{7,3},{8,12},{9,13},{10,... | collective-permute-start | bytes 1179656 | tf_op jit(solution)/shard_map/ppermute | solution.py:45
  185.0 37.1 %collective-permute-start.20 = (bf16[4,2,3,64,256]{4,3,2,1,0:T(8,128)(2,1)}, bf16[4,2,3,64,256]{4,3,2,1,0:T(8,128)(2,1)S(1)}, u32[]{:S(2)}, u32[]{:S(2)}) collective-permute-start(bf16[4,2,3,64,256]{4,3,2,1,0:T(8,128)(2,1)} %get-tuple-element.277.refs_4_), channel_id=1, source_target_pairs={{0,4},{1,5},{2,6},{3,7},{4,0},{5,1},{6,2},{7,3},{8,12},{9,13},{10,... | collective-permute-start | bytes 2359304 | tf_op jit(solution)/shard_map/ppermute | solution.py:45
  186.1 36.1 %collective-permute-start.21 = (bf16[4,2,3,64,256]{4,3,2,1,0:T(8,128)(2,1)}, bf16[4,2,3,64,256]{4,3,2,1,0:T(8,128)(2,1)S(1)}, u32[]{:S(2)}, u32[]{:S(2)}) collective-permute-start(bf16[4,2,3,64,256]{4,3,2,1,0:T(8,128)(2,1)} %get-tuple-element.277.refs_4_), channel_id=1, source_target_pairs={{0,1},{1,0},{2,3},{3,2},{4,5},{5,4},{6,7},{7,6},{8,9},{9,8},{10,11... | collective-permute-start | bytes 2359304 | tf_op jit(solution)/shard_map/ppermute | solution.py:45
  190.1 31.9 %collective-permute-start.18 = (bf16[2,2,3,64,384]{4,3,2,1,0:T(8,128)(2,1)}, bf16[2,2,3,64,384]{4,3,2,1,0:T(8,128)(2,1)S(1)}, u32[]{:S(2)}, u32[]{:S(2)}) collective-permute-start(bf16[2,2,3,64,384]{4,3,2,1,0:T(8,128)(2,1)} %get-tuple-element.297), channel_id=1, source_target_pairs={{0,1},{1,0},{2,3},{3,2},{4,5},{5,4},{6,7},{7,6},{8,9},{9,8},{10,11... | collective-permute-start | bytes 1769480 | tf_op jit(solution)/shard_map/ppermute | solution.py:45
  191.2 30.9 %collective-permute-start.19 = (bf16[2,2,3,64,384]{4,3,2,1,0:T(8,128)(2,1)}, bf16[2,2,3,64,384]{4,3,2,1,0:T(8,128)(2,1)S(1)}, u32[]{:S(2)}, u32[]{:S(2)}) collective-permute-start(bf16[2,2,3,64,384]{4,3,2,1,0:T(8,128)(2,1)} %get-tuple-element.298), channel_id=1, source_target_pairs={{0,4},{1,5},{2,6},{3,7},{4,0},{5,1},{6,2},{7,3},{8,12},{9,13},{10,... | collective-permute-start | bytes 1769480 | tf_op jit(solution)/shard_map/ppermute | solution.py:45
  225.7 46.1 %collective-permute-start.22 = (bf16[2,2,3,64,256]{4,3,2,1,0:T(8,128)(2,1)}, bf16[2,2,3,64,256]{4,3,2,1,0:T(8,128)(2,1)S(1)}, u32[]{:S(2)}, u32[]{:S(2)}) collective-permute-start(bf16[2,2,3,64,256]{4,3,2,1,0:T(8,128)(2,1)} %get-tuple-element.318), channel_id=1, source_target_pairs={{0,1},{1,0},{2,3},{3,2},{4,5},{5,4},{6,7},{7,6},{8,9},{9,8},{10,11... | collective-permute-start | bytes 1179656 | tf_op jit(solution)/shard_map/ppermute | solution.py:45
  226.7 45.2 %collective-permute-start.23 = (bf16[2,2,3,64,256]{4,3,2,1,0:T(8,128)(2,1)}, bf16[2,2,3,64,256]{4,3,2,1,0:T(8,128)(2,1)S(1)}, u32[]{:S(2)}, u32[]{:S(2)}) collective-permute-start(bf16[2,2,3,64,256]{4,3,2,1,0:T(8,128)(2,1)} %get-tuple-element.319), channel_id=1, source_target_pairs={{0,4},{1,5},{2,6},{3,7},{4,0},{5,1},{6,2},{7,3},{8,12},{9,13},{10,... | collective-permute-start | bytes 1179656 | tf_op jit(solution)/shard_map/ppermute | solution.py:45
  227.7 44.2 %collective-permute-start.24 = (bf16[2,2,2,3,64,256]{5,4,3,2,1,0:T(8,128)(2,1)}, bf16[2,2,2,3,64,256]{5,4,3,2,1,0:T(8,128)(2,1)S(1)}, u32[]{:S(2)}, u32[]{:S(2)}) collective-permute-start(bf16[2,2,2,3,64,256]{5,4,3,2,1,0:T(8,128)(2,1)} %get-tuple-element.320), channel_id=1, source_target_pairs={{0,4},{1,5},{2,6},{3,7},{4,0},{5,1},{6,2},{7,3},{8,12},{9,13},{10,... | collective-permute-start | bytes 2359304 | tf_op jit(solution)/shard_map/ppermute | solution.py:45
  228.7 43.2 %collective-permute-start.25 = (bf16[2,2,2,3,64,256]{5,4,3,2,1,0:T(8,128)(2,1)}, bf16[2,2,2,3,64,256]{5,4,3,2,1,0:T(8,128)(2,1)S(1)}, u32[]{:S(2)}, u32[]{:S(2)}) collective-permute-start(bf16[2,2,2,3,64,256]{5,4,3,2,1,0:T(8,128)(2,1)} %get-tuple-element.321), channel_id=1, source_target_pairs={{0,1},{1,0},{2,3},{3,2},{4,5},{5,4},{6,7},{7,6},{8,9},{9,8},{10,11... | collective-permute-start | bytes 2359304 | tf_op jit(solution)/shard_map/ppermute | solution.py:45
  275.9 33.8 %collective-permute-start.26 = (bf16[2,2,3,64,256]{4,3,2,1,0:T(8,128)(2,1)}, bf16[2,2,3,64,256]{4,3,2,1,0:T(8,128)(2,1)S(1)}, u32[]{:S(2)}, u32[]{:S(2)}) collective-permute-start(bf16[2,2,3,64,256]{4,3,2,1,0:T(8,128)(2,1)} %get-tuple-element.343), channel_id=1, source_target_pairs={{0,4},{1,5},{2,6},{3,7},{4,0},{5,1},{6,2},{7,3},{8,12},{9,13},{10,... | collective-permute-start | bytes 1179656 | tf_op jit(solution)/shard_map/ppermute | solution.py:45
  277.0 32.8 %collective-permute-start.27 = (bf16[2,2,3,64,256]{4,3,2,1,0:T(8,128)(2,1)}, bf16[2,2,3,64,256]{4,3,2,1,0:T(8,128)(2,1)S(1)}, u32[]{:S(2)}, u32[]{:S(2)}) collective-permute-start(bf16[2,2,3,64,256]{4,3,2,1,0:T(8,128)(2,1)} %get-tuple-element.344), channel_id=1, source_target_pairs={{0,1},{1,0},{2,3},{3,2},{4,5},{5,4},{6,7},{7,6},{8,9},{9,8},{10,11... | collective-permute-start | bytes 1179656 | tf_op jit(solution)/shard_map/ppermute | solution.py:45
  277.9 31.9 %collective-permute-start.28 = (bf16[2,2,2,3,64,256]{5,4,3,2,1,0:T(8,128)(2,1)S(1)}, bf16[2,2,2,3,64,256]{5,4,3,2,1,0:T(8,128)(2,1)S(1)}, u32[]{:S(2)}, u32[]{:S(2)}) collective-permute-start(bf16[2,2,2,3,64,256]{5,4,3,2,1,0:T(8,128)(2,1)S(1)} %copy-done.25), channel_id=1, source_target_pairs={{0,4},{1,5},{2,6},{3,7},{4,0},{5,1},{6,2},{7,3},{8,12},{9,13},{10,... | collective-permute-start | bytes 2359304 | tf_op jit(solution)/shard_map/ppermute | solution.py:45
  278.9 30.9 %collective-permute-start.29 = (bf16[2,2,2,3,64,256]{5,4,3,2,1,0:T(8,128)(2,1)S(1)}, bf16[2,2,2,3,64,256]{5,4,3,2,1,0:T(8,128)(2,1)S(1)}, u32[]{:S(2)}, u32[]{:S(2)}) collective-permute-start(bf16[2,2,2,3,64,256]{5,4,3,2,1,0:T(8,128)(2,1)S(1)} %copy-done.26), channel_id=1, source_target_pairs={{0,1},{1,0},{2,3},{3,2},{4,5},{5,4},{6,7},{7,6},{8,9},{9,8},{10,11... | collective-permute-start | bytes 2359304 | tf_op jit(solution)/shard_map/ppermute | solution.py:45
  314.9 37.1 %collective-permute-start.32 = (bf16[2,2,3,64,256]{4,3,2,1,0:T(8,128)(2,1)}, bf16[2,2,3,64,256]{4,3,2,1,0:T(8,128)(2,1)}, u32[]{:S(2)}, u32[]{:S(2)}) collective-permute-start(bf16[2,2,3,64,256]{4,3,2,1,0:T(8,128)(2,1)} %get-tuple-element.367), channel_id=1, source_target_pairs={{0,4},{1,5},{2,6},{3,7},{4,0},{5,1},{6,2},{7,3},{8,12},{9,13},{10,... | collective-permute-start | bytes 1179656 | tf_op jit(solution)/shard_map/ppermute | solution.py:45
  316.0 36.0 %collective-permute-start.33 = (bf16[2,2,3,64,256]{4,3,2,1,0:T(8,128)(2,1)}, bf16[2,2,3,64,256]{4,3,2,1,0:T(8,128)(2,1)}, u32[]{:S(2)}, u32[]{:S(2)}) collective-permute-start(bf16[2,2,3,64,256]{4,3,2,1,0:T(8,128)(2,1)} %get-tuple-element.368), channel_id=1, source_target_pairs={{0,1},{1,0},{2,3},{3,2},{4,5},{5,4},{6,7},{7,6},{8,9},{9,8},{10,11... | collective-permute-start | bytes 1179656 | tf_op jit(solution)/shard_map/ppermute | solution.py:45
  316.9 35.1 %all-to-all-start.5 = ((bf16[4,2,3,64,256]{4,3,2,1,0:T(8,128)(2,1)}), bf16[4,2,3,64,256]{4,3,2,1,0:T(8,128)(2,1)}, u32[]{:S(2)}, u32[]{:S(2)}) async-start(bf16[4,2,3,64,256]{4,3,2,1,0:T(8,128)(2,1)} %get-tuple-element.366), calls=%async_computation.5 | async-start | bytes 1572864 | tf_op jit(solution)/shard_map/all_to_all | solution.py:49
  321.5 31.3 %collective-permute-start.31 = (bf16[1024,1024]{1,0:T(8,128)(2,1)}, bf16[1024,1024]{1,0:T(8,128)(2,1)S(1)}, u32[]{:S(2)}, u32[]{:S(2)}) collective-permute-start(bf16[1024,1024]{1,0:T(8,128)(2,1)} %get-tuple-element.356), channel_id=1, source_target_pairs={{0,2},{1,3},{2,0},{3,1},{4,6},{5,7},{6,4},{7,5},{8,10},{9,11},{10,... | collective-permute-start | bytes 6291464 | tf_op jit(solution)/shard_map/ppermute | solution.py:45
  321.6 30.5 %collective-permute-start.34 = (bf16[2,2,2,3,64,384]{5,4,3,2,1,0:T(8,128)(2,1)}, bf16[2,2,2,3,64,384]{5,4,3,2,1,0:T(8,128)(2,1)S(1)}, u32[]{:S(2)}, u32[]{:S(2)}) collective-permute-start(bf16[2,2,2,3,64,384]{5,4,3,2,1,0:T(8,128)(2,1)} %get-tuple-element.369), channel_id=1, source_target_pairs={{0,4},{1,5},{2,6},{3,7},{4,0},{5,1},{6,2},{7,3},{8,12},{9,13},{10,... | collective-permute-start | bytes 3538952 | tf_op jit(solution)/shard_map/ppermute | solution.py:45
  358.9 31.3 %collective-permute-start.37 = (bf16[2,2,3,64,384]{4,3,2,1,0:T(8,128)(2,1)}, bf16[2,2,3,64,384]{4,3,2,1,0:T(8,128)(2,1)S(1)}, u32[]{:S(2)}, u32[]{:S(2)}) collective-permute-start(bf16[2,2,3,64,384]{4,3,2,1,0:T(8,128)(2,1)} %get-tuple-element.386), channel_id=1, source_target_pairs={{0,4},{1,5},{2,6},{3,7},{4,0},{5,1},{6,2},{7,3},{8,12},{9,13},{10,... | collective-permute-start | bytes 1769480 | tf_op jit(solution)/shard_map/ppermute | solution.py:45
  360.9 30.8 %all-to-all-start.6 = ((bf16[4,2,3,64,256]{4,3,2,1,0:T(8,128)(2,1)}), bf16[4,2,3,64,256]{4,3,2,1,0:T(8,128)(2,1)S(1)}, u32[]{:S(2)}, u32[]{:S(2)}) async-start(bf16[4,2,3,64,256]{4,3,2,1,0:T(8,128)(2,1)} %get-tuple-element.385), calls=%async_computation.6 | async-start | bytes 1572864 | tf_op jit(solution)/shard_map/all_to_all | solution.py:49
  393.3 35.6 %collective-permute-start.41 = (bf16[4,4,4,64,256]{4,3,2,1,0:T(8,128)(2,1)}, bf16[4,4,4,64,256]{4,3,2,1,0:T(8,128)(2,1)S(1)}, u32[]{:S(2)}, u32[]{:S(2)}) collective-permute-start(bf16[4,4,4,64,256]{4,3,2,1,0:T(8,128)(2,1)} %get-tuple-element.395), channel_id=1, source_target_pairs={{0,2},{1,3},{2,0},{3,1},{4,6},{5,7},{6,4},{7,5},{8,10},{9,11},{10,... | collective-permute-start | bytes 6291464 | tf_op jit(solution)/shard_map/ppermute | solution.py:45
  399.9 35.8 %all-to-all-start.10 = ((bf16[4,2,3,64,384]{4,3,2,1,0:T(8,128)(2,1)}), bf16[4,2,3,64,384]{4,3,2,1,0:T(8,128)(2,1)}, u32[]{:S(2)}, u32[]{:S(2)}) async-start(bf16[4,2,3,64,384]{4,3,2,1,0:T(8,128)(2,1)} %get-tuple-element.447), calls=%async_computation.10 | async-start | bytes 2359296 | tf_op jit(solution)/shard_map/all_to_all | solution.py:49
  (100 other events, 865.4 us)

commit v6 on v5

--- a/solution.py
+++ b/solution.py
@@ -911,6 +911,7 @@
     if parts > 1:
         steps.append(("sum sides", names[0]))
     places = add(*steps)
+    del places[1]
     result = row_call(
         result_kernel, flip, [hidden, totals[0], ffn_twin], [BF]
     )[0]
@@ -918,7 +919,7 @@
     steps = [("sum sides", names[-1])]
     if parts > 1:
         steps.append(("sum z", names[0]))
-    places = add(*steps)
+    places = add(*steps)[:1]
     (small,) = close([links.sum_rest(small)], places)
     add(("sum z", names[-1]))
     shard = lambda p: jnp.sum(sums[p]["z"].astype(F32), axis=0)

time: 523 us -> 515 us (0.985)
  waiting for transfers between devices: 87 us -> 76.5 us
  local copies, waits for them, and re-layouts: 29.2 us -> 35 us
    ppermute x59, waiting for transfers between devices: 67.7 us -> 53.3 us  [swap(): return lax.ppermute(value, AXES, pairs)]
    unnamed x124 -> x118, local copies, waits for them, and re-layouts: 17.3 us -> 16.8 us
  transfers between devices with their start and end apart: 70 -> 70, of which waited for: 21 -> 19; matrix products, arithmetic and copies ran while one was open for 4% -> 6% of each run, Pallas kernels for 50% -> 51%
where the time goes in v6:
time: 515 us; the launch traced here: 507 us
  Pallas kernels  273 us (53%)
  starting transfers between devices  104 us (20%)
  waiting for transfers between devices  76.5 us (15%)
  local copies, waits for them, and re-layouts  35 us (7%)
  other arithmetic  16.2 us (3%)
    pallas_call x4, Pallas kernels, ffn_piece(): pl.pallas_call(functools.partial(ffn_kernel, first, last, len(ties)), gri...  129 us
    ppermute x59, starting transfers between devices, swap(): return lax.ppermute(value, AXES, pairs)  54.6 us
    ppermute x59, waiting for transfers between devices, swap(): return lax.ppermute(value, AXES, pairs)  53.3 us
    all_to_all x11, starting transfers between devices, turn_z(): lax.all_to_all(value, 'dp', 0, 0, axis_index_groups=groups, tiled=True)  49.7 us
    pallas_call x2, Pallas kernels, mixer_back(): pl.pallas_call(functools.partial(mixer_back_kernel, first, len(ties), min...  43 us
    pallas_call x8, Pallas kernels, small_calls(): pl.pallas_call(body, grid=(max(tiles),), in_specs=[spec(item.shape, count...  33 us
    pallas_call x4, Pallas kernels, row_call(): pl.pallas_call(body, grid=(rows // height,), in_specs=[scalar] + specs +...  30 us
    pallas_call x1, Pallas kernels, mixer_part(): pl.pallas_call(functools.partial(mixer_kernel, first, last, len(ties), mi...  25.1 us
  transfers between devices with their start and end apart: 70, of which 19 were waited for; matrix products, arithmetic and copies ran while one was open for 6% of the time, Pallas kernels for 51%

profile of v6, /device:TPU:0, one launch (start us, length us, event | category | flops | bytes accessed | tf_op | source)
XLA Modules:
  0.0 506.8 jit_solution(17626369963367492324)
XLA Ops:
  3.8 6.4 %all-to-all-start = ((bf16[4,4,64,512]{3,2,1,0:T(8,128)(2,1)}), bf16[4,4,64,512]{3,2,1,0:T(8,128)(2,1)S(1)}, u32[]{:S(2)}, u32[]{:S(2)}) async-start(bf16[4,4,64,512]{3,2,1,0:T(8,128)(2,1)} %broadcast_in_dim.65.refs_2_), calls=%async_computation | async-start | bytes 2097152 | tf_op jit(solution)/shard_map/all_to_all | solution.py:49
  18.4 8.5 %shard_map.186 = (bf16[1024,1024]{1,0:T(8,128)(2,1)}, bf16[1024,1024]{1,0:T(8,128)(2,1)}, bf16[1024,1024]{1,0:T(8,128)(2,1)}, bf16[1024,1024]{1,0:T(8,128)(2,1)}) custom-call(s32[1]{0:T(128)} %bitcast.refs_0_, s32[1]{0:T(128)} %dynamic_slice.9.refs_1_.refs_0_, bf16[1024,1024]{1,0:T(8,128)(2,1)} %refs_2_.1, bf16[1024,1024]{1,0:T(8,128)(2,1)} %refs_3_.1, ...), custom_call_target="tpu_custom_call" | custom-call | flops 20971520 | bytes 12582912 | tf_op jit(solution)/shard_map/pallas_call | solution.py:638
  26.9 9.0 %all-to-all-done.refs_7_ = bf16[4,4,64,512]{3,2,1,0:T(8,128)(2,1)S(1)} async-done(((bf16[4,4,64,512]{3,2,1,0:T(8,128)(2,1)}), bf16[4,4,64,512]{3,2,1,0:T(8,128)(2,1)S(1)}, u32[]{:S(2)}, u32[]{:S(2)}) %all-to-all-start) | async-done | bytes 1048608 | tf_op jit(solution)/shard_map/all_to_all | solution.py:49
  43.5 21.3 %collective-permute-done.1.refs_2_ = bf16[4,4,64,512]{3,2,1,0:T(8,128)(2,1)S(1)} collective-permute-done((bf16[4,4,64,512]{3,2,1,0:T(8,128)(2,1)}, bf16[4,4,64,512]{3,2,1,0:T(8,128)(2,1)S(1)}, u32[]{:S(2)}, u32[]{:S(2)}) %collective-permute-start.1) | collective-permute-done | bytes 1048608 | tf_op jit(solution)/shard_map/ppermute | solution.py:45
  67.3 4.7 all-to-all-start.2
  77.6 9.2 %collective-permute-done.3.refs_2_ = bf16[2,4,64,512]{3,2,1,0:T(8,128)(2,1)S(1)} collective-permute-done((bf16[2,4,64,512]{3,2,1,0:T(8,128)(2,1)}, bf16[2,4,64,512]{3,2,1,0:T(8,128)(2,1)S(1)}, u32[]{:S(2)}, u32[]{:S(2)}) %collective-permute-start.3) | collective-permute-done | bytes 524320 | tf_op jit(solution)/shard_map/ppermute | solution.py:45
  90.0 4.8 shard_map.191.refs_5_
  100.2 3.5 all-to-all-start.3
  104.3 25.1 %shard_map.192 = (f32[3,1024,1024]{2,1,0:T(8,128)}, f32[1024,1024]{1,0:T(8,128)}, bf16[1024,1024]{1,0:T(8,128)(2,1)}, bf16[1024,1024]{1,0:T(8,128)(2,1)}) custom-call(s32[1]{0:T(128)} %dynamic_slice.9.refs_1_.refs_0_, bf16[1024,1024]{1,0:T(8,128)(2,1)} %get-tuple-element.230.refs_1_, bf16[1024,1024]{1,0:T(8,128)(2,1)} %get-tuple-element.231.refs_2_, ...), custom_call_target="tpu_custom_call" | custom-call | flops 34359738368 | bytes 29360128 | tf_op jit(solution)/shard_map/pallas_call | solution.py:466
  129.4 3.6 collective-permute-done.8.refs_5_
  140.4 3.7 all-to-all-start.4
  151.7 27.8 %shard_map.195 = (bf16[2,2,2,3,64,256]{5,4,3,2,1,0:T(8,128)(2,1)}, bf16[2,2,2,3,64,256]{5,4,3,2,1,0:T(8,128)(2,1)}, bf16[2,2,3,64,256]{4,3,2,1,0:T(8,128)(2,1)},...) custom-call(bf16[1024,1024]{1,0:T(8,128)(2,1)} %get-tuple-element.25, ...), custom_call_target="tpu_custom_call" | custom-call | flops 77309411328 | bytes 48234496 | tf_op jit(solution)/shard_map/pallas_call | solution.py:338
  192.2 29.7 %shard_map.198 = (bf16[2,2,2,3,64,256]{5,4,3,2,1,0:T(8,128)(2,1)}, bf16[2,2,2,3,64,256]{5,4,3,2,1,0:T(8,128)(2,1)}, bf16[2,2,3,64,256]{4,3,2,1,0:T(8,128)(2,1)},...) custom-call(bf16[1024,1024]{1,0:T(8,128)(2,1)} %get-tuple-element.25, ...), custom_call_target="tpu_custom_call" | custom-call | flops 77309411328 | bytes 48234496 | tf_op jit(solution)/shard_map/pallas_call | solution.py:338
  229.7 42.0 %shard_map.201 = (bf16[2,2,2,3,64,384]{5,4,3,2,1,0:T(8,128)(2,1)}, bf16[2,2,2,3,64,384]{5,4,3,2,1,0:T(8,128)(2,1)}, bf16[2,2,3,64,384]{4,3,2,1,0:T(8,128)(2,1)},...) custom-call(bf16[1024,1024]{1,0:T(8,128)(2,1)} %get-tuple-element.25, ...), custom_call_target="tpu_custom_call" | custom-call | flops 115964116992 | bytes 51380224 | tf_op jit(solution)/shard_map/pallas_call | solution.py:338
  279.8 29.7 %shard_map.204 = (bf16[2,2,2,3,64,256]{5,4,3,2,1,0:T(8,128)(2,1)}, bf16[2,2,2,3,64,256]{5,4,3,2,1,0:T(8,128)(2,1)}, bf16[2,2,3,64,256]{4,3,2,1,0:T(8,128)(2,1)},...) custom-call(bf16[1024,1024]{1,0:T(8,128)(2,1)} %get-tuple-element.25, ...), custom_call_target="tpu_custom_call" | custom-call | flops 77309411328 | bytes 48234496 | tf_op jit(solution)/shard_map/pallas_call | solution.py:338
  311.0 3.8 shard_map.209
  316.8 4.6 all-to-all-start.5
  323.6 7.3 %shard_map.207 = (bf16[1024,1024]{1,0:T(8,128)(2,1)}, f32[8,1024]{1,0:T(8,128)}) custom-call(s32[1]{0:T(128)} %bitcast.refs_0_, f32[1024,1024]{1,0:T(8,128)} %get-tuple-element.346.refs_1_, bf16[1024,1024]{1,0:T(8,128)(2,1)} %collective-permute-done.30.refs_2_, f32[1024,1024]{1,0:T(8,128)} %get-tuple-element.245.refs_3_.refs_1_, ...), custom_call_target="tpu_custom_call" | custom-call | flops 20971520 | bytes 12582912 | tf_op jit(solution)/shard_map/pallas_call | solution.py:638
  331.0 20.9 %shard_map.208 = (bf16[4,4,4,64,256]{4,3,2,1,0:T(8,128)(2,1)}, bf16[4,4,4,64,256]{4,3,2,1,0:T(8,128)(2,1)}, f32[8,512]{1,0:T(8,128)}, f32[1024,1024]{1,0:T(8,128)}) custom-call(s32[1]{0:T(128)} %dynamic_slice.9.refs_1_.refs_0_, bf16[1024,1024]{1,0:T(8,128)(2,1)} %get-tuple-element.230.refs_1_, bf16[1024,1024]{1,0:T(8,128)(2,1)} %get-tuple-element.348.refs_2_.refs_3_, ...), custom_call_target="tpu_custom_call" | custom-call | flops 34359738368 | bytes 23068672 | tf_op jit(solution)/shard_map/pallas_call | solution.py:573
  354.0 4.7 shard_map.212
  360.7 4.9 all-to-all-start.6
  367.8 22.1 %shard_map.211 = (bf16[4,4,4,64,256]{4,3,2,1,0:T(8,128)(2,1)}, bf16[4,4,4,64,256]{4,3,2,1,0:T(8,128)(2,1)}, f32[8,512]{1,0:T(8,128)}, f32[1024,1024]{1,0:T(8,128)}) custom-call(s32[1]{0:T(128)} %dynamic_slice.9.refs_1_.refs_0_, bf16[1024,1024]{1,0:T(8,128)(2,1)} %get-tuple-element.230.refs_1_, ...), custom_call_target="tpu_custom_call", output_to_operand_aliasing={{3}: (7, {})} | custom-call | flops 34359738368 | bytes 23068672 | tf_op jit(solution)/shard_map/pallas_call | solution.py:573
  393.0 6.6 %shard_map.216 = (bf16[4,2,3,64,384]{4,3,2,1,0:T(8,128)(2,1)}, bf16[2,2,3,64,256]{4,3,2,1,0:T(8,128)(2,1)}, bf16[2,2,3,64,256]{4,3,2,1,0:T(8,128)(2,1)}, bf16[2,...) custom-call(bf16[4,2,3,64,384]{4,3,2,1,0:T(8,128)(2,1)} %get-tuple-e, ...), custom_call_target="tpu_custom_call" | custom-call | bytes 22544384 | tf_op jit(solution)/shard_map/pallas_call | solution.py:118
  399.6 5.3 %all-to-all-start.9 = ((bf16[4,2,3,64,384]{4,3,2,1,0:T(8,128)(2,1)}), bf16[4,2,3,64,384]{4,3,2,1,0:T(8,128)(2,1)}, u32[]{:S(2)}, u32[]{:S(2)}) async-start(bf16[4,2,3,64,384]{4,3,2,1,0:T(8,128)(2,1)} %get-tuple-element.443), calls=%async_computation.9 | async-start | bytes 2359296 | tf_op jit(solution)/shard_map/all_to_all | solution.py:49
  418.4 7.6 %shard_map.215 = (f32[1024,1024]{1,0:T(8,128)}, f32[8,1024]{1,0:T(8,128)}) custom-call(s32[1]{0:T(128)} %bitcast.refs_0_, f32[1024,1024]{1,0:T(8,128)} %get-tuple-element.389.refs_1_, bf16[1024,1024]{1,0:T(8,128)(2,1)} %get-tuple-element.231.refs_2_, bf16[1024,1024]{1,0:T(8,128)(2,1)} %get-tuple-element.348.refs_2_.refs_3_, f32[1,1024]{1,0:T(1,128)} %reshape.202.refs_4_), custom_call_target="tpu_custom_call" | custom-call | flops 20971520 | bytes 12582912 | tf_op jit(solution)/shard_map/pallas_call | solution.py:638
  430.1 5.2 %shard_map.218 = (bf16[2,2,4,64,256]{4,3,2,1,0:T(8,128)(2,1)}, bf16[2,2,4,64,256]{4,3,2,1,0:T(8,128)(2,1)}, bf16[2,4,64,256]{3,2,1,0:T(8,128)(2,1)}, bf16[2,4,64...) custom-call(bf16[4,4,4,64,256]{4,3,2,1,0:T(8,128)(2,1)} %get-tuple-e, ...), custom_call_target="tpu_custom_call" | custom-call | bytes 17825792 | tf_op jit(solution)/shard_map/pallas_call | solution.py:118
  435.3 4.8 all-to-all-start.10
  447.7 6.5 %shard_map.214.refs_0_ = bf16[1024,1024]{1,0:T(8,128)(2,1)} custom-call(s32[1]{0:T(128)} %bitcast.refs_0_, f32[1024,1024]{1,0:T(8,128)} %get-tuple-element.245.refs_3_.refs_1_, f32[1024,1024]{1,0:T(8,128)} %get-tuple-element.345.refs_2_, bf16[1024,1024]{1,0:T(8,128)(2,1)} %get-tuple-element.388.refs_3_), custom_call_target="tpu_custom_call" | custom-call | flops 20971520 | bytes 12582912 | tf_op jit(solution)/shard_map/pallas_call | solution.py:638
  454.3 5.6 %collective-permute-done.47 = f32[5,1024]{1,0:T(8,128)S(1)} collective-permute-done((f32[5,1024]{1,0:T(8,128)S(1)}, f32[5,1024]{1,0:T(8,128)S(1)}, u32[]{:S(2)}, u32[]{:S(2)}) %collective-permute-start.47) | collective-permute-done | bytes 20512 | tf_op jit(solution)/shard_map/ppermute | solution.py:45
  473.6 4.8 all-to-all-start.7
  484.6 4.2 all-to-all-done.7
  494.6 8.0 %all-to-all-done.8 = bf16[4,4,64,256]{3,2,1,0:T(8,128)(2,1)S(1)} async-done(((bf16[4,4,64,256]{3,2,1,0:T(8,128)(2,1)}), bf16[4,4,64,256]{3,2,1,0:T(8,128)(2,1)S(1)}, u32[]{:S(2)}, u32[]{:S(2)}) %all-to-all-start.8) | async-done | bytes 524320 | tf_op jit(solution)/shard_map/all_to_all | solution.py:49
  (328 shorter events, 149.0 us)
Async XLA Ops:
  3.8 32.2 %all-to-all-start = ((bf16[4,4,64,512]{3,2,1,0:T(8,128)(2,1)}), bf16[4,4,64,512]{3,2,1,0:T(8,128)(2,1)S(1)}, u32[]{:S(2)}, u32[]{:S(2)}) async-start(bf16[4,4,64,512]{3,2,1,0:T(8,128)(2,1)} %broadcast_in_dim.65.refs_2_), calls=%async_computation | async-start | bytes 2097152 | tf_op jit(solution)/shard_map/all_to_all | solution.py:49
  96.1 50.1 %collective-permute-start.11 = (bf16[1024,1024]{1,0:T(8,128)(2,1)}, bf16[1024,1024]{1,0:T(8,128)(2,1)}, u32[]{:S(2)}, u32[]{:S(2)}) collective-permute-start(bf16[1024,1024]{1,0:T(8,128)(2,1)} %get-tuple-element.255), channel_id=1, source_target_pairs={{0,2},{1,3},{2,0},{3,1},{4,6},{5,7},{6,4},{7,5},{8,10},{9,11},{10,... | collective-permute-start | bytes 6291464 | tf_op jit(solution)/shard_map/ppermute | solution.py:45
  96.6 32.8 %collective-permute-start.6 = (bf16[4,2,3,64,256]{4,3,2,1,0:T(8,128)(2,1)S(1)}, bf16[4,2,3,64,256]{4,3,2,1,0:T(8,128)(2,1)S(1)}, u32[]{:S(2)}, u32[]{:S(2)}) collective-permute-start(bf16[4,2,3,64,256]{4,3,2,1,0:T(8,128)(2,1)S(1)} %copy-done.14), channel_id=1, source_target_pairs={{0,4},{1,5},{2,6},{3,7},{4,0},{5,1},{6,2},{7,3},{8,12},{9,13},{10,... | collective-permute-start | bytes 2359304 | tf_op jit(solution)/shard_map/ppermute | solution.py:45
  97.6 31.8 %collective-permute-start.7 = (bf16[4,2,3,64,256]{4,3,2,1,0:T(8,128)(2,1)S(1)}, bf16[4,2,3,64,256]{4,3,2,1,0:T(8,128)(2,1)}, u32[]{:S(2)}, u32[]{:S(2)}) collective-permute-start(bf16[4,2,3,64,256]{4,3,2,1,0:T(8,128)(2,1)S(1)} %copy-done.14), channel_id=1, source_target_pairs={{0,1},{1,0},{2,3},{3,2},{4,5},{5,4},{6,7},{7,6},{8,9},{9,8},{10,11... | collective-permute-start | bytes 2359304 | tf_op jit(solution)/shard_map/ppermute | solution.py:45
  99.1 33.9 %collective-permute-start.8 = (bf16[4,2,3,64,256]{4,3,2,1,0:T(8,128)(2,1)}, bf16[4,2,3,64,256]{4,3,2,1,0:T(8,128)(2,1)}, u32[]{:S(2)}, u32[]{:S(2)}) collective-permute-start(bf16[4,2,3,64,256]{4,3,2,1,0:T(8,128)(2,1)} %get-tuple-element.250.refs_4_), channel_id=1, source_target_pairs={{0,4},{1,5},{2,6},{3,7},{4,0},{5,1},{6,2},{7,3},{8,12},{9,13},{10,... | collective-permute-start | bytes 2359304 | tf_op jit(solution)/shard_map/ppermute | solution.py:45
  100.2 33.6 %all-to-all-start.3 = ((bf16[4,2,3,64,384]{4,3,2,1,0:T(8,128)(2,1)}), bf16[4,2,3,64,384]{4,3,2,1,0:T(8,128)(2,1)S(1)}, u32[]{:S(2)}, u32[]{:S(2)}) async-start(bf16[4,2,3,64,384]{4,3,2,1,0:T(8,128)(2,1)} %get-tuple-element.251), calls=%async_computation.3 | async-start | bytes 2359296 | tf_op jit(solution)/shard_map/all_to_all | solution.py:49
  139.5 44.2 %collective-permute-start.16 = (bf16[4,2,3,64,384]{4,3,2,1,0:T(8,128)(2,1)}, bf16[4,2,3,64,384]{4,3,2,1,0:T(8,128)(2,1)S(1)}, u32[]{:S(2)}, u32[]{:S(2)}) collective-permute-start(bf16[4,2,3,64,384]{4,3,2,1,0:T(8,128)(2,1)} %get-tuple-element.273.refs_4_), channel_id=1, source_target_pairs={{0,4},{1,5},{2,6},{3,7},{4,0},{5,1},{6,2},{7,3},{8,12},{9,13},{10,... | collective-permute-start | bytes 3538952 | tf_op jit(solution)/shard_map/ppermute | solution.py:45
  140.4 43.3 %all-to-all-start.4 = ((bf16[4,2,3,64,256]{4,3,2,1,0:T(8,128)(2,1)}), bf16[4,2,3,64,256]{4,3,2,1,0:T(8,128)(2,1)S(1)}, u32[]{:S(2)}, u32[]{:S(2)}) async-start(bf16[4,2,3,64,256]{4,3,2,1,0:T(8,128)(2,1)} %get-tuple-element.274), calls=%async_computation.4 | async-start | bytes 1572864 | tf_op jit(solution)/shard_map/all_to_all | solution.py:49
  146.2 37.5 %collective-permute-start.17 = (bf16[4,2,3,64,384]{4,3,2,1,0:T(8,128)(2,1)S(1)}, bf16[4,2,3,64,384]{4,3,2,1,0:T(8,128)(2,1)}, u32[]{:S(2)}, u32[]{:S(2)}) collective-permute-start(bf16[4,2,3,64,384]{4,3,2,1,0:T(8,128)(2,1)S(1)} %copy-done.16), channel_id=1, source_target_pairs={{0,1},{1,0},{2,3},{3,2},{4,5},{5,4},{6,7},{7,6},{8,9},{9,8},{10,11... | collective-permute-start | bytes 3538952 | tf_op jit(solution)/shard_map/ppermute | solution.py:45
  148.8 33.5 %collective-permute-start.14 = (bf16[2,2,3,64,256]{4,3,2,1,0:T(8,128)(2,1)}, bf16[2,2,3,64,256]{4,3,2,1,0:T(8,128)(2,1)S(1)}, u32[]{:S(2)}, u32[]{:S(2)}) collective-permute-start(bf16[2,2,3,64,256]{4,3,2,1,0:T(8,128)(2,1)} %get-tuple-element.271), channel_id=1, source_target_pairs={{0,1},{1,0},{2,3},{3,2},{4,5},{5,4},{6,7},{7,6},{8,9},{9,8},{10,11... | collective-permute-start | bytes 1179656 | tf_op jit(solution)/shard_map/ppermute | solution.py:45
  150.7 33.0 %collective-permute-start.15 = (bf16[2,2,3,64,256]{4,3,2,1,0:T(8,128)(2,1)}, bf16[2,2,3,64,256]{4,3,2,1,0:T(8,128)(2,1)}, u32[]{:S(2)}, u32[]{:S(2)}) collective-permute-start(bf16[2,2,3,64,256]{4,3,2,1,0:T(8,128)(2,1)} %get-tuple-element.272), channel_id=1, source_target_pairs={{0,4},{1,5},{2,6},{3,7},{4,0},{5,1},{6,2},{7,3},{8,12},{9,13},{10,... | collective-permute-start | bytes 1179656 | tf_op jit(solution)/shard_map/ppermute | solution.py:45
  185.0 37.0 %collective-permute-start.20 = (bf16[4,2,3,64,256]{4,3,2,1,0:T(8,128)(2,1)}, bf16[4,2,3,64,256]{4,3,2,1,0:T(8,128)(2,1)S(1)}, u32[]{:S(2)}, u32[]{:S(2)}) collective-permute-start(bf16[4,2,3,64,256]{4,3,2,1,0:T(8,128)(2,1)} %get-tuple-element.275.refs_4_), channel_id=1, source_target_pairs={{0,4},{1,5},{2,6},{3,7},{4,0},{5,1},{6,2},{7,3},{8,12},{9,13},{10,... | collective-permute-start | bytes 2359304 | tf_op jit(solution)/shard_map/ppermute | solution.py:45
  186.1 36.0 %collective-permute-start.21 = (bf16[4,2,3,64,256]{4,3,2,1,0:T(8,128)(2,1)}, bf16[4,2,3,64,256]{4,3,2,1,0:T(8,128)(2,1)S(1)}, u32[]{:S(2)}, u32[]{:S(2)}) collective-permute-start(bf16[4,2,3,64,256]{4,3,2,1,0:T(8,128)(2,1)} %get-tuple-element.275.refs_4_), channel_id=1, source_target_pairs={{0,1},{1,0},{2,3},{3,2},{4,5},{5,4},{6,7},{7,6},{8,9},{9,8},{10,11... | collective-permute-start | bytes 2359304 | tf_op jit(solution)/shard_map/ppermute | solution.py:45
  190.1 31.8 %collective-permute-start.18 = (bf16[2,2,3,64,384]{4,3,2,1,0:T(8,128)(2,1)}, bf16[2,2,3,64,384]{4,3,2,1,0:T(8,128)(2,1)S(1)}, u32[]{:S(2)}, u32[]{:S(2)}) collective-permute-start(bf16[2,2,3,64,384]{4,3,2,1,0:T(8,128)(2,1)} %get-tuple-element.295), channel_id=1, source_target_pairs={{0,1},{1,0},{2,3},{3,2},{4,5},{5,4},{6,7},{7,6},{8,9},{9,8},{10,11... | collective-permute-start | bytes 1769480 | tf_op jit(solution)/shard_map/ppermute | solution.py:45
  191.2 30.8 %collective-permute-start.19 = (bf16[2,2,3,64,384]{4,3,2,1,0:T(8,128)(2,1)}, bf16[2,2,3,64,384]{4,3,2,1,0:T(8,128)(2,1)S(1)}, u32[]{:S(2)}, u32[]{:S(2)}) collective-permute-start(bf16[2,2,3,64,384]{4,3,2,1,0:T(8,128)(2,1)} %get-tuple-element.296), channel_id=1, source_target_pairs={{0,4},{1,5},{2,6},{3,7},{4,0},{5,1},{6,2},{7,3},{8,12},{9,13},{10,... | collective-permute-start | bytes 1769480 | tf_op jit(solution)/shard_map/ppermute | solution.py:45
  225.6 46.1 %collective-permute-start.22 = (bf16[2,2,3,64,256]{4,3,2,1,0:T(8,128)(2,1)}, bf16[2,2,3,64,256]{4,3,2,1,0:T(8,128)(2,1)S(1)}, u32[]{:S(2)}, u32[]{:S(2)}) collective-permute-start(bf16[2,2,3,64,256]{4,3,2,1,0:T(8,128)(2,1)} %get-tuple-element.316), channel_id=1, source_target_pairs={{0,1},{1,0},{2,3},{3,2},{4,5},{5,4},{6,7},{7,6},{8,9},{9,8},{10,11... | collective-permute-start | bytes 1179656 | tf_op jit(solution)/shard_map/ppermute | solution.py:45
  226.5 45.2 %collective-permute-start.23 = (bf16[2,2,3,64,256]{4,3,2,1,0:T(8,128)(2,1)}, bf16[2,2,3,64,256]{4,3,2,1,0:T(8,128)(2,1)S(1)}, u32[]{:S(2)}, u32[]{:S(2)}) collective-permute-start(bf16[2,2,3,64,256]{4,3,2,1,0:T(8,128)(2,1)} %get-tuple-element.317), channel_id=1, source_target_pairs={{0,4},{1,5},{2,6},{3,7},{4,0},{5,1},{6,2},{7,3},{8,12},{9,13},{10,... | collective-permute-start | bytes 1179656 | tf_op jit(solution)/shard_map/ppermute | solution.py:45
  227.6 44.2 %collective-permute-start.24 = (bf16[2,2,2,3,64,256]{5,4,3,2,1,0:T(8,128)(2,1)}, bf16[2,2,2,3,64,256]{5,4,3,2,1,0:T(8,128)(2,1)S(1)}, u32[]{:S(2)}, u32[]{:S(2)}) collective-permute-start(bf16[2,2,2,3,64,256]{5,4,3,2,1,0:T(8,128)(2,1)} %get-tuple-element.318), channel_id=1, source_target_pairs={{0,4},{1,5},{2,6},{3,7},{4,0},{5,1},{6,2},{7,3},{8,12},{9,13},{10,... | collective-permute-start | bytes 2359304 | tf_op jit(solution)/shard_map/ppermute | solution.py:45
  228.6 43.2 %collective-permute-start.25 = (bf16[2,2,2,3,64,256]{5,4,3,2,1,0:T(8,128)(2,1)}, bf16[2,2,2,3,64,256]{5,4,3,2,1,0:T(8,128)(2,1)S(1)}, u32[]{:S(2)}, u32[]{:S(2)}) collective-permute-start(bf16[2,2,2,3,64,256]{5,4,3,2,1,0:T(8,128)(2,1)} %get-tuple-element.319), channel_id=1, source_target_pairs={{0,1},{1,0},{2,3},{3,2},{4,5},{5,4},{6,7},{7,6},{8,9},{9,8},{10,11... | collective-permute-start | bytes 2359304 | tf_op jit(solution)/shard_map/ppermute | solution.py:45
  275.8 33.8 %collective-permute-start.26 = (bf16[2,2,3,64,256]{4,3,2,1,0:T(8,128)(2,1)}, bf16[2,2,3,64,256]{4,3,2,1,0:T(8,128)(2,1)S(1)}, u32[]{:S(2)}, u32[]{:S(2)}) collective-permute-start(bf16[2,2,3,64,256]{4,3,2,1,0:T(8,128)(2,1)} %get-tuple-element.341), channel_id=1, source_target_pairs={{0,4},{1,5},{2,6},{3,7},{4,0},{5,1},{6,2},{7,3},{8,12},{9,13},{10,... | collective-permute-start | bytes 1179656 | tf_op jit(solution)/shard_map/ppermute | solution.py:45
  276.8 32.8 %collective-permute-start.27 = (bf16[2,2,3,64,256]{4,3,2,1,0:T(8,128)(2,1)}, bf16[2,2,3,64,256]{4,3,2,1,0:T(8,128)(2,1)S(1)}, u32[]{:S(2)}, u32[]{:S(2)}) collective-permute-start(bf16[2,2,3,64,256]{4,3,2,1,0:T(8,128)(2,1)} %get-tuple-element.342), channel_id=1, source_target_pairs={{0,1},{1,0},{2,3},{3,2},{4,5},{5,4},{6,7},{7,6},{8,9},{9,8},{10,11... | collective-permute-start | bytes 1179656 | tf_op jit(solution)/shard_map/ppermute | solution.py:45
  277.8 31.9 %collective-permute-start.28 = (bf16[2,2,2,3,64,256]{5,4,3,2,1,0:T(8,128)(2,1)S(1)}, bf16[2,2,2,3,64,256]{5,4,3,2,1,0:T(8,128)(2,1)S(1)}, u32[]{:S(2)}, u32[]{:S(2)}) collective-permute-start(bf16[2,2,2,3,64,256]{5,4,3,2,1,0:T(8,128)(2,1)S(1)} %copy-done.22), channel_id=1, source_target_pairs={{0,4},{1,5},{2,6},{3,7},{4,0},{5,1},{6,2},{7,3},{8,12},{9,13},{10,... | collective-permute-start | bytes 2359304 | tf_op jit(solution)/shard_map/ppermute | solution.py:45
  278.7 30.9 %collective-permute-start.29 = (bf16[2,2,2,3,64,256]{5,4,3,2,1,0:T(8,128)(2,1)S(1)}, bf16[2,2,2,3,64,256]{5,4,3,2,1,0:T(8,128)(2,1)S(1)}, u32[]{:S(2)}, u32[]{:S(2)}) collective-permute-start(bf16[2,2,2,3,64,256]{5,4,3,2,1,0:T(8,128)(2,1)S(1)} %copy-done.23), channel_id=1, source_target_pairs={{0,1},{1,0},{2,3},{3,2},{4,5},{5,4},{6,7},{7,6},{8,9},{9,8},{10,11... | collective-permute-start | bytes 2359304 | tf_op jit(solution)/shard_map/ppermute | solution.py:45
  314.8 37.0 %collective-permute-start.32 = (bf16[2,2,3,64,256]{4,3,2,1,0:T(8,128)(2,1)}, bf16[2,2,3,64,256]{4,3,2,1,0:T(8,128)(2,1)}, u32[]{:S(2)}, u32[]{:S(2)}) collective-permute-start(bf16[2,2,3,64,256]{4,3,2,1,0:T(8,128)(2,1)} %get-tuple-element.365), channel_id=1, source_target_pairs={{0,4},{1,5},{2,6},{3,7},{4,0},{5,1},{6,2},{7,3},{8,12},{9,13},{10,... | collective-permute-start | bytes 1179656 | tf_op jit(solution)/shard_map/ppermute | solution.py:45
  315.8 36.0 %collective-permute-start.33 = (bf16[2,2,3,64,256]{4,3,2,1,0:T(8,128)(2,1)}, bf16[2,2,3,64,256]{4,3,2,1,0:T(8,128)(2,1)}, u32[]{:S(2)}, u32[]{:S(2)}) collective-permute-start(bf16[2,2,3,64,256]{4,3,2,1,0:T(8,128)(2,1)} %get-tuple-element.366), channel_id=1, source_target_pairs={{0,1},{1,0},{2,3},{3,2},{4,5},{5,4},{6,7},{7,6},{8,9},{9,8},{10,11... | collective-permute-start | bytes 1179656 | tf_op jit(solution)/shard_map/ppermute | solution.py:45
  316.8 35.1 %all-to-all-start.5 = ((bf16[4,2,3,64,256]{4,3,2,1,0:T(8,128)(2,1)}), bf16[4,2,3,64,256]{4,3,2,1,0:T(8,128)(2,1)}, u32[]{:S(2)}, u32[]{:S(2)}) async-start(bf16[4,2,3,64,256]{4,3,2,1,0:T(8,128)(2,1)} %get-tuple-element.364), calls=%async_computation.5 | async-start | bytes 1572864 | tf_op jit(solution)/shard_map/all_to_all | solution.py:49
  321.4 31.3 %collective-permute-start.31 = (bf16[1024,1024]{1,0:T(8,128)(2,1)}, bf16[1024,1024]{1,0:T(8,128)(2,1)S(1)}, u32[]{:S(2)}, u32[]{:S(2)}) collective-permute-start(bf16[1024,1024]{1,0:T(8,128)(2,1)} %get-tuple-element.354), channel_id=1, source_target_pairs={{0,2},{1,3},{2,0},{3,1},{4,6},{5,7},{6,4},{7,5},{8,10},{9,11},{10,... | collective-permute-start | bytes 6291464 | tf_op jit(solution)/shard_map/ppermute | solution.py:45
  358.7 31.2 %collective-permute-start.37 = (bf16[2,2,3,64,384]{4,3,2,1,0:T(8,128)(2,1)}, bf16[2,2,3,64,384]{4,3,2,1,0:T(8,128)(2,1)S(1)}, u32[]{:S(2)}, u32[]{:S(2)}) collective-permute-start(bf16[2,2,3,64,384]{4,3,2,1,0:T(8,128)(2,1)} %get-tuple-element.384), channel_id=1, source_target_pairs={{0,4},{1,5},{2,6},{3,7},{4,0},{5,1},{6,2},{7,3},{8,12},{9,13},{10,... | collective-permute-start | bytes 1769480 | tf_op jit(solution)/shard_map/ppermute | solution.py:45
  360.7 30.7 %all-to-all-start.6 = ((bf16[4,2,3,64,256]{4,3,2,1,0:T(8,128)(2,1)}), bf16[4,2,3,64,256]{4,3,2,1,0:T(8,128)(2,1)S(1)}, u32[]{:S(2)}, u32[]{:S(2)}) async-start(bf16[4,2,3,64,256]{4,3,2,1,0:T(8,128)(2,1)} %get-tuple-element.383), calls=%async_computation.6 | async-start | bytes 1572864 | tf_op jit(solution)/shard_map/all_to_all | solution.py:49
  393.0 35.5 %collective-permute-start.41 = (bf16[4,4,4,64,256]{4,3,2,1,0:T(8,128)(2,1)}, bf16[4,4,4,64,256]{4,3,2,1,0:T(8,128)(2,1)S(1)}, u32[]{:S(2)}, u32[]{:S(2)}) collective-permute-start(bf16[4,4,4,64,256]{4,3,2,1,0:T(8,128)(2,1)} %get-tuple-element.393), channel_id=1, source_target_pairs={{0,2},{1,3},{2,0},{3,1},{4,6},{5,7},{6,4},{7,5},{8,10},{9,11},{10,... | collective-permute-start | bytes 6291464 | tf_op jit(solution)/shard_map/ppermute | solution.py:45
  399.6 35.8 %all-to-all-start.9 = ((bf16[4,2,3,64,384]{4,3,2,1,0:T(8,128)(2,1)}), bf16[4,2,3,64,384]{4,3,2,1,0:T(8,128)(2,1)}, u32[]{:S(2)}, u32[]{:S(2)}) async-start(bf16[4,2,3,64,384]{4,3,2,1,0:T(8,128)(2,1)} %get-tuple-element.443), calls=%async_computation.9 | async-start | bytes 2359296 | tf_op jit(solution)/shard_map/all_to_all | solution.py:49
  435.3 38.2 %all-to-all-start.10 = ((bf16[4,2,3,64,256]{4,3,2,1,0:T(8,128)(2,1)}), bf16[4,2,3,64,256]{4,3,2,1,0:T(8,128)(2,1)S(1)}, u32[]{:S(2)}, u32[]{:S(2)}) async-start(bf16[4,2,3,64,256]{4,3,2,1,0:T(8,128)(2,1)} %get-tuple-element.444), calls=%async_computation.10 | async-start | bytes 1572864 | tf_op jit(solution)/shard_map/all_to_all | solution.py:49
  (97 other events, 867.7 us)

commit v7 on v6

--- a/solution.py
+++ b/solution.py
@@ -873,7 +873,7 @@
         if p:
             places = [start("sum core", names[0])]
         if p == parts - 1:
-            places += add(("sum z", last - 2), ("sum sides", last - 1), ("sum corner", last))
+            places += add(("sum z", last - 2), ("sum sides", last - 1), ("sum corner", last))[1:]
         keep, send, tap_grads, grad_normed = mixer_back(
             own_lengths, normed, grad_mix, project, conv, mixer_cells, grad_normed, [],
             tile, p, parts,

time: 515 us -> 517 us (level)
    unnamed x118 -> x116, local copies, waits for them, and re-layouts: 16.8 us -> 16.6 us
where the time goes in v7:
time: 517 us; the launch traced here: 508 us
  Pallas kernels  273 us (53%)
  starting transfers between devices  104 us (20%)
  waiting for transfers between devices  76.5 us (15%)
  local copies, waits for them, and re-layouts  35 us (7%)
  other arithmetic  17.4 us (3%)
    pallas_call x4, Pallas kernels, ffn_piece(): pl.pallas_call(functools.partial(ffn_kernel, first, last, len(ties)), gri...  129 us
    ppermute x59, starting transfers between devices, swap(): return lax.ppermute(value, AXES, pairs)  54.4 us
    ppermute x59, waiting for transfers between devices, swap(): return lax.ppermute(value, AXES, pairs)  53.5 us
    all_to_all x11, starting transfers between devices, turn_z(): lax.all_to_all(value, 'dp', 0, 0, axis_index_groups=groups, tiled=True)  49.7 us
    pallas_call x2, Pallas kernels, mixer_back(): pl.pallas_call(functools.partial(mixer_back_kernel, first, len(ties), min...  43 us
    pallas_call x8, Pallas kernels, small_calls(): pl.pallas_call(body, grid=(max(tiles),), in_specs=[spec(item.shape, count...  33 us
    pallas_call x4, Pallas kernels, row_call(): pl.pallas_call(body, grid=(rows // height,), in_specs=[scalar] + specs +...  30 us
    pallas_call x1, Pallas kernels, mixer_part(): pl.pallas_call(functools.partial(mixer_kernel, first, last, len(ties), mi...  25 us
  transfers between devices with their start and end apart: 70, of which 19 were waited for; matrix products, arithmetic and copies ran while one was open for 6% of the time, Pallas kernels for 51%

profile of v7, /device:TPU:0, one launch (start us, length us, event | category | flops | bytes accessed | tf_op | source)
XLA Modules:
  0.0 507.8 jit_solution(1341367527437407264)
XLA Ops:
  3.8 6.4 %all-to-all-start = ((bf16[4,4,64,512]{3,2,1,0:T(8,128)(2,1)}), bf16[4,4,64,512]{3,2,1,0:T(8,128)(2,1)S(1)}, u32[]{:S(2)}, u32[]{:S(2)}) async-start(bf16[4,4,64,512]{3,2,1,0:T(8,128)(2,1)} %broadcast_in_dim.65.refs_2_), calls=%async_computation | async-start | bytes 2097152 | tf_op jit(solution)/shard_map/all_to_all | solution.py:49
  18.6 8.5 %shard_map.186 = (bf16[1024,1024]{1,0:T(8,128)(2,1)}, bf16[1024,1024]{1,0:T(8,128)(2,1)}, bf16[1024,1024]{1,0:T(8,128)(2,1)}, bf16[1024,1024]{1,0:T(8,128)(2,1)}) custom-call(s32[1]{0:T(128)} %bitcast.refs_0_, s32[1]{0:T(128)} %dynamic_slice.9.refs_1_.refs_0_, bf16[1024,1024]{1,0:T(8,128)(2,1)} %refs_2_.1, bf16[1024,1024]{1,0:T(8,128)(2,1)} %refs_3_.1, ...), custom_call_target="tpu_custom_call" | custom-call | flops 20971520 | bytes 12582912 | tf_op jit(solution)/shard_map/pallas_call | solution.py:638
  27.1 8.9 %all-to-all-done.refs_7_ = bf16[4,4,64,512]{3,2,1,0:T(8,128)(2,1)S(1)} async-done(((bf16[4,4,64,512]{3,2,1,0:T(8,128)(2,1)}), bf16[4,4,64,512]{3,2,1,0:T(8,128)(2,1)S(1)}, u32[]{:S(2)}, u32[]{:S(2)}) %all-to-all-start) | async-done | bytes 1048608 | tf_op jit(solution)/shard_map/all_to_all | solution.py:49
  43.6 21.3 %collective-permute-done.1.refs_2_ = bf16[4,4,64,512]{3,2,1,0:T(8,128)(2,1)S(1)} collective-permute-done((bf16[4,4,64,512]{3,2,1,0:T(8,128)(2,1)}, bf16[4,4,64,512]{3,2,1,0:T(8,128)(2,1)S(1)}, u32[]{:S(2)}, u32[]{:S(2)}) %collective-permute-start.1) | collective-permute-done | bytes 1048608 | tf_op jit(solution)/shard_map/ppermute | solution.py:45
  67.4 4.7 all-to-all-start.2
  77.7 9.2 %collective-permute-done.3.refs_2_ = bf16[2,4,64,512]{3,2,1,0:T(8,128)(2,1)S(1)} collective-permute-done((bf16[2,4,64,512]{3,2,1,0:T(8,128)(2,1)}, bf16[2,4,64,512]{3,2,1,0:T(8,128)(2,1)S(1)}, u32[]{:S(2)}, u32[]{:S(2)}) %collective-permute-start.3) | collective-permute-done | bytes 524320 | tf_op jit(solution)/shard_map/ppermute | solution.py:45
  90.1 4.8 shard_map.191.refs_5_
  100.2 3.5 all-to-all-start.3
  104.4 25.0 %shard_map.192 = (f32[3,1024,1024]{2,1,0:T(8,128)}, f32[1024,1024]{1,0:T(8,128)}, bf16[1024,1024]{1,0:T(8,128)(2,1)}, bf16[1024,1024]{1,0:T(8,128)(2,1)}) custom-call(s32[1]{0:T(128)} %dynamic_slice.9.refs_1_.refs_0_, bf16[1024,1024]{1,0:T(8,128)(2,1)} %get-tuple-element.229.refs_1_, bf16[1024,1024]{1,0:T(8,128)(2,1)} %get-tuple-element.230.refs_2_, ...), custom_call_target="tpu_custom_call" | custom-call | flops 34359738368 | bytes 29360128 | tf_op jit(solution)/shard_map/pallas_call | solution.py:466
  129.4 3.7 collective-permute-done.8.refs_5_
  140.4 3.7 all-to-all-start.4
  151.8 27.9 %shard_map.195 = (bf16[2,2,2,3,64,256]{5,4,3,2,1,0:T(8,128)(2,1)}, bf16[2,2,2,3,64,256]{5,4,3,2,1,0:T(8,128)(2,1)}, bf16[2,2,3,64,256]{4,3,2,1,0:T(8,128)(2,1)},...) custom-call(bf16[1024,1024]{1,0:T(8,128)(2,1)} %get-tuple-element.25, ...), custom_call_target="tpu_custom_call" | custom-call | flops 77309411328 | bytes 48234496 | tf_op jit(solution)/shard_map/pallas_call | solution.py:338
  192.2 29.8 %shard_map.198 = (bf16[2,2,2,3,64,256]{5,4,3,2,1,0:T(8,128)(2,1)}, bf16[2,2,2,3,64,256]{5,4,3,2,1,0:T(8,128)(2,1)}, bf16[2,2,3,64,256]{4,3,2,1,0:T(8,128)(2,1)},...) custom-call(bf16[1024,1024]{1,0:T(8,128)(2,1)} %get-tuple-element.25, ...), custom_call_target="tpu_custom_call" | custom-call | flops 77309411328 | bytes 48234496 | tf_op jit(solution)/shard_map/pallas_call | solution.py:338
  229.7 42.0 %shard_map.201 = (bf16[2,2,2,3,64,384]{5,4,3,2,1,0:T(8,128)(2,1)}, bf16[2,2,2,3,64,384]{5,4,3,2,1,0:T(8,128)(2,1)}, bf16[2,2,3,64,384]{4,3,2,1,0:T(8,128)(2,1)},...) custom-call(bf16[1024,1024]{1,0:T(8,128)(2,1)} %get-tuple-element.25, ...), custom_call_target="tpu_custom_call" | custom-call | flops 115964116992 | bytes 51380224 | tf_op jit(solution)/shard_map/pallas_call | solution.py:338
  279.9 29.7 %shard_map.204 = (bf16[2,2,2,3,64,256]{5,4,3,2,1,0:T(8,128)(2,1)}, bf16[2,2,2,3,64,256]{5,4,3,2,1,0:T(8,128)(2,1)}, bf16[2,2,3,64,256]{4,3,2,1,0:T(8,128)(2,1)},...) custom-call(bf16[1024,1024]{1,0:T(8,128)(2,1)} %get-tuple-element.25, ...), custom_call_target="tpu_custom_call" | custom-call | flops 77309411328 | bytes 48234496 | tf_op jit(solution)/shard_map/pallas_call | solution.py:338
  311.1 3.7 shard_map.209
  316.9 4.6 all-to-all-start.5
  323.7 7.4 %shard_map.207 = (bf16[1024,1024]{1,0:T(8,128)(2,1)}, f32[8,1024]{1,0:T(8,128)}) custom-call(s32[1]{0:T(128)} %bitcast.refs_0_, f32[1024,1024]{1,0:T(8,128)} %get-tuple-element.345.refs_1_, bf16[1024,1024]{1,0:T(8,128)(2,1)} %collective-permute-done.30.refs_2_, f32[1024,1024]{1,0:T(8,128)} %get-tuple-element.244.refs_3_.refs_1_, ...), custom_call_target="tpu_custom_call" | custom-call | flops 20971520 | bytes 12582912 | tf_op jit(solution)/shard_map/pallas_call | solution.py:638
  331.0 20.9 %shard_map.208 = (bf16[4,4,4,64,256]{4,3,2,1,0:T(8,128)(2,1)}, bf16[4,4,4,64,256]{4,3,2,1,0:T(8,128)(2,1)}, f32[8,512]{1,0:T(8,128)}, f32[1024,1024]{1,0:T(8,128)}) custom-call(s32[1]{0:T(128)} %dynamic_slice.9.refs_1_.refs_0_, bf16[1024,1024]{1,0:T(8,128)(2,1)} %get-tuple-element.229.refs_1_, bf16[1024,1024]{1,0:T(8,128)(2,1)} %get-tuple-element.347.refs_2_.refs_3_, ...), custom_call_target="tpu_custom_call" | custom-call | flops 34359738368 | bytes 23068672 | tf_op jit(solution)/shard_map/pallas_call | solution.py:573
  354.2 4.7 shard_map.212
  363.0 4.8 all-to-all-start.8
  367.8 22.1 %shard_map.211 = (bf16[4,4,4,64,256]{4,3,2,1,0:T(8,128)(2,1)}, bf16[4,4,4,64,256]{4,3,2,1,0:T(8,128)(2,1)}, f32[8,512]{1,0:T(8,128)}, f32[1024,1024]{1,0:T(8,128)}) custom-call(s32[1]{0:T(128)} %dynamic_slice.9.refs_1_.refs_0_, bf16[1024,1024]{1,0:T(8,128)(2,1)} %get-tuple-element.229.refs_1_, ...), custom_call_target="tpu_custom_call", output_to_operand_aliasing={{3}: (7, {})} | custom-call | flops 34359738368 | bytes 23068672 | tf_op jit(solution)/shard_map/pallas_call | solution.py:573
  392.9 6.6 %shard_map.216 = (bf16[4,2,3,64,384]{4,3,2,1,0:T(8,128)(2,1)}, bf16[2,2,3,64,256]{4,3,2,1,0:T(8,128)(2,1)}, bf16[2,2,3,64,256]{4,3,2,1,0:T(8,128)(2,1)}, bf16[2,...) custom-call(bf16[4,2,3,64,384]{4,3,2,1,0:T(8,128)(2,1)} %get-tuple-e, ...), custom_call_target="tpu_custom_call" | custom-call | bytes 22544384 | tf_op jit(solution)/shard_map/pallas_call | solution.py:118
  399.5 5.3 %all-to-all-start.9 = ((bf16[4,2,3,64,384]{4,3,2,1,0:T(8,128)(2,1)}), bf16[4,2,3,64,384]{4,3,2,1,0:T(8,128)(2,1)}, u32[]{:S(2)}, u32[]{:S(2)}) async-start(bf16[4,2,3,64,384]{4,3,2,1,0:T(8,128)(2,1)} %get-tuple-element.441), calls=%async_computation.9 | async-start | bytes 2359296 | tf_op jit(solution)/shard_map/all_to_all | solution.py:49
  418.3 7.6 %shard_map.215 = (f32[1024,1024]{1,0:T(8,128)}, f32[8,1024]{1,0:T(8,128)}) custom-call(s32[1]{0:T(128)} %bitcast.refs_0_, f32[1024,1024]{1,0:T(8,128)} %get-tuple-element.387.refs_1_, bf16[1024,1024]{1,0:T(8,128)(2,1)} %get-tuple-element.230.refs_2_, bf16[1024,1024]{1,0:T(8,128)(2,1)} %get-tuple-element.347.refs_2_.refs_3_, f32[1,1024]{1,0:T(1,128)} %reshape.202.refs_4_), custom_call_target="tpu_custom_call" | custom-call | flops 20971520 | bytes 12582912 | tf_op jit(solution)/shard_map/pallas_call | solution.py:638
  430.0 5.2 %shard_map.218 = (bf16[2,2,4,64,256]{4,3,2,1,0:T(8,128)(2,1)}, bf16[2,2,4,64,256]{4,3,2,1,0:T(8,128)(2,1)}, bf16[2,4,64,256]{3,2,1,0:T(8,128)(2,1)}, bf16[2,4,64...) custom-call(bf16[4,4,4,64,256]{4,3,2,1,0:T(8,128)(2,1)} %get-tuple-e, ...), custom_call_target="tpu_custom_call" | custom-call | bytes 17825792 | tf_op jit(solution)/shard_map/pallas_call | solution.py:118
  435.1 4.8 all-to-all-start.10
  447.5 6.5 %shard_map.214.refs_0_ = bf16[1024,1024]{1,0:T(8,128)(2,1)} custom-call(s32[1]{0:T(128)} %bitcast.refs_0_, f32[1024,1024]{1,0:T(8,128)} %get-tuple-element.244.refs_3_.refs_1_, f32[1024,1024]{1,0:T(8,128)} %get-tuple-element.344.refs_2_, bf16[1024,1024]{1,0:T(8,128)(2,1)} %get-tuple-element.386.refs_3_), custom_call_target="tpu_custom_call" | custom-call | flops 20971520 | bytes 12582912 | tf_op jit(solution)/shard_map/pallas_call | solution.py:638
  454.0 5.7 %collective-permute-done.47 = f32[5,1024]{1,0:T(8,128)S(1)} collective-permute-done((f32[5,1024]{1,0:T(8,128)S(1)}, f32[5,1024]{1,0:T(8,128)S(1)}, u32[]{:S(2)}, u32[]{:S(2)}) %collective-permute-start.47) | collective-permute-done | bytes 20512 | tf_op jit(solution)/shard_map/ppermute | solution.py:45
  474.6 4.8 all-to-all-start.6
  485.6 4.2 all-to-all-done.6
  495.6 8.0 %all-to-all-done.7 = bf16[4,4,64,256]{3,2,1,0:T(8,128)(2,1)S(1)} async-done(((bf16[4,4,64,256]{3,2,1,0:T(8,128)(2,1)}), bf16[4,4,64,256]{3,2,1,0:T(8,128)(2,1)S(1)}, u32[]{:S(2)}, u32[]{:S(2)}) %all-to-all-start.7) | async-done | bytes 524320 | tf_op jit(solution)/shard_map/all_to_all | solution.py:49
  (326 shorter events, 149.9 us)
Async XLA Ops:
  3.8 32.2 %all-to-all-start = ((bf16[4,4,64,512]{3,2,1,0:T(8,128)(2,1)}), bf16[4,4,64,512]{3,2,1,0:T(8,128)(2,1)S(1)}, u32[]{:S(2)}, u32[]{:S(2)}) async-start(bf16[4,4,64,512]{3,2,1,0:T(8,128)(2,1)} %broadcast_in_dim.65.refs_2_), calls=%async_computation | async-start | bytes 2097152 | tf_op jit(solution)/shard_map/all_to_all | solution.py:49
  96.2 50.0 %collective-permute-start.11 = (bf16[1024,1024]{1,0:T(8,128)(2,1)}, bf16[1024,1024]{1,0:T(8,128)(2,1)}, u32[]{:S(2)}, u32[]{:S(2)}) collective-permute-start(bf16[1024,1024]{1,0:T(8,128)(2,1)} %get-tuple-element.254), channel_id=1, source_target_pairs={{0,2},{1,3},{2,0},{3,1},{4,6},{5,7},{6,4},{7,5},{8,10},{9,11},{10,... | collective-permute-start | bytes 6291464 | tf_op jit(solution)/shard_map/ppermute | solution.py:45
  96.7 32.7 %collective-permute-start.6 = (bf16[4,2,3,64,256]{4,3,2,1,0:T(8,128)(2,1)S(1)}, bf16[4,2,3,64,256]{4,3,2,1,0:T(8,128)(2,1)S(1)}, u32[]{:S(2)}, u32[]{:S(2)}) collective-permute-start(bf16[4,2,3,64,256]{4,3,2,1,0:T(8,128)(2,1)S(1)} %copy-done.13), channel_id=1, source_target_pairs={{0,4},{1,5},{2,6},{3,7},{4,0},{5,1},{6,2},{7,3},{8,12},{9,13},{10,... | collective-permute-start | bytes 2359304 | tf_op jit(solution)/shard_map/ppermute | solution.py:45
  97.6 31.8 %collective-permute-start.7 = (bf16[4,2,3,64,256]{4,3,2,1,0:T(8,128)(2,1)S(1)}, bf16[4,2,3,64,256]{4,3,2,1,0:T(8,128)(2,1)}, u32[]{:S(2)}, u32[]{:S(2)}) collective-permute-start(bf16[4,2,3,64,256]{4,3,2,1,0:T(8,128)(2,1)S(1)} %copy-done.13), channel_id=1, source_target_pairs={{0,1},{1,0},{2,3},{3,2},{4,5},{5,4},{6,7},{7,6},{8,9},{9,8},{10,11... | collective-permute-start | bytes 2359304 | tf_op jit(solution)/shard_map/ppermute | solution.py:45
  99.1 34.0 %collective-permute-start.8 = (bf16[4,2,3,64,256]{4,3,2,1,0:T(8,128)(2,1)}, bf16[4,2,3,64,256]{4,3,2,1,0:T(8,128)(2,1)}, u32[]{:S(2)}, u32[]{:S(2)}) collective-permute-start(bf16[4,2,3,64,256]{4,3,2,1,0:T(8,128)(2,1)} %get-tuple-element.249.refs_4_), channel_id=1, source_target_pairs={{0,4},{1,5},{2,6},{3,7},{4,0},{5,1},{6,2},{7,3},{8,12},{9,13},{10,... | collective-permute-start | bytes 2359304 | tf_op jit(solution)/shard_map/ppermute | solution.py:45
  100.2 33.5 %all-to-all-start.3 = ((bf16[4,2,3,64,384]{4,3,2,1,0:T(8,128)(2,1)}), bf16[4,2,3,64,384]{4,3,2,1,0:T(8,128)(2,1)S(1)}, u32[]{:S(2)}, u32[]{:S(2)}) async-start(bf16[4,2,3,64,384]{4,3,2,1,0:T(8,128)(2,1)} %get-tuple-element.250), calls=%async_computation.3 | async-start | bytes 2359296 | tf_op jit(solution)/shard_map/all_to_all | solution.py:49
  139.5 44.1 %collective-permute-start.16 = (bf16[4,2,3,64,384]{4,3,2,1,0:T(8,128)(2,1)}, bf16[4,2,3,64,384]{4,3,2,1,0:T(8,128)(2,1)S(1)}, u32[]{:S(2)}, u32[]{:S(2)}) collective-permute-start(bf16[4,2,3,64,384]{4,3,2,1,0:T(8,128)(2,1)} %get-tuple-element.272.refs_4_), channel_id=1, source_target_pairs={{0,4},{1,5},{2,6},{3,7},{4,0},{5,1},{6,2},{7,3},{8,12},{9,13},{10,... | collective-permute-start | bytes 3538952 | tf_op jit(solution)/shard_map/ppermute | solution.py:45
  140.4 43.3 %all-to-all-start.4 = ((bf16[4,2,3,64,256]{4,3,2,1,0:T(8,128)(2,1)}), bf16[4,2,3,64,256]{4,3,2,1,0:T(8,128)(2,1)S(1)}, u32[]{:S(2)}, u32[]{:S(2)}) async-start(bf16[4,2,3,64,256]{4,3,2,1,0:T(8,128)(2,1)} %get-tuple-element.273), calls=%async_computation.4 | async-start | bytes 1572864 | tf_op jit(solution)/shard_map/all_to_all | solution.py:49
  146.2 37.5 %collective-permute-start.17 = (bf16[4,2,3,64,384]{4,3,2,1,0:T(8,128)(2,1)S(1)}, bf16[4,2,3,64,384]{4,3,2,1,0:T(8,128)(2,1)}, u32[]{:S(2)}, u32[]{:S(2)}) collective-permute-start(bf16[4,2,3,64,384]{4,3,2,1,0:T(8,128)(2,1)S(1)} %copy-done.15), channel_id=1, source_target_pairs={{0,1},{1,0},{2,3},{3,2},{4,5},{5,4},{6,7},{7,6},{8,9},{9,8},{10,11... | collective-permute-start | bytes 3538952 | tf_op jit(solution)/shard_map/ppermute | solution.py:45
  148.8 33.5 %collective-permute-start.14 = (bf16[2,2,3,64,256]{4,3,2,1,0:T(8,128)(2,1)}, bf16[2,2,3,64,256]{4,3,2,1,0:T(8,128)(2,1)S(1)}, u32[]{:S(2)}, u32[]{:S(2)}) collective-permute-start(bf16[2,2,3,64,256]{4,3,2,1,0:T(8,128)(2,1)} %get-tuple-element.270), channel_id=1, source_target_pairs={{0,1},{1,0},{2,3},{3,2},{4,5},{5,4},{6,7},{7,6},{8,9},{9,8},{10,11... | collective-permute-start | bytes 1179656 | tf_op jit(solution)/shard_map/ppermute | solution.py:45
  150.7 33.0 %collective-permute-start.15 = (bf16[2,2,3,64,256]{4,3,2,1,0:T(8,128)(2,1)}, bf16[2,2,3,64,256]{4,3,2,1,0:T(8,128)(2,1)}, u32[]{:S(2)}, u32[]{:S(2)}) collective-permute-start(bf16[2,2,3,64,256]{4,3,2,1,0:T(8,128)(2,1)} %get-tuple-element.271), channel_id=1, source_target_pairs={{0,4},{1,5},{2,6},{3,7},{4,0},{5,1},{6,2},{7,3},{8,12},{9,13},{10,... | collective-permute-start | bytes 1179656 | tf_op jit(solution)/shard_map/ppermute | solution.py:45
  185.0 37.1 %collective-permute-start.20 = (bf16[4,2,3,64,256]{4,3,2,1,0:T(8,128)(2,1)}, bf16[4,2,3,64,256]{4,3,2,1,0:T(8,128)(2,1)S(1)}, u32[]{:S(2)}, u32[]{:S(2)}) collective-permute-start(bf16[4,2,3,64,256]{4,3,2,1,0:T(8,128)(2,1)} %get-tuple-element.274.refs_4_), channel_id=1, source_target_pairs={{0,4},{1,5},{2,6},{3,7},{4,0},{5,1},{6,2},{7,3},{8,12},{9,13},{10,... | collective-permute-start | bytes 2359304 | tf_op jit(solution)/shard_map/ppermute | solution.py:45
  186.2 36.0 %collective-permute-start.21 = (bf16[4,2,3,64,256]{4,3,2,1,0:T(8,128)(2,1)}, bf16[4,2,3,64,256]{4,3,2,1,0:T(8,128)(2,1)S(1)}, u32[]{:S(2)}, u32[]{:S(2)}) collective-permute-start(bf16[4,2,3,64,256]{4,3,2,1,0:T(8,128)(2,1)} %get-tuple-element.274.refs_4_), channel_id=1, source_target_pairs={{0,1},{1,0},{2,3},{3,2},{4,5},{5,4},{6,7},{7,6},{8,9},{9,8},{10,11... | collective-permute-start | bytes 2359304 | tf_op jit(solution)/shard_map/ppermute | solution.py:45
  190.2 31.8 %collective-permute-start.18 = (bf16[2,2,3,64,384]{4,3,2,1,0:T(8,128)(2,1)}, bf16[2,2,3,64,384]{4,3,2,1,0:T(8,128)(2,1)S(1)}, u32[]{:S(2)}, u32[]{:S(2)}) collective-permute-start(bf16[2,2,3,64,384]{4,3,2,1,0:T(8,128)(2,1)} %get-tuple-element.294), channel_id=1, source_target_pairs={{0,1},{1,0},{2,3},{3,2},{4,5},{5,4},{6,7},{7,6},{8,9},{9,8},{10,11... | collective-permute-start | bytes 1769480 | tf_op jit(solution)/shard_map/ppermute | solution.py:45
  225.7 46.1 %collective-permute-start.22 = (bf16[2,2,3,64,256]{4,3,2,1,0:T(8,128)(2,1)}, bf16[2,2,3,64,256]{4,3,2,1,0:T(8,128)(2,1)S(1)}, u32[]{:S(2)}, u32[]{:S(2)}) collective-permute-start(bf16[2,2,3,64,256]{4,3,2,1,0:T(8,128)(2,1)} %get-tuple-element.315), channel_id=1, source_target_pairs={{0,1},{1,0},{2,3},{3,2},{4,5},{5,4},{6,7},{7,6},{8,9},{9,8},{10,11... | collective-permute-start | bytes 1179656 | tf_op jit(solution)/shard_map/ppermute | solution.py:45
  226.5 45.2 %collective-permute-start.23 = (bf16[2,2,3,64,256]{4,3,2,1,0:T(8,128)(2,1)}, bf16[2,2,3,64,256]{4,3,2,1,0:T(8,128)(2,1)S(1)}, u32[]{:S(2)}, u32[]{:S(2)}) collective-permute-start(bf16[2,2,3,64,256]{4,3,2,1,0:T(8,128)(2,1)} %get-tuple-element.316), channel_id=1, source_target_pairs={{0,4},{1,5},{2,6},{3,7},{4,0},{5,1},{6,2},{7,3},{8,12},{9,13},{10,... | collective-permute-start | bytes 1179656 | tf_op jit(solution)/shard_map/ppermute | solution.py:45
  227.7 44.1 %collective-permute-start.24 = (bf16[2,2,2,3,64,256]{5,4,3,2,1,0:T(8,128)(2,1)}, bf16[2,2,2,3,64,256]{5,4,3,2,1,0:T(8,128)(2,1)S(1)}, u32[]{:S(2)}, u32[]{:S(2)}) collective-permute-start(bf16[2,2,2,3,64,256]{5,4,3,2,1,0:T(8,128)(2,1)} %get-tuple-element.317), channel_id=1, source_target_pairs={{0,4},{1,5},{2,6},{3,7},{4,0},{5,1},{6,2},{7,3},{8,12},{9,13},{10,... | collective-permute-start | bytes 2359304 | tf_op jit(solution)/shard_map/ppermute | solution.py:45
  228.6 43.2 %collective-permute-start.25 = (bf16[2,2,2,3,64,256]{5,4,3,2,1,0:T(8,128)(2,1)}, bf16[2,2,2,3,64,256]{5,4,3,2,1,0:T(8,128)(2,1)S(1)}, u32[]{:S(2)}, u32[]{:S(2)}) collective-permute-start(bf16[2,2,2,3,64,256]{5,4,3,2,1,0:T(8,128)(2,1)} %get-tuple-element.318), channel_id=1, source_target_pairs={{0,1},{1,0},{2,3},{3,2},{4,5},{5,4},{6,7},{7,6},{8,9},{9,8},{10,11... | collective-permute-start | bytes 2359304 | tf_op jit(solution)/shard_map/ppermute | solution.py:45
  275.8 33.8 %collective-permute-start.26 = (bf16[2,2,3,64,256]{4,3,2,1,0:T(8,128)(2,1)}, bf16[2,2,3,64,256]{4,3,2,1,0:T(8,128)(2,1)S(1)}, u32[]{:S(2)}, u32[]{:S(2)}) collective-permute-start(bf16[2,2,3,64,256]{4,3,2,1,0:T(8,128)(2,1)} %get-tuple-element.340), channel_id=1, source_target_pairs={{0,4},{1,5},{2,6},{3,7},{4,0},{5,1},{6,2},{7,3},{8,12},{9,13},{10,... | collective-permute-start | bytes 1179656 | tf_op jit(solution)/shard_map/ppermute | solution.py:45
  277.0 32.7 %collective-permute-start.27 = (bf16[2,2,3,64,256]{4,3,2,1,0:T(8,128)(2,1)}, bf16[2,2,3,64,256]{4,3,2,1,0:T(8,128)(2,1)S(1)}, u32[]{:S(2)}, u32[]{:S(2)}) collective-permute-start(bf16[2,2,3,64,256]{4,3,2,1,0:T(8,128)(2,1)} %get-tuple-element.341), channel_id=1, source_target_pairs={{0,1},{1,0},{2,3},{3,2},{4,5},{5,4},{6,7},{7,6},{8,9},{9,8},{10,11... | collective-permute-start | bytes 1179656 | tf_op jit(solution)/shard_map/ppermute | solution.py:45
  277.8 31.8 %collective-permute-start.28 = (bf16[2,2,2,3,64,256]{5,4,3,2,1,0:T(8,128)(2,1)S(1)}, bf16[2,2,2,3,64,256]{5,4,3,2,1,0:T(8,128)(2,1)S(1)}, u32[]{:S(2)}, u32[]{:S(2)}) collective-permute-start(bf16[2,2,2,3,64,256]{5,4,3,2,1,0:T(8,128)(2,1)S(1)} %copy-done.21), channel_id=1, source_target_pairs={{0,4},{1,5},{2,6},{3,7},{4,0},{5,1},{6,2},{7,3},{8,12},{9,13},{10,... | collective-permute-start | bytes 2359304 | tf_op jit(solution)/shard_map/ppermute | solution.py:45
  278.8 31.0 %collective-permute-start.29 = (bf16[2,2,2,3,64,256]{5,4,3,2,1,0:T(8,128)(2,1)S(1)}, bf16[2,2,2,3,64,256]{5,4,3,2,1,0:T(8,128)(2,1)S(1)}, u32[]{:S(2)}, u32[]{:S(2)}) collective-permute-start(bf16[2,2,2,3,64,256]{5,4,3,2,1,0:T(8,128)(2,1)S(1)} %copy-done.22), channel_id=1, source_target_pairs={{0,1},{1,0},{2,3},{3,2},{4,5},{5,4},{6,7},{7,6},{8,9},{9,8},{10,11... | collective-permute-start | bytes 2359304 | tf_op jit(solution)/shard_map/ppermute | solution.py:45
  314.8 37.1 %collective-permute-start.32 = (bf16[2,2,3,64,256]{4,3,2,1,0:T(8,128)(2,1)}, bf16[2,2,3,64,256]{4,3,2,1,0:T(8,128)(2,1)}, u32[]{:S(2)}, u32[]{:S(2)}) collective-permute-start(bf16[2,2,3,64,256]{4,3,2,1,0:T(8,128)(2,1)} %get-tuple-element.364), channel_id=1, source_target_pairs={{0,4},{1,5},{2,6},{3,7},{4,0},{5,1},{6,2},{7,3},{8,12},{9,13},{10,... | collective-permute-start | bytes 1179656 | tf_op jit(solution)/shard_map/ppermute | solution.py:45
  316.0 35.9 %collective-permute-start.33 = (bf16[2,2,3,64,256]{4,3,2,1,0:T(8,128)(2,1)}, bf16[2,2,3,64,256]{4,3,2,1,0:T(8,128)(2,1)}, u32[]{:S(2)}, u32[]{:S(2)}) collective-permute-start(bf16[2,2,3,64,256]{4,3,2,1,0:T(8,128)(2,1)} %get-tuple-element.365), channel_id=1, source_target_pairs={{0,1},{1,0},{2,3},{3,2},{4,5},{5,4},{6,7},{7,6},{8,9},{9,8},{10,11... | collective-permute-start | bytes 1179656 | tf_op jit(solution)/shard_map/ppermute | solution.py:45
  316.9 35.1 %all-to-all-start.5 = ((bf16[4,2,3,64,256]{4,3,2,1,0:T(8,128)(2,1)}), bf16[4,2,3,64,256]{4,3,2,1,0:T(8,128)(2,1)}, u32[]{:S(2)}, u32[]{:S(2)}) async-start(bf16[4,2,3,64,256]{4,3,2,1,0:T(8,128)(2,1)} %get-tuple-element.363), calls=%async_computation.5 | async-start | bytes 1572864 | tf_op jit(solution)/shard_map/all_to_all | solution.py:49
  321.5 31.3 %collective-permute-start.31 = (bf16[1024,1024]{1,0:T(8,128)(2,1)}, bf16[1024,1024]{1,0:T(8,128)(2,1)S(1)}, u32[]{:S(2)}, u32[]{:S(2)}) collective-permute-start(bf16[1024,1024]{1,0:T(8,128)(2,1)} %get-tuple-element.353), channel_id=1, source_target_pairs={{0,2},{1,3},{2,0},{3,1},{4,6},{5,7},{6,4},{7,5},{8,10},{9,11},{10,... | collective-permute-start | bytes 6291464 | tf_op jit(solution)/shard_map/ppermute | solution.py:45
  358.9 31.0 %collective-permute-start.37 = (bf16[2,2,3,64,384]{4,3,2,1,0:T(8,128)(2,1)}, bf16[2,2,3,64,384]{4,3,2,1,0:T(8,128)(2,1)S(1)}, u32[]{:S(2)}, u32[]{:S(2)}) collective-permute-start(bf16[2,2,3,64,384]{4,3,2,1,0:T(8,128)(2,1)} %get-tuple-element.382), channel_id=1, source_target_pairs={{0,4},{1,5},{2,6},{3,7},{4,0},{5,1},{6,2},{7,3},{8,12},{9,13},{10,... | collective-permute-start | bytes 1769480 | tf_op jit(solution)/shard_map/ppermute | solution.py:45
  360.7 30.8 %collective-permute-start.36 = (bf16[4,4,4,64,256]{4,3,2,1,0:T(8,128)(2,1)}, bf16[4,4,4,64,256]{4,3,2,1,0:T(8,128)(2,1)S(1)}, u32[]{:S(2)}, u32[]{:S(2)}) collective-permute-start(bf16[4,4,4,64,256]{4,3,2,1,0:T(8,128)(2,1)} %get-tuple-element.374), channel_id=1, source_target_pairs={{0,2},{1,3},{2,0},{3,1},{4,6},{5,7},{6,4},{7,5},{8,10},{9,11},{10,... | collective-permute-start | bytes 6291464 | tf_op jit(solution)/shard_map/ppermute | solution.py:45
  363.0 36.5 %all-to-all-start.8 = ((bf16[4,2,3,64,256]{4,3,2,1,0:T(8,128)(2,1)}), bf16[4,2,3,64,256]{4,3,2,1,0:T(8,128)(2,1)}, u32[]{:S(2)}, u32[]{:S(2)}) async-start(bf16[4,2,3,64,256]{4,3,2,1,0:T(8,128)(2,1)} %get-tuple-element.440), calls=%async_computation.8 | async-start | bytes 1572864 | tf_op jit(solution)/shard_map/all_to_all | solution.py:49
  392.9 35.4 %collective-permute-start.41 = (bf16[4,4,4,64,256]{4,3,2,1,0:T(8,128)(2,1)}, bf16[4,4,4,64,256]{4,3,2,1,0:T(8,128)(2,1)S(1)}, u32[]{:S(2)}, u32[]{:S(2)}) collective-permute-start(bf16[4,4,4,64,256]{4,3,2,1,0:T(8,128)(2,1)} %get-tuple-element.391), channel_id=1, source_target_pairs={{0,2},{1,3},{2,0},{3,1},{4,6},{5,7},{6,4},{7,5},{8,10},{9,11},{10,... | collective-permute-start | bytes 6291464 | tf_op jit(solution)/shard_map/ppermute | solution.py:45
  399.5 35.7 %all-to-all-start.9 = ((bf16[4,2,3,64,384]{4,3,2,1,0:T(8,128)(2,1)}), bf16[4,2,3,64,384]{4,3,2,1,0:T(8,128)(2,1)}, u32[]{:S(2)}, u32[]{:S(2)}) async-start(bf16[4,2,3,64,384]{4,3,2,1,0:T(8,128)(2,1)} %get-tuple-element.441), calls=%async_computation.9 | async-start | bytes 2359296 | tf_op jit(solution)/shard_map/all_to_all | solution.py:49
  435.1 39.4 %all-to-all-start.10 = ((bf16[4,2,3,64,256]{4,3,2,1,0:T(8,128)(2,1)}), bf16[4,2,3,64,256]{4,3,2,1,0:T(8,128)(2,1)S(1)}, u32[]{:S(2)}, u32[]{:S(2)}) async-start(bf16[4,2,3,64,256]{4,3,2,1,0:T(8,128)(2,1)} %get-tuple-element.442), calls=%async_computation.10 | async-start | bytes 1572864 | tf_op jit(solution)/shard_map/all_to_all | solution.py:49
  (96 other events, 875.3 us)
